TPU v7x, 1024 devices: a whole 8x8x8 slice. The times are simulated.
1024 devices in a mesh: expert: 64 (over y_hi, x, core), dp: 16 (over y_lo, z).
Axes of the slice: x: 8, y: 8 (y_hi: 4, y_lo: 2; y = y_hi * 2 + y_lo), z: 8, core: 2. Of those that a mesh axis runs over, the one named last changes fastest.
Arguments:
- tokens: bfloat16 [131072, 2048], P(('expert', 'dp')), may hold values from -6 to 6
- cotangent: bfloat16 [131072, 2048], P(('expert', 'dp')), may hold values from -1.5 to 1.5
- gate_scores: bfloat16 [131072], P(('expert', 'dp')), may hold values from 0.19921875 to 1
- expert_ids: int32 [131072], P(('expert', 'dp')), may hold values from 0 to 63, as said below
- slot_index: int32 [131072], P(('expert', 'dp')), may hold values from 0 to 3, as said below
- gate_weight: bfloat16 [64, 2048, 384], P('expert'), may hold values from -0.125 to 0.125
- up_weight: bfloat16 [64, 2048, 384], P('expert'), may hold values from -0.125 to 0.125
- down_weight: bfloat16 [64, 384, 2048], P('expert'), may hold values from -0.3125 to 0.3125
Outputs:
- token_grad: bfloat16 [131072, 2048], P(('expert', 'dp'))
- score_grad: bfloat16 [131072], P(('expert', 'dp'))
- grad_gate: bfloat16 [64, 2048, 384], P('expert', 'dp')
- grad_up: bfloat16 [64, 2048, 384], P('expert', 'dp')
- grad_down: bfloat16 [64, 384, 2048], P('expert', None, 'dp')
Inputs may be any that keep to these rules, and one draw needn't show every extreme that they name: `expert_ids`: within the 128 tokens of one device no expert is named more than 4 times, and some expert exactly 4 times. `slot_index`: tokens of one device with the same expert have distinct slots.
All inputs are finite; a program needn't handle non-finite values.
Results may differ from a plain program's by a relative error of at most 0.024.
Values may be sent and summed in bfloat16 or wider, within the bound.
No kernel may reach another device: no remote copies, remote signals or barrier semaphores. Data moves between devices by JAX's collectives and lax.ppermute only.
A program may use at most 64 MiB of HBM per device.

v0:
```python
import jax
import jax.numpy as jnp
from jax import lax
from jax.sharding import PartitionSpec as P


def silu_parts(pre_gate):
    sigmoid = jax.nn.sigmoid(pre_gate)
    return (sigmoid, pre_gate * sigmoid)


def contract(left, right, left_dim, right_dim):
    return lax.dot_general(
        left, right, (((left_dim,), (right_dim,)), ((), ())), preferred_element_type=jnp.float32
    )


def on_device(
    tokens, cotangent, gate_scores, expert_ids, slot_index, gate_weight, up_weight, down_weight
):
    experts = lax.axis_size("expert")
    token_count = tokens.shape[0]
    features = tokens.shape[1]
    capacity = 2 * token_count // experts
    slot_count = experts * capacity
    position = expert_ids * capacity + slot_index
    send_inputs = (
        jnp.zeros((slot_count, features), tokens.dtype)
        .at[position]
        .set(tokens)
        .reshape(experts, capacity, features)
    )
    send_cotan = (
        jnp.zeros((slot_count, features), cotangent.dtype)
        .at[position]
        .set(cotangent)
        .reshape(experts, capacity, features)
    )
    send_scores = (
        jnp.zeros((slot_count,), gate_scores.dtype)
        .at[position]
        .set(gate_scores)
        .reshape(experts, capacity)
    )
    inputs, cotan_rows, score_rows = (
        lax.all_to_all(send_inputs, "expert", split_axis=0, concat_axis=0, tiled=True),
        lax.all_to_all(send_cotan, "expert", split_axis=0, concat_axis=0, tiled=True),
        lax.all_to_all(send_scores, "expert", split_axis=0, concat_axis=0, tiled=True),
    )
    inputs = inputs.reshape(slot_count, features)
    cotan_rows = cotan_rows.reshape(slot_count, features)
    score_rows = score_rows.reshape(slot_count)
    gate_matrix = gate_weight[0]
    up_matrix = up_weight[0]
    down_matrix = down_weight[0]
    pre_gate = jnp.dot(inputs, gate_matrix, preferred_element_type=jnp.float32)
    pre_up = jnp.dot(inputs, up_matrix, preferred_element_type=jnp.float32)
    sigmoid, activated = silu_parts(pre_gate)
    hidden = (activated * pre_up).astype(jnp.bfloat16)
    output = jnp.dot(hidden, down_matrix, preferred_element_type=jnp.float32)
    cotan_float = cotan_rows.astype(jnp.float32)
    slot_score = jnp.sum(cotan_float * output, axis=1).astype(jnp.bfloat16)
    scaled = (score_rows.astype(jnp.float32)[:, None] * cotan_float).astype(jnp.bfloat16)
    hidden_grad = contract(scaled, down_matrix, 1, 1)
    up_grad = (hidden_grad * activated).astype(jnp.bfloat16)
    pre_grad = (hidden_grad * pre_up * sigmoid * (1.0 + pre_gate * (1.0 - sigmoid))).astype(
        jnp.bfloat16
    )
    part_down = contract(hidden, scaled, 0, 0)
    input_grad = (
        contract(pre_grad, gate_matrix, 1, 1) + contract(up_grad, up_matrix, 1, 1)
    ).astype(jnp.bfloat16)
    part_gate = contract(inputs, pre_grad, 0, 0)
    part_up = contract(inputs, up_grad, 0, 0)
    returned, returned_score = (
        lax.all_to_all(
            input_grad.reshape(experts, capacity, features),
            "expert",
            split_axis=0,
            concat_axis=0,
            tiled=True,
        ),
        lax.all_to_all(
            slot_score.reshape(experts, capacity), "expert", split_axis=0, concat_axis=0, tiled=True
        ),
    )
    summed_gate, summed_up, summed_down = (
        lax.psum_scatter(
            part_gate[None].astype(jnp.bfloat16), "dp", scatter_dimension=1, tiled=True
        ).astype(jnp.float32),
        lax.psum_scatter(
            part_up[None].astype(jnp.bfloat16), "dp", scatter_dimension=1, tiled=True
        ).astype(jnp.float32),
        lax.psum_scatter(
            part_down[None].astype(jnp.bfloat16), "dp", scatter_dimension=2, tiled=True
        ).astype(jnp.float32),
    )
    grad_down = summed_down.astype(jnp.bfloat16)
    grad_gate = summed_gate.astype(jnp.bfloat16)
    grad_up = summed_up.astype(jnp.bfloat16)
    token_grad = returned.reshape(slot_count, features)[position]
    score_grad = returned_score.reshape(slot_count)[position]
    return (token_grad, score_grad, grad_gate, grad_up, grad_down)


def solution(mesh):
    placed = (
        P(("expert", "dp"), None),
        P(("expert", "dp"), None),
        P(("expert", "dp")),
        P(("expert", "dp")),
        P(("expert", "dp")),
        P("expert", None, None),
        P("expert", None, None),
        P("expert", None, None),
    )
    return jax.shard_map(
        on_device,
        mesh=mesh,
        in_specs=placed,
        out_specs=(
            P(("expert", "dp"), None),
            P(("expert", "dp")),
            P("expert", "dp", None),
            P("expert", "dp", None),
            P("expert", None, "dp"),
        ),
        check_vma=False,
    )
```

profile of v0, /device:TPU:2, one launch (start us, length us, event | category | flops | bytes accessed | tf_op | source)
XLA Modules:
  0.0 412.2 jit_solution(9147331621415809608)
XLA Ops:
  7.2 0.8 compare_select_fusion
  8.0 1.5 scatter_custom_fusion
  9.5 0.7 all_to_all.25
  10.2 17.2 %all-to-all-start = ((bf16[64,1,4]{2,1,0:T(2,128)(2,1)}), bf16[64,1,4]{2,1,0:T(2,128)(2,1)S(1)}, u32[]{:S(2)}, u32[]{:S(2)}) async-start(bf16[64,1,4]{2,1,0:T(2,128)(2,1)} %all_to_all.25), calls=%async_computation | async-start | bytes 65536 | tf_op jit(solution)/shard_map/all_to_all | solution.py:48
  27.4 2.2 scatter_custom_fusion.1
  29.6 1.2 reshape.72
  30.9 7.6 %all-to-all-done = bf16[64,1,4]{2,1,0:T(2,128)(2,1)S(1)} async-done(((bf16[64,1,4]{2,1,0:T(2,128)(2,1)}), bf16[64,1,4]{2,1,0:T(2,128)(2,1)S(1)}, u32[]{:S(2)}, u32[]{:S(2)}) %all-to-all-start) | async-done | bytes 544 | tf_op jit(solution)/shard_map/all_to_all | solution.py:48
  38.4 5.5 %all-to-all-start.1 = ((bf16[64,4,2048]{2,1,0:T(4,128)(2,1)}), bf16[64,4,2048]{2,1,0:T(4,128)(2,1)S(1)}, u32[]{:S(2)}, u32[]{:S(2)}) async-start(bf16[64,4,2048]{2,1,0:T(4,128)(2,1)} %reshape.72), calls=%async_computation.1 | async-start | bytes 2097152 | tf_op jit(solution)/shard_map/all_to_all | solution.py:47
  43.9 3.0 scatter_custom_fusion.2
  46.9 2.3 reshape.73
  49.1 23.6 %all-to-all-done.1 = bf16[64,4,2048]{2,1,0:T(4,128)(2,1)S(1)} async-done(((bf16[64,4,2048]{2,1,0:T(4,128)(2,1)}), bf16[64,4,2048]{2,1,0:T(4,128)(2,1)S(1)}, u32[]{:S(2)}, u32[]{:S(2)}) %all-to-all-start.1) | async-done | bytes 1048608 | tf_op jit(solution)/shard_map/all_to_all | solution.py:47
  72.8 8.0 %all-to-all-start.2 = ((bf16[64,4,2048]{2,1,0:T(4,128)(2,1)}), bf16[64,4,2048]{2,1,0:T(4,128)(2,1)}, u32[]{:S(2)}, u32[]{:S(2)}) async-start(bf16[64,4,2048]{2,1,0:T(4,128)(2,1)} %reshape.73), calls=%async_computation.2 | async-start | bytes 2097152 | tf_op jit(solution)/shard_map/all_to_all | solution.py:46
  80.8 0.1 convert_reduce_fusion
  80.9 0.1 reshape.80
  81.1 1.5 multiply_convert_fusion.1
  82.5 2.1 convert_element_type.87
  84.7 24.8 %all-to-all-done.2 = bf16[64,4,2048]{2,1,0:T(4,128)(2,1)} async-done(((bf16[64,4,2048]{2,1,0:T(4,128)(2,1)}), bf16[64,4,2048]{2,1,0:T(4,128)(2,1)}, u32[]{:S(2)}, u32[]{:S(2)}) %all-to-all-start.2) | async-done | bytes 1048608 | tf_op jit(solution)/shard_map/all_to_all | solution.py:46
  109.5 1.3 reshape.74
  110.8 2.3 fusion.6
  113.1 0.7 fusion.12
  113.9 0.8 multiply_convert_fusion.3
  114.7 2.5 reshape.79
  117.2 3.5 fusion.2
  120.7 8.5 %copy.15 = bf16[1,384,2048]{1,0,2:T(2,128)(2,1)} copy(bf16[1,384,2048]{2,1,0:T(8,128)(2,1)} %fusion.2) | data formatting | bytes 3145728
  129.1 3.4 copy.19
  132.5 0.2 reduce-scatter.6.cloned.1.call-start
  132.8 1.9 fusion
  134.8 1.9 fusion.1
  136.7 1.4 copy-done.3
  138.1 2.4 fusion.14
  140.5 0.8 convert_element_type.108
  141.2 7.9 %all-to-all-start.4 = ((bf16[64,1,4]{2,1,0:T(2,128)(2,1)}), bf16[64,1,4]{2,1,0:T(2,128)(2,1)S(1)}, u32[]{:S(2)}, u32[]{:S(2)}) async-start(bf16[64,1,4]{2,1,0:T(2,128)(2,1)} %convert_element_type.108), calls=%async_computation.4 | async-start | bytes 65536 | tf_op jit(solution)/shard_map/all_to_all | solution.py:83
  149.2 2.3 fusion.4
  151.4 0.7 fusion.3
  152.2 1.2 reshape.75
  153.4 6.7 %all-to-all-done.4 = bf16[64,1,4]{2,1,0:T(2,128)(2,1)S(1)} async-done(((bf16[64,1,4]{2,1,0:T(2,128)(2,1)}), bf16[64,1,4]{2,1,0:T(2,128)(2,1)S(1)}, u32[]{:S(2)}, u32[]{:S(2)}) %all-to-all-start.4) | async-done | bytes 544 | tf_op jit(solution)/shard_map/all_to_all | solution.py:83
  160.1 6.3 %all-to-all-start.3 = ((bf16[64,4,2048]{2,1,0:T(4,128)(2,1)}), bf16[64,4,2048]{2,1,0:T(4,128)(2,1)}, u32[]{:S(2)}, u32[]{:S(2)}) async-start(bf16[64,4,2048]{2,1,0:T(4,128)(2,1)} %reshape.75), calls=%async_computation.3 | async-start | bytes 2097152 | tf_op jit(solution)/shard_map/all_to_all | solution.py:76
  166.4 0.1 reduce
  166.5 0.1 reshape.77
  166.6 1.7 gather_fusion.1
  168.3 27.1 %all-to-all-done.3 = bf16[64,4,2048]{2,1,0:T(4,128)(2,1)} async-done(((bf16[64,4,2048]{2,1,0:T(4,128)(2,1)}), bf16[64,4,2048]{2,1,0:T(4,128)(2,1)}, u32[]{:S(2)}, u32[]{:S(2)}) %all-to-all-start.3) | async-done | bytes 1048608 | tf_op jit(solution)/shard_map/all_to_all | solution.py:76
  195.4 1.3 reshape.76
  196.7 1.7 gather_fusion
  198.5 41.7 %reduce-scatter.10.cloned.1.call-done = bf16[128,384]{1,0:T(8,128)(2,1)} async-done(((bf16[2048,384]{1,0:T(8,128)(2,1)}), bf16[128,384]{1,0:T(8,128)(2,1)}) %reduce-scatter.10.cloned.1.call-update) | async-done | bytes 98320
  240.1 1.0 reshape_bitcast_fusion
  241.1 0.8 copy.16
  241.9 83.8 %reduce-scatter.6.cloned.1.call-done = bf16[1,128,384]{2,1,0:T(8,128)(2,1)} async-done(((bf16[1,2048,384]{2,1,0:T(8,128)(2,1)}), bf16[1,128,384]{2,1,0:T(8,128)(2,1)}) %reduce-scatter.6.cloned.1.call-update) | async-done | bytes 98320 | tf_op jit(solution)/shard_map/reduce_scatter | solution.py:88
  325.8 79.9 %reduce-scatter.8.cloned.1.call-done = bf16[1,128,384]{2,1,0:T(8,128)(2,1)} async-done(((bf16[1,2048,384]{2,1,0:T(8,128)(2,1)}), bf16[1,128,384]{2,1,0:T(8,128)(2,1)}) %reduce-scatter.8.cloned.1.call-update) | async-done | bytes 98320 | tf_op jit(solution)/shard_map/reduce_scatter | solution.py:91
  (18 shorter events, 0.2 us)
Async XLA Ops:
  7.2 106.7 %copy-start = (bf16[1,2048,384]{2,1,0:T(8,128)(2,1)S(1)}, bf16[1,2048,384]{2,1,0:T(8,128)(2,1)}, u32[]{:S(2)}) copy-start(bf16[1,2048,384]{2,1,0:T(8,128)(2,1)} %param.14) | copy-start | bytes 4718596
  10.2 28.2 %all-to-all-start = ((bf16[64,1,4]{2,1,0:T(2,128)(2,1)}), bf16[64,1,4]{2,1,0:T(2,128)(2,1)S(1)}, u32[]{:S(2)}, u32[]{:S(2)}) async-start(bf16[64,1,4]{2,1,0:T(2,128)(2,1)} %all_to_all.25), calls=%async_computation | async-start | bytes 65536 | tf_op jit(solution)/shard_map/all_to_all | solution.py:48
  38.4 34.4 %all-to-all-start.1 = ((bf16[64,4,2048]{2,1,0:T(4,128)(2,1)}), bf16[64,4,2048]{2,1,0:T(4,128)(2,1)S(1)}, u32[]{:S(2)}, u32[]{:S(2)}) async-start(bf16[64,4,2048]{2,1,0:T(4,128)(2,1)} %reshape.72), calls=%async_computation.1 | async-start | bytes 2097152 | tf_op jit(solution)/shard_map/all_to_all | solution.py:47
  72.8 9.7 %copy-start.1 = (bf16[64,4,2048]{2,1,0:T(4,128)(2,1)}, bf16[64,4,2048]{2,1,0:T(4,128)(2,1)S(1)}, u32[]{:S(2)}) copy-start(bf16[64,4,2048]{2,1,0:T(4,128)(2,1)S(1)} %all-to-all-done.1) | copy-start | bytes 3145732
  72.8 36.7 %all-to-all-start.2 = ((bf16[64,4,2048]{2,1,0:T(4,128)(2,1)}), bf16[64,4,2048]{2,1,0:T(4,128)(2,1)}, u32[]{:S(2)}, u32[]{:S(2)}) async-start(bf16[64,4,2048]{2,1,0:T(4,128)(2,1)} %reshape.73), calls=%async_computation.2 | async-start | bytes 2097152 | tf_op jit(solution)/shard_map/all_to_all | solution.py:46
  80.8 159.4 %reduce-scatter.10.cloned.1.call-start = ((), (), s32[]{:S(2)}) async-start(), calls=%async_computation.10 | async-start | bytes 1671168
  110.8 2.3 copy-start.2
  110.8 2.3 copy-start.4
  114.7 18.1 %copy-start.5 = (bf16[256,384]{1,0:T(8,128)(2,1)}, bf16[256,384]{1,0:T(8,128)(2,1)S(1)}, u32[]{:S(2)}) copy-start(bf16[256,384]{1,0:T(8,128)(2,1)S(1)} %get-tuple-element.6) | copy-start | bytes 589828
  132.5 193.2 %reduce-scatter.6.cloned.1.call-start = ((), (), s32[]{:S(2)}) async-start(), calls=%async_computation.8 | async-start | bytes 1671168 | tf_op jit(solution)/shard_map/reduce_scatter | solution.py:88
  134.7 270.9 %reduce-scatter.8.cloned.1.call-start = ((), (), s32[]{:S(2)}) async-start(), calls=%async_computation.9 | async-start | bytes 1671168 | tf_op jit(solution)/shard_map/reduce_scatter | solution.py:91
  136.7 1.4 copy-start.3
  141.2 18.9 %all-to-all-start.4 = ((bf16[64,1,4]{2,1,0:T(2,128)(2,1)}), bf16[64,1,4]{2,1,0:T(2,128)(2,1)S(1)}, u32[]{:S(2)}, u32[]{:S(2)}) async-start(bf16[64,1,4]{2,1,0:T(2,128)(2,1)} %convert_element_type.108), calls=%async_computation.4 | async-start | bytes 65536 | tf_op jit(solution)/shard_map/all_to_all | solution.py:83
  160.1 35.3 %all-to-all-start.3 = ((bf16[64,4,2048]{2,1,0:T(4,128)(2,1)}), bf16[64,4,2048]{2,1,0:T(4,128)(2,1)}, u32[]{:S(2)}, u32[]{:S(2)}) async-start(bf16[64,4,2048]{2,1,0:T(4,128)(2,1)} %reshape.75), calls=%async_computation.3 | async-start | bytes 2097152 | tf_op jit(solution)/shard_map/all_to_all | solution.py:76
Sparse Core Ops, SparseCore 0:
  132.7 107.4 reduce-scatter.9
  244.5 81.2 reduce-scatter.5
  329.8 75.8 reduce-scatter.7
where the time goes:
time: 413 us; the launch traced here: 412 us
  waiting for transfers between devices  295 us (71%)
  starting transfers between devices  45.2 us (11%)
  local copies, waits for them, and re-layouts  38.9 us (9%)
  matrix products  16.5 us (4%)
  between operations  14 us (3%)
    reduce_scatter x1, waiting for transfers between devices, on_device(): lax.psum_scatter(part_gate[None].astype(jnp.bfloat16), 'dp', scatter_dime...  83.8 us
    reduce_scatter x1, waiting for transfers between devices, on_device(): lax.psum_scatter(part_up[None].astype(jnp.bfloat16), 'dp', scatter_dimens...  79.9 us
    unnamed x4, waiting for transfers between devices  41.7 us
    all_to_all x1, waiting for transfers between devices, on_device(): lax.all_to_all(input_grad.reshape(experts, capacity, features), 'expert',...  27.1 us
    all_to_all x1, waiting for transfers between devices, on_device(): lax.all_to_all(send_inputs, 'expert', split_axis=0, concat_axis=0, tiled=...  24.8 us
    all_to_all x1, waiting for transfers between devices, on_device(): lax.all_to_all(send_cotan, 'expert', split_axis=0, concat_axis=0, tiled=T...  23.6 us
    all_to_all x1, starting transfers between devices, on_device(): lax.all_to_all(send_scores, 'expert', split_axis=0, concat_axis=0, tiled=...  17.2 us
    unnamed x16, local copies, waits for them, and re-layouts  15 us
  transfers between devices with their start and end apart: 8, of which 8 were waited for; matrix products, arithmetic and copies ran while one was open for 7% of the time, Pallas kernels for 0%

commit v1 on v0

v1 whole, which is shorter than its diff:
```python
import functools

import jax
import jax.numpy as jnp
from jax import lax
from jax.experimental import pallas as pl
from jax.experimental.pallas import tpu as pltpu
from jax.sharding import PartitionSpec as P

F32 = jnp.float32
BF16 = jnp.bfloat16
LANES = 128


def dot(left, right, left_dim, right_dim):
    return lax.dot_general(
        left, right, (((left_dim,), (right_dim,)), ((), ())), preferred_element_type=F32
    )


def dispatch_kernel(capacity, ids_ref, slot_ref, score_ref, tokens_ref, cotan_ref, out_ref):
    rows, count = out_ref.shape[0], tokens_ref.shape[0]
    position = ids_ref[...] * (2 * capacity) + slot_ref[...]
    row = lax.broadcasted_iota(jnp.int32, (rows, count), 0)
    pick_token = jnp.where(row == position, F32(1), F32(0)).astype(BF16)
    pick_cotan = jnp.where(
        row == position + capacity, score_ref[...].astype(F32), F32(0)
    ).astype(BF16)
    out_ref[...] = (
        dot(pick_token, tokens_ref[...], 1, 0) + dot(pick_cotan, cotan_ref[...], 1, 0)
    ).astype(BF16)


def dispatch(expert_ids, slot_index, gate_scores, tokens, cotangent, experts, capacity):
    count, features = tokens.shape
    rows = experts * 2 * capacity
    block = min(512, features)
    small = pl.BlockSpec((1, count), lambda i: (0, 0))
    wide = pl.BlockSpec((count, block), lambda i: (0, i))
    return pl.pallas_call(
        functools.partial(dispatch_kernel, capacity),
        grid=(features // block,),
        in_specs=[small, small, small, wide, wide],
        out_specs=pl.BlockSpec((rows, block), lambda i: (0, i)),
        out_shape=jax.ShapeDtypeStruct((rows, features), BF16),
        compiler_params=pltpu.CompilerParams(vmem_limit_bytes=24 * 2**20),
        name="dispatch",
    )(
        expert_ids.reshape(1, count),
        slot_index.reshape(1, count),
        gate_scores.reshape(1, count),
        tokens,
        cotangent,
    )


def pick_rows(slots, rows, capacity, half):
    slot = lax.broadcasted_iota(jnp.int32, (slots, rows), 0)
    row = lax.broadcasted_iota(jnp.int32, (slots, rows), 1)
    wanted = (slot // capacity) * (2 * capacity) + slot % capacity + half * capacity
    return jnp.where(row == wanted, F32(1), F32(0)).astype(BF16)


def expert_kernel(
    capacity, recv_ref, gate_ref, up_ref, down_ref, grads_ref, inner_ref, score_ref,
    inputs, scaled, hidden_sc, inner_sc,
):
    rows = recv_ref.shape[0]
    slots = rows // 2
    hidden_size = gate_ref.shape[1]
    block = grads_ref.shape[0]
    step = pl.program_id(0)

    @pl.when(step == 0)
    def _():
        received = recv_ref[...]
        inputs[...] = dot(pick_rows(slots, rows, capacity, 0), received, 1, 0).astype(BF16)
        scaled[...] = dot(pick_rows(slots, rows, capacity, 1), received, 1, 0).astype(BF16)
        pre_gate = dot(inputs[...], gate_ref[...], 1, 0)
        pre_up = dot(inputs[...], up_ref[...], 1, 0)
        hidden_grad = dot(scaled[...], down_ref[...], 1, 1)
        sigmoid = jax.nn.sigmoid(pre_gate)
        activated = pre_gate * sigmoid
        hidden = (activated * pre_up).astype(BF16)
        hidden_sc[...] = hidden
        inner_sc[:, :hidden_size] = (
            hidden_grad * pre_up * sigmoid * (1.0 + pre_gate * (1.0 - sigmoid))
        ).astype(BF16)
        inner_sc[:, hidden_size:] = (hidden_grad * activated).astype(BF16)
        inner_ref[...] = inner_sc[...]
        score = jnp.sum(hidden.astype(F32) * hidden_grad, axis=1, keepdims=True)
        score_ref[...] = jnp.broadcast_to(score, score_ref.shape).astype(BF16)

    columns = pl.ds(pl.multiple_of(step * block, block), block)
    grads_ref[:, : 2 * hidden_size] = dot(inputs[:, columns], inner_sc[...], 0, 0).astype(BF16)
    grads_ref[:, 2 * hidden_size :] = dot(scaled[:, columns], hidden_sc[...], 0, 0).astype(BF16)


def expert_grads(received, gate, up, down, capacity):
    rows, features = received.shape
    hidden_size = gate.shape[1]
    slots = rows // 2
    block = min(256, features)
    whole = lambda shape: pl.BlockSpec(shape, lambda i: (0, 0))
    return pl.pallas_call(
        functools.partial(expert_kernel, capacity),
        grid=(features // block,),
        in_specs=[whole(received.shape), whole(gate.shape), whole(up.shape), whole(down.shape)],
        out_specs=[
            pl.BlockSpec((block, 3 * hidden_size), lambda i: (i, 0)),
            whole((slots, 2 * hidden_size)),
            whole((slots, LANES)),
        ],
        out_shape=[
            jax.ShapeDtypeStruct((features, 3 * hidden_size), BF16),
            jax.ShapeDtypeStruct((slots, 2 * hidden_size), BF16),
            jax.ShapeDtypeStruct((slots, LANES), BF16),
        ],
        scratch_shapes=[
            pltpu.VMEM((slots, features), BF16),
            pltpu.VMEM((slots, features), BF16),
            pltpu.VMEM((slots, hidden_size), BF16),
            pltpu.VMEM((slots, 2 * hidden_size), BF16),
        ],
        compiler_params=pltpu.CompilerParams(vmem_limit_bytes=40 * 2**20),
        name="expert_grads",
    )(received, gate, up, down)


def return_kernel(capacity, inner_ref, score_ref, gate_ref, up_ref, out_ref):
    slots = inner_ref.shape[0]
    rows = out_ref.shape[0]
    hidden_size = gate_ref.shape[1]
    half = gate_ref.shape[0] // 2
    total = jnp.zeros((rows, half), F32)
    for part in range(2):
        piece = pl.ds(part * half, half)
        input_grad = dot(inner_ref[:, :hidden_size], gate_ref[piece, :], 1, 1) + dot(
            inner_ref[:, hidden_size:], up_ref[piece, :], 1, 1
        )
        spread = pick_rows(slots, rows, capacity, part)
        total += dot(spread, input_grad.astype(BF16), 0, 0)
        if part == 0:
            out_ref[:, half:] = dot(spread, score_ref[...], 0, 0).astype(BF16)
    out_ref[:, :half] = total.astype(BF16)


def return_rows(inner, score, gate, up, capacity):
    slots = inner.shape[0]
    half = gate.shape[0] // 2
    return pl.pallas_call(
        functools.partial(return_kernel, capacity),
        out_shape=jax.ShapeDtypeStruct((2 * slots, half + LANES), BF16),
        compiler_params=pltpu.CompilerParams(vmem_limit_bytes=40 * 2**20),
        name="return_rows",
    )(inner, score, gate, up)


def combine_kernel(capacity, ids_ref, slot_ref, score_ref, rows_ref, token_ref, grad_ref):
    rows = rows_ref.shape[0]
    count = token_ref.shape[0]
    half = token_ref.shape[1] // 2
    position = ids_ref[...] * (2 * capacity) + slot_ref[...]
    row = lax.broadcasted_iota(jnp.int32, (rows, count), 0)
    for part in range(2):
        pick = jnp.where(row == position + part * capacity, F32(1), F32(0)).astype(BF16)
        token_ref[:, part * half : (part + 1) * half] = dot(
            pick, rows_ref[:, :half], 0, 0
        ).astype(BF16)
        if part == 0:
            score = dot(rows_ref[:, half:], pick, 0, 0)
            grad_ref[...] = (score[0:1, :] / score_ref[...].astype(F32)).astype(BF16)


def combine(expert_ids, slot_index, gate_scores, rows, features, capacity):
    count = expert_ids.shape[0]
    return pl.pallas_call(
        functools.partial(combine_kernel, capacity),
        out_shape=[
            jax.ShapeDtypeStruct((count, features), BF16),
            jax.ShapeDtypeStruct((1, count), BF16),
        ],
        compiler_params=pltpu.CompilerParams(vmem_limit_bytes=24 * 2**20),
        name="combine",
    )(
        expert_ids.reshape(1, count),
        slot_index.reshape(1, count),
        gate_scores.reshape(1, count),
        rows,
    )


def split_kernel(summed_ref, gate_ref, up_ref, down_ref):
    hidden_size = gate_ref.shape[1]
    gate_ref[...] = summed_ref[:, :hidden_size]
    up_ref[...] = summed_ref[:, hidden_size : 2 * hidden_size]
    down_ref[...] = summed_ref[:, 2 * hidden_size :].astype(F32).T.astype(BF16)


def split_grads(summed):
    block, width = summed.shape
    hidden_size = width // 3
    return pl.pallas_call(
        split_kernel,
        out_shape=[
            jax.ShapeDtypeStruct((block, hidden_size), BF16),
            jax.ShapeDtypeStruct((block, hidden_size), BF16),
            jax.ShapeDtypeStruct((hidden_size, block), BF16),
        ],
        name="split_grads",
    )(summed)


def on_device(
    tokens, cotangent, gate_scores, expert_ids, slot_index, gate_weight, up_weight, down_weight
):
    experts = lax.axis_size("expert")
    count, features = tokens.shape
    capacity = 2 * count // experts
    gate, up, down = gate_weight[0], up_weight[0], down_weight[0]
    send = dispatch(expert_ids, slot_index, gate_scores, tokens, cotangent, experts, capacity)
    received = lax.all_to_all(
        send.reshape(experts, 2 * capacity, features),
        "expert", split_axis=0, concat_axis=0, tiled=True,
    ).reshape(send.shape)
    grads, inner, score = expert_grads(received, gate, up, down, capacity)
    summed = lax.psum_scatter(grads, "dp", scatter_dimension=0, tiled=True)
    back = return_rows(inner, score, gate, up, capacity)
    returned = lax.all_to_all(
        back.reshape(experts, 2 * capacity, back.shape[1]),
        "expert", split_axis=0, concat_axis=0, tiled=True,
    ).reshape(back.shape)
    token_grad, score_grad = combine(
        expert_ids, slot_index, gate_scores, returned, features, capacity
    )
    grad_gate, grad_up, grad_down = split_grads(summed)
    return token_grad, score_grad.reshape(count), grad_gate[None], grad_up[None], grad_down[None]


def solution(mesh):
    both = ("expert", "dp")
    return jax.shard_map(
        on_device,
        mesh=mesh,
        in_specs=(
            P(both, None),
            P(both, None),
            P(both),
            P(both),
            P(both),
            P("expert", None, None),
            P("expert", None, None),
            P("expert", None, None),
        ),
        out_specs=(
            P(both, None),
            P(both),
            P("expert", "dp", None),
            P("expert", "dp", None),
            P("expert", None, "dp"),
        ),
        check_vma=False,
    )
```

time: 413 us -> 222 us (0.54)
  the two profiles are of different devices: /device:TPU:2 before, /device:TPU:20 now
where the time goes in v1:
time: 222 us
  blocking collectives  107 us (48%)
  waiting for transfers between devices  79.5 us (36%)
  between operations  14.1 us (6%)
  Pallas kernels  13 us (6%)
  local copies, waits for them, and re-layouts  7.66 us (3%)
    reduce_scatter x1, waiting for transfers between devices, on_device(): summed = lax.psum_scatter(grads, 'dp', scatter_dimension=0, tiled=True)  79.4 us
    all_to_all x1, blocking collectives, on_device(): lax.all_to_all(send.reshape(experts, 2 * capacity, features), 'expert', s...  64.3 us
    all_to_all x1, blocking collectives, on_device(): lax.all_to_all(back.reshape(experts, 2 * capacity, back.shape[1]), 'exper...  43.2 us
    unnamed x28, local copies, waits for them, and re-layouts  7.66 us
    pallas_call x1, Pallas kernels, expert_grads(): pl.pallas_call(functools.partial(expert_kernel, capacity), grid=(features...  6.21 us
  transfers between devices with their start and end apart: 1, of which 1 were waited for; matrix products, arithmetic and copies ran while one was open for 0% of the time, Pallas kernels for 1%

profile of v1, /device:TPU:20, one launch (start us, length us, event | category | flops | bytes accessed | tf_op | source)
XLA Modules:
  0.0 221.8 jit_solution(9691554701497792286)
XLA Ops:
  7.2 0.0 reduce-scatter.2.cloned.1.call-start
  7.2 0.0 copy-start.4
  7.2 1.0 copy-done.4
  8.3 0.0 copy-start.5
  8.3 1.0 copy-done.5
  9.3 0.0 copy-start.8
  9.3 0.7 copy-done.8
  10.0 0.0 copy-start.10
  10.0 0.7 copy-done.10
  10.6 0.0 copy-start.12
  10.6 0.7 copy-done.12
  11.3 0.0 copy-start.3
  11.3 1.9 dispatch.1
  13.2 0.0 copy-start
  13.2 0.0 copy-start.1
  13.2 64.3 %all_to_all.10 = bf16[64,8,2048]{2,1,0:T(8,128)(2,1)S(1)} all-to-all(bf16[64,8,2048]{2,1,0:T(8,128)(2,1)S(1)} %bitcast.15), channel_id=1, replica_groups=mesh['expert'=64,'dp'=16] {'expert'}, dimensions={0} | all-to-all | bytes 4194304 | tf_op jit(solution)/shard_map/all_to_all | solution.py:222
  77.5 0.0 copy-done.3
  77.5 0.0 copy-done
  77.5 0.0 copy-done.1
  77.5 6.2 %expert_grads.1 = (bf16[2048,1152]{1,0:T(8,128)(2,1)S(1)}, bf16[256,768]{1,0:T(8,128)(2,1)S(1)}, bf16[256,128]{1,0:T(8,128)(2,1)S(1)}) custom-call(bf16[512,2048]{1,0:T(8,128)(2,1)S(1)} %bitcast.14, bf16[2048,384]{1,0:T(8,128)(2,1)S(1)} %bitcast.16, bf16[2048,384]{1,0:T(8,128)(2,1)S(1)} %bitcast.18, bf16[384,2048]{1,0:T(8,128)(2,1)S(1)} %bitcast.22), custom_call_target="tpu_custom_call" | custom-call | tf_op jit(solution)/shard_map/expert_grads/pallas_call | solution.py:105
  83.7 0.0 copy-start.2
  83.7 2.1 copy-done.2
  85.8 0.0 copy-start.6
  85.8 0.6 copy-done.6
  86.5 0.0 reduce-scatter.2.cloned.1.call-update
  86.5 0.0 copy-start.7
  86.5 0.8 copy-done.7
  87.3 1.9 return_rows.1
  89.2 0.0 copy-start.9
  89.2 0.0 copy-start.11
  89.3 0.0 copy-start.13
  89.3 43.2 %all_to_all.11 = bf16[64,8,1152]{2,1,0:T(8,128)(2,1)S(1)} all-to-all(bf16[64,8,1152]{2,1,0:T(8,128)(2,1)S(1)} %bitcast.21), channel_id=1, replica_groups=mesh['expert'=64,'dp'=16] {'expert'}, dimensions={0} | all-to-all | bytes 2359296 | tf_op jit(solution)/shard_map/all_to_all | solution.py:229
  132.5 0.0 copy-done.9
  132.5 0.0 copy-done.11
  132.5 0.0 copy-done.13
  132.5 1.3 combine.1
  133.8 79.4 %reduce-scatter.2.cloned.1.call-done.summed_ref = bf16[128,1152]{1,0:T(8,128)(2,1)} async-done(((bf16[2048,1152]{1,0:T(8,128)(2,1)}), bf16[128,1152]{1,0:T(8,128)(2,1)}) %reduce-scatter.2.cloned.1.call-update) | async-done | bytes 294928 | tf_op jit(solution)/shard_map/reduce_scatter | solution.py:227
  213.2 1.7 split_grads.1
Async XLA Ops:
  7.2 206.1 %reduce-scatter.2.cloned.1.call-start = ((), (), s32[]{:S(2)}) async-start(), calls=%async_computation.3 | async-start | bytes 5013504 | tf_op jit(solution)/shard_map/reduce_scatter | solution.py:227
  7.2 1.0 copy-start.4
  8.3 1.0 copy-start.5
  9.3 0.7 copy-start.8
  10.0 0.7 copy-start.10
  10.6 0.7 copy-start.12
  11.3 66.2 %copy-start.3 = (bf16[1,384,2048]{2,1,0:T(8,128)(2,1)S(1)}, bf16[1,384,2048]{2,1,0:T(8,128)(2,1)}, u32[]{:S(2)}) copy-start(bf16[1,384,2048]{2,1,0:T(8,128)(2,1)} %param.15) | copy-start | bytes 4718596
  13.2 64.3 %copy-start = (bf16[1,2048,384]{2,1,0:T(8,128)(2,1)S(1)}, bf16[1,2048,384]{2,1,0:T(8,128)(2,1)}, u32[]{:S(2)}) copy-start(bf16[1,2048,384]{2,1,0:T(8,128)(2,1)} %param.13) | copy-start | bytes 4718596
  13.2 64.3 %copy-start.1 = (bf16[1,2048,384]{2,1,0:T(8,128)(2,1)S(1)}, bf16[1,2048,384]{2,1,0:T(8,128)(2,1)}, u32[]{:S(2)}) copy-start(bf16[1,2048,384]{2,1,0:T(8,128)(2,1)} %param.14) | copy-start | bytes 4718596
  83.7 2.1 copy-start.2
  85.8 0.6 copy-start.6
  86.5 0.8 copy-start.7
  89.2 43.2 %copy-start.9 = (s32[128]{0:T(128)S(1)}, s32[128]{0:T(128)}, u32[]{:S(2)}) copy-start(s32[128]{0:T(128)} %param.11) | copy-start | bytes 1540
  89.2 43.2 %copy-start.11 = (s32[128]{0:T(128)S(1)}, s32[128]{0:T(128)}, u32[]{:S(2)}) copy-start(s32[128]{0:T(128)} %param.12) | copy-start | bytes 1540
  89.3 43.2 %copy-start.13 = (bf16[128]{0:T(256)(128)(2,1)S(1)}, bf16[128]{0:T(256)(128)(2,1)}, u32[]{:S(2)}) copy-start(bf16[128]{0:T(256)(128)(2,1)} %param.10) | copy-start | bytes 772
Sparse Core Ops, SparseCore 0:
  86.6 126.5 reduce-scatter.1

commit v2 on v1

--- a/solution.py
+++ b/solution.py
@@ -43,7 +43,7 @@
         in_specs=[small, small, small, wide, wide],
         out_specs=pl.BlockSpec((rows, block), lambda i: (0, i)),
         out_shape=jax.ShapeDtypeStruct((rows, features), BF16),
-        compiler_params=pltpu.CompilerParams(vmem_limit_bytes=24 * 2**20),
+        compiler_params=pltpu.CompilerParams(vmem_limit_bytes=60 * 2**20),
         name="dispatch",
     )(
         expert_ids.reshape(1, count),
@@ -62,14 +62,15 @@
 
 
 def expert_kernel(
-    capacity, recv_ref, gate_ref, up_ref, down_ref, grads_ref, inner_ref, score_ref,
+    capacity, side_ref, recv_ref, gate_ref, up_ref, down_ref, grads_ref, inner_ref, score_ref,
     inputs, scaled, hidden_sc, inner_sc,
 ):
     rows = recv_ref.shape[0]
     slots = rows // 2
     hidden_size = gate_ref.shape[1]
-    block = grads_ref.shape[0]
+    block = grads_ref.shape[0] // 2
     step = pl.program_id(0)
+    side = side_ref[0]
 
     @pl.when(step == 0)
     def _():
@@ -91,40 +92,51 @@
         score = jnp.sum(hidden.astype(F32) * hidden_grad, axis=1, keepdims=True)
         score_ref[...] = jnp.broadcast_to(score, score_ref.shape).astype(BF16)
 
-    columns = pl.ds(pl.multiple_of(step * block, block), block)
-    grads_ref[:, : 2 * hidden_size] = dot(inputs[:, columns], inner_sc[...], 0, 0).astype(BF16)
-    grads_ref[:, 2 * hidden_size :] = dot(scaled[:, columns], hidden_sc[...], 0, 0).astype(BF16)
-
-
-def expert_grads(received, gate, up, down, capacity):
+    for piece in range(2):
+        owner = side if piece else 1 - side
+        first = (owner * pl.num_programs(0) + step) * block
+        columns = pl.ds(pl.multiple_of(first, block), block)
+        rows_out = slice(piece * block, (piece + 1) * block)
+        grads_ref[rows_out, : 2 * hidden_size] = dot(
+            inputs[:, columns], inner_sc[...], 0, 0
+        ).astype(BF16)
+        grads_ref[rows_out, 2 * hidden_size :] = dot(
+            scaled[:, columns], hidden_sc[...], 0, 0
+        ).astype(BF16)
+
+
+def expert_grads(side, ring, received, gate, up, down, capacity):
     rows, features = received.shape
     hidden_size = gate.shape[1]
     slots = rows // 2
-    block = min(256, features)
-    whole = lambda shape: pl.BlockSpec(shape, lambda i: (0, 0))
+    block = features // ring
+    whole = lambda shape: pl.BlockSpec(shape, lambda i, side: (0, 0))
     return pl.pallas_call(
         functools.partial(expert_kernel, capacity),
-        grid=(features // block,),
-        in_specs=[whole(received.shape), whole(gate.shape), whole(up.shape), whole(down.shape)],
-        out_specs=[
-            pl.BlockSpec((block, 3 * hidden_size), lambda i: (i, 0)),
-            whole((slots, 2 * hidden_size)),
-            whole((slots, LANES)),
-        ],
+        grid_spec=pltpu.PrefetchScalarGridSpec(
+            num_scalar_prefetch=1,
+            grid=(ring,),
+            in_specs=[whole(received.shape), whole(gate.shape), whole(up.shape), whole(down.shape)],
+            out_specs=[
+                pl.BlockSpec((block, 3 * hidden_size), lambda i, side: (i, 0)),
+                whole((slots, 2 * hidden_size)),
+                whole((slots, LANES)),
+            ],
+            scratch_shapes=[
+                pltpu.VMEM((slots, features), BF16),
+                pltpu.VMEM((slots, features), BF16),
+                pltpu.VMEM((slots, hidden_size), BF16),
+                pltpu.VMEM((slots, 2 * hidden_size), BF16),
+            ],
+        ),
         out_shape=[
-            jax.ShapeDtypeStruct((features, 3 * hidden_size), BF16),
+            pltpu.HBM((features, 3 * hidden_size), BF16),
             jax.ShapeDtypeStruct((slots, 2 * hidden_size), BF16),
             jax.ShapeDtypeStruct((slots, LANES), BF16),
         ],
-        scratch_shapes=[
-            pltpu.VMEM((slots, features), BF16),
-            pltpu.VMEM((slots, features), BF16),
-            pltpu.VMEM((slots, hidden_size), BF16),
-            pltpu.VMEM((slots, 2 * hidden_size), BF16),
-        ],
         compiler_params=pltpu.CompilerParams(vmem_limit_bytes=40 * 2**20),
         name="expert_grads",
-    )(received, gate, up, down)
+    )(side, received, gate, up, down)
 
 
 def return_kernel(capacity, inner_ref, score_ref, gate_ref, up_ref, out_ref):
@@ -190,25 +202,36 @@
     )
 
 
-def split_kernel(summed_ref, gate_ref, up_ref, down_ref):
+def split_kernel(kept_ref, arrived_ref, gate_ref, up_ref, down_ref):
     hidden_size = gate_ref.shape[1]
-    gate_ref[...] = summed_ref[:, :hidden_size]
-    up_ref[...] = summed_ref[:, hidden_size : 2 * hidden_size]
-    down_ref[...] = summed_ref[:, 2 * hidden_size :].astype(F32).T.astype(BF16)
-
-
-def split_grads(summed):
-    block, width = summed.shape
+    total = kept_ref[...].astype(F32) + arrived_ref[...].astype(F32)
+    gate_ref[...] = total[:, :hidden_size].astype(BF16)
+    up_ref[...] = total[:, hidden_size : 2 * hidden_size].astype(BF16)
+    down_ref[...] = total[:, 2 * hidden_size :].T.astype(BF16)
+
+
+def split_grads(summed, arrived):
+    block, width = arrived.shape
     hidden_size = width // 3
     return pl.pallas_call(
         split_kernel,
+        grid=(1,),
+        in_specs=[
+            pl.BlockSpec((block, width), lambda i: (1, 0)),
+            pl.BlockSpec((block, width), lambda i: (0, 0)),
+        ],
+        out_specs=[
+            pl.BlockSpec((block, hidden_size), lambda i: (0, 0)),
+            pl.BlockSpec((block, hidden_size), lambda i: (0, 0)),
+            pl.BlockSpec((hidden_size, block), lambda i: (0, 0)),
+        ],
         out_shape=[
             jax.ShapeDtypeStruct((block, hidden_size), BF16),
             jax.ShapeDtypeStruct((block, hidden_size), BF16),
             jax.ShapeDtypeStruct((hidden_size, block), BF16),
         ],
         name="split_grads",
-    )(summed)
+    )(summed, arrived)
 
 
 def on_device(
@@ -223,8 +246,16 @@
         send.reshape(experts, 2 * capacity, features),
         "expert", split_axis=0, concat_axis=0, tiled=True,
     ).reshape(send.shape)
-    grads, inner, score = expert_grads(received, gate, up, down, capacity)
-    summed = lax.psum_scatter(grads, "dp", scatter_dimension=0, tiled=True)
+    ring = lax.axis_size("dp") // 2
+    side = (lax.axis_index("dp") >= ring).astype(jnp.int32).reshape(1)
+    grads, inner, score = expert_grads(side, ring, received, gate, up, down, capacity)
+    summed = lax.psum_scatter(
+        grads, "dp", scatter_dimension=0, tiled=True,
+        axis_index_groups=[[s * ring + i for i in range(ring)] for s in range(2)],
+    )
+    arrived = lax.ppermute(
+        summed[: summed.shape[0] // 2], "dp", [(i, (i + ring) % (2 * ring)) for i in range(2 * ring)]
+    )
     back = return_rows(inner, score, gate, up, capacity)
     returned = lax.all_to_all(
         back.reshape(experts, 2 * capacity, back.shape[1]),
@@ -233,7 +264,7 @@
     token_grad, score_grad = combine(
         expert_ids, slot_index, gate_scores, returned, features, capacity
     )
-    grad_gate, grad_up, grad_down = split_grads(summed)
+    grad_gate, grad_up, grad_down = split_grads(summed, arrived)
     return token_grad, score_grad.reshape(count), grad_gate[None], grad_up[None], grad_down[None]
 
 

time: 222 us -> 194 us (0.87)
  the two profiles are of different devices: /device:TPU:20 before, /device:TPU:1 now
where the time goes in v2:
time: 194 us; the launch traced here: 193 us
  waiting for transfers between devices  121 us (62%)
  starting transfers between devices  30.1 us (16%)
  Pallas kernels  17.9 us (9%)
  between operations  14.1 us (7%)
  local copies, waits for them, and re-layouts  10.3 us (5%)
    reduce_scatter x1, waiting for transfers between devices, on_device(): lax.psum_scatter(grads, 'dp', scatter_dimension=0, tiled=True, axis_index...  62.5 us
    all_to_all x1, waiting for transfers between devices, on_device(): lax.all_to_all(send.reshape(experts, 2 * capacity, features), 'expert', s...  52.8 us
    all_to_all x1, starting transfers between devices, on_device(): lax.all_to_all(send.reshape(experts, 2 * capacity, features), 'expert', s...  18.3 us
    unnamed x24, local copies, waits for them, and re-layouts  9.31 us
    all_to_all x1, starting transfers between devices, on_device(): lax.all_to_all(back.reshape(experts, 2 * capacity, back.shape[1]), 'exper...  8.6 us
    pallas_call x1, Pallas kernels, expert_grads(): pl.pallas_call(functools.partial(expert_kernel, capacity), grid_spec=pltp...  8.37 us
    ppermute x1, waiting for transfers between devices, on_device(): lax.ppermute(summed[:summed.shape[0] // 2], 'dp', [(i, (i + ring) % (2 *...  5.35 us
    pallas_call x1, Pallas kernels, dispatch(): pl.pallas_call(functools.partial(dispatch_kernel, capacity), grid=(featur...  4.5 us
  transfers between devices with their start and end apart: 4, of which 3 were waited for; matrix products, arithmetic and copies ran while one was open for 1% of the time, Pallas kernels for 2%

profile of v2, /device:TPU:1, one launch (start us, length us, event | category | flops | bytes accessed | tf_op | source)
XLA Modules:
  0.0 193.0 jit_solution(4680861646239547947)
XLA Ops:
  7.2 4.5 %dispatch.1 = bf16[512,2048]{1,0:T(8,128)(2,1)} custom-call(s32[1,128]{1,0:T(1,128)} %bitcast.23, s32[1,128]{1,0:T(1,128)} %bitcast.25, bf16[1,128]{1,0:T(2,128)(2,1)} %bitcast.27, bf16[128,2048]{1,0:T(8,128)(2,1)} %tokens_ref.1, bf16[128,2048]{1,0:T(8,128)(2,1)} %cotan_ref.1), custom_call_target="tpu_custom_call" | custom-call | tf_op jit(solution)/shard_map/dispatch/pallas_call | solution.py:40
  11.7 18.3 %all-to-all-start = ((bf16[64,8,2048]{2,1,0:T(8,128)(2,1)}), bf16[64,8,2048]{2,1,0:T(8,128)(2,1)S(1)}, u32[]{:S(2)}, u32[]{:S(2)}) async-start(bf16[64,8,2048]{2,1,0:T(8,128)(2,1)} %bitcast.29), calls=%async_computation | async-start | bytes 4194304 | tf_op jit(solution)/shard_map/all_to_all | solution.py:245
  30.0 0.0 reduce-scatter.2.cloned.1.call-start
  30.0 52.8 %all-to-all-done = bf16[64,8,2048]{2,1,0:T(8,128)(2,1)S(1)} async-done(((bf16[64,8,2048]{2,1,0:T(8,128)(2,1)}), bf16[64,8,2048]{2,1,0:T(8,128)(2,1)S(1)}, u32[]{:S(2)}, u32[]{:S(2)}) %all-to-all-start) | async-done | bytes 2097184 | tf_op jit(solution)/shard_map/all_to_all | solution.py:245
  82.8 0.0 copy-start
  82.8 1.4 copy-done
  84.2 0.0 copy-start.2
  84.2 1.4 copy-done.2
  85.6 0.0 copy-start.5
  85.6 1.4 copy-done.5
  87.0 8.4 %expert_grads.1 = (bf16[2048,1152]{1,0:T(8,128)(2,1)}, bf16[256,768]{1,0:T(8,128)(2,1)S(1)}, bf16[256,128]{1,0:T(8,128)(2,1)S(1)}) custom-call(s32[1]{0:T(128)} %bitcast.3.side_ref, bf16[512,2048]{1,0:T(8,128)(2,1)S(1)} %bitcast.15, bf16[2048,384]{1,0:T(8,128)(2,1)S(1)} %bitcast.16, bf16[2048,384]{1,0:T(8,128)(2,1)S(1)} %bitcast.18, ...), custom_call_target="tpu_custom_call" | custom-call | tf_op jit(solution)/shard_map/expert_grads/pallas_call | solution.py:114
  95.4 0.0 copy-start.6
  95.4 0.6 copy-done.6
  96.0 0.0 copy-start.1
  96.0 0.0 copy-start.3
  96.0 0.0 reduce-scatter.2.cloned.1.call-update
  96.1 1.4 copy-done.1
  97.5 0.5 copy-done.3
  97.9 0.0 copy-start.7
  97.9 0.8 copy-done.7
  98.8 1.9 return_rows.1
  100.7 0.0 copy-start.4
  100.7 1.0 copy-done.4
  101.7 0.0 copy-start.8
  101.7 0.0 copy-start.9
  101.7 0.0 copy-start.10
  101.7 8.6 %all-to-all-start.1 = ((bf16[64,8,1152]{2,1,0:T(8,128)(2,1)}), bf16[64,8,1152]{2,1,0:T(8,128)(2,1)S(1)}, u32[]{:S(2)}, u32[]{:S(2)}) async-start(bf16[64,8,1152]{2,1,0:T(8,128)(2,1)} %bitcast.21), calls=%async_computation.1 | async-start | bytes 2359296 | tf_op jit(solution)/shard_map/all_to_all | solution.py:260
  110.3 62.5 %reduce-scatter.2.cloned.1.call-done.kept_ref = bf16[256,1152]{1,0:T(8,128)(2,1)} async-done(((bf16[2048,1152]{1,0:T(8,128)(2,1)}), bf16[256,1152]{1,0:T(8,128)(2,1)}) %reduce-scatter.2.cloned.1.call-update) | async-done | bytes 589840 | tf_op jit(solution)/shard_map/reduce_scatter | solution.py:252
  172.8 1.0 slice.4
  173.8 3.1 %collective-permute-start = (bf16[128,1152]{1,0:T(8,128)(2,1)S(1)}, bf16[128,1152]{1,0:T(8,128)(2,1)S(1)}, u32[]{:S(2)}, u32[]{:S(2)}) collective-permute-start(bf16[128,1152]{1,0:T(8,128)(2,1)S(1)} %slice.4), channel_id=1, source_target_pairs={{0,8},{1,9},{2,10},{3,11},{4,12},{5,13},{6,14},{7,15},{8,0},{9,1},... | collective-permute-start | bytes 884744 | tf_op jit(solution)/shard_map/ppermute | solution.py:256
  176.9 0.0 all-to-all-done.1
  177.0 0.0 copy-done.8
  177.0 0.0 copy-done.9
  177.0 0.0 copy-done.10
  177.0 1.3 combine.1
  178.3 5.3 %collective-permute-done.arrived_ref = bf16[128,1152]{1,0:T(8,128)(2,1)S(1)} collective-permute-done((bf16[128,1152]{1,0:T(8,128)(2,1)S(1)}, bf16[128,1152]{1,0:T(8,128)(2,1)S(1)}, u32[]{:S(2)}, u32[]{:S(2)}) %collective-permute-start) | collective-permute-done | bytes 294944 | tf_op jit(solution)/shard_map/ppermute | solution.py:256
  183.6 0.0 copy-start.11
  183.6 0.7 copy-done.11
  184.4 1.8 split_grads.1
Async XLA Ops:
  11.7 71.2 %all-to-all-start = ((bf16[64,8,2048]{2,1,0:T(8,128)(2,1)}), bf16[64,8,2048]{2,1,0:T(8,128)(2,1)S(1)}, u32[]{:S(2)}, u32[]{:S(2)}) async-start(bf16[64,8,2048]{2,1,0:T(8,128)(2,1)} %bitcast.29), calls=%async_computation | async-start | bytes 4194304 | tf_op jit(solution)/shard_map/all_to_all | solution.py:245
  30.0 142.9 %reduce-scatter.2.cloned.1.call-start = ((), (), s32[]{:S(2)}) async-start(), calls=%async_computation.3 | async-start | bytes 5308416 | tf_op jit(solution)/shard_map/reduce_scatter | solution.py:252
  82.8 1.4 copy-start
  84.2 1.4 copy-start.2
  85.6 1.4 copy-start.5
  95.4 0.6 copy-start.6
  96.0 1.4 copy-start.1
  96.0 1.9 copy-start.3
  97.9 0.8 copy-start.7
  100.7 1.1 copy-start.4
  101.7 75.2 %copy-start.8 = (s32[128]{0:T(128)S(1)}, s32[128]{0:T(128)}, u32[]{:S(2)}) copy-start(s32[128]{0:T(128)} %param.11) | copy-start | bytes 1540
  101.7 75.3 %copy-start.9 = (s32[128]{0:T(128)S(1)}, s32[128]{0:T(128)}, u32[]{:S(2)}) copy-start(s32[128]{0:T(128)} %param.12) | copy-start | bytes 1540
  101.7 75.3 %copy-start.10 = (bf16[128]{0:T(256)(128)(2,1)S(1)}, bf16[128]{0:T(256)(128)(2,1)}, u32[]{:S(2)}) copy-start(bf16[128]{0:T(256)(128)(2,1)} %param.10) | copy-start | bytes 772
  101.7 75.2 %all-to-all-start.1 = ((bf16[64,8,1152]{2,1,0:T(8,128)(2,1)}), bf16[64,8,1152]{2,1,0:T(8,128)(2,1)S(1)}, u32[]{:S(2)}, u32[]{:S(2)}) async-start(bf16[64,8,1152]{2,1,0:T(8,128)(2,1)} %bitcast.21), calls=%async_computation.1 | async-start | bytes 2359296 | tf_op jit(solution)/shard_map/all_to_all | solution.py:260
  173.8 9.8 %collective-permute-start = (bf16[128,1152]{1,0:T(8,128)(2,1)S(1)}, bf16[128,1152]{1,0:T(8,128)(2,1)S(1)}, u32[]{:S(2)}, u32[]{:S(2)}) collective-permute-start(bf16[128,1152]{1,0:T(8,128)(2,1)S(1)} %slice.4), channel_id=1, source_target_pairs={{0,8},{1,9},{2,10},{3,11},{4,12},{5,13},{6,14},{7,15},{8,0},{9,1},... | collective-permute-start | bytes 884744 | tf_op jit(solution)/shard_map/ppermute | solution.py:256
  183.6 0.7 copy-start.11
Sparse Core Ops, SparseCore 0:
  96.2 76.5 reduce-scatter.1

commit v3 on v1

v3 whole, which is shorter than its diff:
```python
import functools

import jax
import jax.numpy as jnp
from jax import lax
from jax.experimental import pallas as pl
from jax.experimental.pallas import tpu as pltpu
from jax.sharding import PartitionSpec as P

F32 = jnp.float32
BF16 = jnp.bfloat16
LANES = 128


def dot(left, right, left_dim, right_dim):
    return lax.dot_general(
        left, right, (((left_dim,), (right_dim,)), ((), ())), preferred_element_type=F32
    )


def in_hbm(*arrays):
    return [pltpu.with_memory_space_constraint(array, pltpu.HBM) for array in arrays]


def on_chip(*arrays):
    return [pltpu.with_memory_space_constraint(array, pltpu.VMEM) for array in arrays]


ANYWHERE = pl.BlockSpec(memory_space=pltpu.HBM)
ON_CHIP = pl.BlockSpec(memory_space=pltpu.VMEM)
CHUNKS = 4


def dispatch_kernel(
    capacity, ids_hbm, slot_hbm, score_hbm, tokens_hbm, cotan_hbm, out_ref,
    ids_ref, slot_ref, score_ref, rows_ref, sems,
):
    rows, (count, features) = out_ref.shape[0], tokens_hbm.shape
    chunk = features // CHUNKS
    columns = [slice(i * chunk, (i + 1) * chunk) for i in range(CHUNKS)]
    copies = [
        pltpu.make_async_copy(ids_hbm, ids_ref, sems.at[0]),
        pltpu.make_async_copy(slot_hbm, slot_ref, sems.at[1]),
        pltpu.make_async_copy(score_hbm, score_ref, sems.at[2]),
    ]
    for i, c in enumerate(columns):
        copies += [
            pltpu.make_async_copy(tokens_hbm.at[:, c], rows_ref.at[:count, c], sems.at[3 + 2 * i]),
            pltpu.make_async_copy(cotan_hbm.at[:, c], rows_ref.at[count:, c], sems.at[4 + 2 * i]),
        ]
    for copy in copies:
        copy.start()
    for copy in copies[:3]:
        copy.wait()
    position = ids_ref[...] * (2 * capacity) + slot_ref[...]
    row = lax.broadcasted_iota(jnp.int32, (rows, count), 0)
    pick_token = jnp.where(row == position, F32(1), F32(0))
    pick_cotan = jnp.where(row == position + capacity, score_ref[...].astype(F32), F32(0))
    pick = jnp.concatenate([pick_token, pick_cotan], axis=1).astype(BF16)
    for i, c in enumerate(columns):
        copies[3 + 2 * i].wait()
        copies[4 + 2 * i].wait()
        out_ref[:, c] = dot(pick, rows_ref[:, c], 1, 0).astype(BF16)


def dispatch(expert_ids, slot_index, gate_scores, tokens, cotangent, experts, capacity):
    count, features = tokens.shape
    rows = experts * 2 * capacity
    return pl.pallas_call(
        functools.partial(dispatch_kernel, capacity),
        in_specs=[ANYWHERE] * 5,
        out_specs=ON_CHIP,
        out_shape=pltpu.VMEM((rows, features), BF16),
        scratch_shapes=[
            pltpu.VMEM((1, count), jnp.int32),
            pltpu.VMEM((1, count), jnp.int32),
            pltpu.VMEM((1, count), BF16),
            pltpu.VMEM((2 * count, features), BF16),
            pltpu.SemaphoreType.DMA((3 + 2 * CHUNKS,)),
        ],
        compiler_params=pltpu.CompilerParams(vmem_limit_bytes=24 * 2**20),
        name="dispatch",
    )(
        *in_hbm(
            expert_ids.reshape(1, count),
            slot_index.reshape(1, count),
            gate_scores.reshape(1, count),
            tokens,
            cotangent,
        )
    )


def pick_rows(slots, rows, capacity, half):
    slot = lax.broadcasted_iota(jnp.int32, (slots, rows), 0)
    row = lax.broadcasted_iota(jnp.int32, (slots, rows), 1)
    wanted = (slot // capacity) * (2 * capacity) + slot % capacity + half * capacity
    return jnp.where(row == wanted, F32(1), F32(0)).astype(BF16)


def expert_kernel(
    capacity, ring, side_ref, recv_ref, gate_hbm, up_hbm, down_hbm, grads_hbm, inner_ref, score_ref,
    gate_ref, up_ref, down_ref, inputs, scaled, hidden_sc, grads_ref, sems, out_sems,
):
    rows, features = recv_ref.shape
    slots = rows // 2
    hidden_size = gate_ref.shape[1]
    side = side_ref[0]
    copies = [
        pltpu.make_async_copy(source, target, sems.at[i])
        for i, (source, target) in enumerate(
            ((gate_hbm, gate_ref), (up_hbm, up_ref), (down_hbm, down_ref))
        )
    ]
    for copy in copies:
        copy.start()
    received = recv_ref[...]
    inputs[...] = dot(pick_rows(slots, rows, capacity, 0), received, 1, 0).astype(BF16)
    scaled[...] = dot(pick_rows(slots, rows, capacity, 1), received, 1, 0).astype(BF16)
    copies[0].wait()
    pre_gate = dot(inputs[...], gate_ref[...], 1, 0)
    copies[1].wait()
    pre_up = dot(inputs[...], up_ref[...], 1, 0)
    copies[2].wait()
    hidden_grad = dot(scaled[...], down_ref[...], 1, 1)
    sigmoid = jax.nn.sigmoid(pre_gate)
    activated = pre_gate * sigmoid
    hidden = (activated * pre_up).astype(BF16)
    hidden_sc[...] = hidden
    inner_ref[:, :hidden_size] = (
        hidden_grad * pre_up * sigmoid * (1.0 + pre_gate * (1.0 - sigmoid))
    ).astype(BF16)
    inner_ref[:, hidden_size:] = (hidden_grad * activated).astype(BF16)
    score = jnp.sum(hidden.astype(F32) * hidden_grad, axis=1, keepdims=True)
    score_ref[...] = jnp.broadcast_to(score, score_ref.shape).astype(BF16)

    block = features // (2 * ring)
    writes = []
    for step in range(ring):
        for piece in range(2):
            owner = side if piece else 1 - side
            columns = pl.ds(pl.multiple_of((owner * ring + step) * block, block), block)
            first = (2 * step + piece) * block
            grads_ref[first : first + block, : 2 * hidden_size] = dot(
                inputs[:, columns], inner_ref[...], 0, 0
            ).astype(BF16)
            grads_ref[first : first + block, 2 * hidden_size :] = dot(
                scaled[:, columns], hidden_sc[...], 0, 0
            ).astype(BF16)
        done = slice(2 * step * block, 2 * (step + 1) * block)
        writes.append(
            pltpu.make_async_copy(grads_ref.at[done], grads_hbm.at[done], out_sems.at[step])
        )
        writes[-1].start()
    for write in writes:
        write.wait()


def expert_grads(side, ring, received, gate, up, down, capacity):
    rows, features = received.shape
    hidden_size = gate.shape[1]
    slots = rows // 2
    return pl.pallas_call(
        functools.partial(expert_kernel, capacity, ring),
        in_specs=[pl.BlockSpec(memory_space=pltpu.SMEM), ON_CHIP, ANYWHERE, ANYWHERE, ANYWHERE],
        out_specs=[ANYWHERE, ON_CHIP, ON_CHIP],
        out_shape=[
            pltpu.HBM((features, 3 * hidden_size), BF16),
            pltpu.VMEM((slots, 2 * hidden_size), BF16),
            pltpu.VMEM((slots, LANES), BF16),
        ],
        scratch_shapes=[
            pltpu.VMEM(gate.shape, BF16),
            pltpu.VMEM(up.shape, BF16),
            pltpu.VMEM(down.shape, BF16),
            pltpu.VMEM((slots, features), BF16),
            pltpu.VMEM((slots, features), BF16),
            pltpu.VMEM((slots, hidden_size), BF16),
            pltpu.VMEM((features, 3 * hidden_size), BF16),
            pltpu.SemaphoreType.DMA((3,)),
            pltpu.SemaphoreType.DMA((ring,)),
        ],
        compiler_params=pltpu.CompilerParams(vmem_limit_bytes=40 * 2**20),
        name="expert_grads",
    )(side, *on_chip(received), *in_hbm(gate, up, down))


def return_kernel(capacity, inner_ref, score_ref, gate_ref, up_ref, out_ref):
    slots = inner_ref.shape[0]
    rows = out_ref.shape[0]
    hidden_size = gate_ref.shape[1]
    half = gate_ref.shape[0] // 2
    total = jnp.zeros((rows, half), F32)
    for part in range(2):
        piece = pl.ds(part * half, half)
        input_grad = dot(inner_ref[:, :hidden_size], gate_ref[piece, :], 1, 1) + dot(
            inner_ref[:, hidden_size:], up_ref[piece, :], 1, 1
        )
        spread = pick_rows(slots, rows, capacity, part)
        total += dot(spread, input_grad.astype(BF16), 0, 0)
        if part == 0:
            out_ref[:, half:] = dot(spread, score_ref[...], 0, 0).astype(BF16)
    out_ref[:, :half] = total.astype(BF16)


def return_rows(inner, score, gate, up, capacity):
    slots = inner.shape[0]
    half = gate.shape[0] // 2
    return pl.pallas_call(
        functools.partial(return_kernel, capacity),
        out_shape=jax.ShapeDtypeStruct((2 * slots, half + LANES), BF16),
        compiler_params=pltpu.CompilerParams(vmem_limit_bytes=40 * 2**20),
        name="return_rows",
    )(*on_chip(inner, score), gate, up)


def combine_kernel(capacity, ids_ref, slot_ref, score_ref, rows_ref, token_ref, grad_ref):
    rows = rows_ref.shape[0]
    count = token_ref.shape[0]
    half = token_ref.shape[1] // 2
    position = ids_ref[...] * (2 * capacity) + slot_ref[...]
    row = lax.broadcasted_iota(jnp.int32, (rows, count), 0)
    for part in range(2):
        pick = jnp.where(row == position + part * capacity, F32(1), F32(0)).astype(BF16)
        token_ref[:, part * half : (part + 1) * half] = dot(
            pick, rows_ref[:, :half], 0, 0
        ).astype(BF16)
        if part == 0:
            score = dot(rows_ref[:, half:], pick, 0, 0)
            grad_ref[...] = (score[0:1, :] / score_ref[...].astype(F32)).astype(BF16)


def combine(expert_ids, slot_index, gate_scores, rows, features, capacity):
    count = expert_ids.shape[0]
    return pl.pallas_call(
        functools.partial(combine_kernel, capacity),
        out_shape=[
            jax.ShapeDtypeStruct((count, features), BF16),
            jax.ShapeDtypeStruct((1, count), BF16),
        ],
        compiler_params=pltpu.CompilerParams(vmem_limit_bytes=24 * 2**20),
        name="combine",
    )(
        expert_ids.reshape(1, count),
        slot_index.reshape(1, count),
        gate_scores.reshape(1, count),
        rows,
    )


def halves_kernel(summed_hbm, sent_ref, kept_ref, sems):
    block = sent_ref.shape[0]
    copies = [
        pltpu.make_async_copy(summed_hbm.at[:block], sent_ref, sems.at[0]),
        pltpu.make_async_copy(summed_hbm.at[block:], kept_ref, sems.at[1]),
    ]
    for copy in copies:
        copy.start()
    for copy in copies:
        copy.wait()


def halves(summed):
    half = (summed.shape[0] // 2, summed.shape[1])
    return pl.pallas_call(
        halves_kernel,
        in_specs=[ANYWHERE],
        out_specs=[ON_CHIP, ON_CHIP],
        out_shape=[pltpu.VMEM(half, BF16), pltpu.VMEM(half, BF16)],
        scratch_shapes=[pltpu.SemaphoreType.DMA((2,))],
        name="halves",
    )(*in_hbm(summed))


def split_kernel(kept_ref, arrived_ref, gate_ref, up_ref, down_ref):
    hidden_size = gate_ref.shape[1]
    total = kept_ref[...].astype(F32) + arrived_ref[...].astype(F32)
    gate_ref[...] = total[:, :hidden_size].astype(BF16)
    up_ref[...] = total[:, hidden_size : 2 * hidden_size].astype(BF16)
    down_ref[...] = total[:, 2 * hidden_size :].T.astype(BF16)


def split_grads(kept, arrived):
    block, width = arrived.shape
    hidden_size = width // 3
    return pl.pallas_call(
        split_kernel,
        in_specs=[ON_CHIP, ON_CHIP],
        out_shape=[
            jax.ShapeDtypeStruct((block, hidden_size), BF16),
            jax.ShapeDtypeStruct((block, hidden_size), BF16),
            jax.ShapeDtypeStruct((hidden_size, block), BF16),
        ],
        name="split_grads",
    )(*on_chip(kept, arrived))


def on_device(
    tokens, cotangent, gate_scores, expert_ids, slot_index, gate_weight, up_weight, down_weight
):
    experts = lax.axis_size("expert")
    count, features = tokens.shape
    capacity = 2 * count // experts
    gate, up, down = gate_weight[0], up_weight[0], down_weight[0]
    send = dispatch(expert_ids, slot_index, gate_scores, tokens, cotangent, experts, capacity)
    received = lax.all_to_all(
        send.reshape(experts, 2 * capacity, features),
        "expert", split_axis=0, concat_axis=0, tiled=True,
    ).reshape(send.shape)
    ring = lax.axis_size("dp") // 2
    side = (lax.axis_index("dp") >= ring).astype(jnp.int32).reshape(1)
    grads, inner, score = expert_grads(side, ring, received, gate, up, down, capacity)
    summed = lax.psum_scatter(
        grads, "dp", scatter_dimension=0, tiled=True,
        axis_index_groups=[[s * ring + i for i in range(ring)] for s in range(2)],
    )
    back = return_rows(inner, score, gate, up, capacity)
    returned = lax.all_to_all(
        back.reshape(experts, 2 * capacity, back.shape[1]),
        "expert", split_axis=0, concat_axis=0, tiled=True,
    ).reshape(back.shape)
    summed, returned = lax.optimization_barrier((summed, returned))
    sent, kept = halves(summed)
    arrived = lax.ppermute(sent, "dp", [(i, (i + ring) % (2 * ring)) for i in range(2 * ring)])
    token_grad, score_grad = combine(
        expert_ids, slot_index, gate_scores, returned, features, capacity
    )
    grad_gate, grad_up, grad_down = split_grads(kept, arrived)
    return token_grad, score_grad.reshape(count), grad_gate[None], grad_up[None], grad_down[None]


def solution(mesh):
    both = ("expert", "dp")
    return jax.shard_map(
        on_device,
        mesh=mesh,
        in_specs=(
            P(both, None),
            P(both, None),
            P(both),
            P(both),
            P(both),
            P("expert", None, None),
            P("expert", None, None),
            P("expert", None, None),
        ),
        out_specs=(
            P(both, None),
            P(both),
            P("expert", "dp", None),
            P("expert", "dp", None),
            P("expert", None, "dp"),
        ),
        check_vma=False,
    )
```

time: 222 us -> 186 us (0.84)
  the two profiles are of different devices: /device:TPU:20 before, /device:TPU:1 now
where the time goes in v3:
time: 186 us; the launch traced here: 185 us
  waiting for transfers between devices  90.2 us (48%)
  blocking collectives  40.7 us (22%)
  starting transfers between devices  21.5 us (12%)
  Pallas kernels  14.2 us (8%)
  between operations  14.1 us (8%)
  local copies, waits for them, and re-layouts  4.66 us (3%)
    all_to_all x1, waiting for transfers between devices, on_device(): lax.all_to_all(send.reshape(experts, 2 * capacity, features), 'expert', s...  52.8 us
    all_to_all x1, blocking collectives, on_device(): lax.all_to_all(back.reshape(experts, 2 * capacity, back.shape[1]), 'exper...  40.7 us
    reduce_scatter x1, waiting for transfers between devices, on_device(): lax.psum_scatter(grads, 'dp', scatter_dimension=0, tiled=True, axis_index...  32 us
    all_to_all x1, starting transfers between devices, on_device(): lax.all_to_all(send.reshape(experts, 2 * capacity, features), 'expert', s...  18.3 us
    pallas_call x1, Pallas kernels, expert_grads(): pl.pallas_call(functools.partial(expert_kernel, capacity, ring), in_specs...  6.85 us
    ppermute x1, waiting for transfers between devices, on_device(): lax.ppermute(sent, 'dp', [(i, (i + ring) % (2 * ring)) for i in range(2 *...  5.35 us
    unnamed x16, local copies, waits for them, and re-layouts  4.66 us
  transfers between devices with their start and end apart: 3, of which 3 were waited for; matrix products, arithmetic and copies ran while one was open for 0% of the time, Pallas kernels for 2%

profile of v3, /device:TPU:1, one launch (start us, length us, event | category | flops | bytes accessed | tf_op | source)
XLA Modules:
  0.0 185.4 jit_solution(17482799005607547588)
XLA Ops:
  7.2 2.3 %dispatch.1 = bf16[512,2048]{1,0:T(8,128)(2,1)S(1)} custom-call(s32[1,128]{1,0:T(1,128)} %bitcast.23, s32[1,128]{1,0:T(1,128)} %bitcast.25, bf16[1,128]{1,0:T(2,128)(2,1)} %bitcast.27, bf16[128,2048]{1,0:T(8,128)(2,1)} %tokens_hbm.1, bf16[128,2048]{1,0:T(8,128)(2,1)} %cotan_hbm.1), custom_call_target="tpu_custom_call" | custom-call | tf_op jit(solution)/shard_map/dispatch/pallas_call | solution.py:69
  9.5 0.0 copy-start
  9.5 1.3 copy-done
  10.8 18.3 %all-to-all-start = ((bf16[64,8,2048]{2,1,0:T(8,128)(2,1)}), bf16[64,8,2048]{2,1,0:T(8,128)(2,1)S(1)}, u32[]{:S(2)}, u32[]{:S(2)}) async-start(bf16[64,8,2048]{2,1,0:T(8,128)(2,1)} %bitcast.16), calls=%async_computation | async-start | bytes 4194304 | tf_op jit(solution)/shard_map/all_to_all | solution.py:306
  29.1 0.0 reduce-scatter.2.cloned.1.call-start
  29.2 52.8 %all-to-all-done = bf16[64,8,2048]{2,1,0:T(8,128)(2,1)S(1)} async-done(((bf16[64,8,2048]{2,1,0:T(8,128)(2,1)}), bf16[64,8,2048]{2,1,0:T(8,128)(2,1)S(1)}, u32[]{:S(2)}, u32[]{:S(2)}) %all-to-all-start) | async-done | bytes 2097184 | tf_op jit(solution)/shard_map/all_to_all | solution.py:306
  82.0 6.8 %expert_grads.1 = (bf16[2048,1152]{1,0:T(8,128)(2,1)}, bf16[256,768]{1,0:T(8,128)(2,1)S(1)}, bf16[256,128]{1,0:T(8,128)(2,1)S(1)}) custom-call(s32[1]{0:T(128)} %bitcast.3.side_ref, bf16[512,2048]{1,0:T(8,128)(2,1)S(1)} %bitcast.15, bf16[2048,384]{1,0:T(8,128)(2,1)} %bitcast.17, bf16[2048,384]{1,0:T(8,128)(2,1)} %bitcast.19, bf16[384,2048]{1,0:T(8,128)(2,1)} %bitcast.29), custom_call_target="tpu_custom_call" | custom-call | tf_op jit(solution)/shard_map/expert_grads/pallas_call | solution.py:163
  88.8 0.0 copy-start.3
  88.8 0.6 copy-done.3
  89.5 0.0 copy-start.1
  89.5 0.0 copy-start.2
  89.5 0.0 reduce-scatter.2.cloned.1.call-update
  89.5 1.4 copy-done.1
  90.9 0.5 copy-done.2
  91.3 0.0 copy-start.4
  91.3 0.8 copy-done.4
  92.2 1.9 %return_rows.1 = bf16[512,1152]{1,0:T(8,128)(2,1)S(1)} custom-call(bf16[256,768]{1,0:T(8,128)(2,1)S(1)} %get-tuple-element.18.inner_ref, bf16[256,128]{1,0:T(8,128)(2,1)S(1)} %copy-done.4, bf16[2048,384]{1,0:T(8,128)(2,1)S(1)} %bitcast.18, bf16[2048,384]{1,0:T(8,128)(2,1)S(1)} %bitcast.20), custom_call_target="tpu_custom_call" | custom-call | tf_op jit(solution)/shard_map/return_rows/pallas_call | solution.py:209
  94.1 0.0 copy-start.5
  94.1 0.0 copy-start.6
  94.1 0.0 copy-start.7
  94.1 40.7 %all_to_all.10 = bf16[64,8,1152]{2,1,0:T(8,128)(2,1)S(1)} all-to-all(bf16[64,8,1152]{2,1,0:T(8,128)(2,1)S(1)} %bitcast.22), channel_id=1, replica_groups=mesh['expert'=64,'dp'=16] {'expert'}, dimensions={0} | all-to-all | bytes 2359296 | tf_op jit(solution)/shard_map/all_to_all | solution.py:318
  134.8 32.0 %reduce-scatter.2.cloned.1.call-done.summed_hbm = bf16[256,1152]{1,0:T(8,128)(2,1)} async-done(((bf16[2048,1152]{1,0:T(8,128)(2,1)}), bf16[256,1152]{1,0:T(8,128)(2,1)}) %reduce-scatter.2.cloned.1.call-update) | async-done | bytes 589840 | tf_op jit(solution)/shard_map/reduce_scatter | solution.py:313
  166.8 1.1 halves.1
  167.9 3.1 %collective-permute-start = (bf16[128,1152]{1,0:T(8,128)(2,1)S(1)}, bf16[128,1152]{1,0:T(8,128)(2,1)S(1)}, u32[]{:S(2)}, u32[]{:S(2)}) collective-permute-start(bf16[128,1152]{1,0:T(8,128)(2,1)S(1)} %get-tuple-element.25), channel_id=1, source_target_pairs={{0,8},{1,9},{2,10},{3,11},{4,12},{5,13},{6,14},{7,15},{8,0},{9,1},... | collective-permute-start | bytes 884744 | tf_op jit(solution)/shard_map/ppermute | solution.py:324
  171.1 0.0 copy-done.5
  171.1 0.0 copy-done.6
  171.1 0.0 copy-done.7
  171.1 1.3 combine.1
  172.4 5.3 %collective-permute-done.arrived_ref = bf16[128,1152]{1,0:T(8,128)(2,1)S(1)} collective-permute-done((bf16[128,1152]{1,0:T(8,128)(2,1)S(1)}, bf16[128,1152]{1,0:T(8,128)(2,1)S(1)}, u32[]{:S(2)}, u32[]{:S(2)}) %collective-permute-start) | collective-permute-done | bytes 294944 | tf_op jit(solution)/shard_map/ppermute | solution.py:324
  177.7 0.8 split_grads.1
Async XLA Ops:
  9.5 1.3 copy-start
  10.8 71.2 %all-to-all-start = ((bf16[64,8,2048]{2,1,0:T(8,128)(2,1)}), bf16[64,8,2048]{2,1,0:T(8,128)(2,1)S(1)}, u32[]{:S(2)}, u32[]{:S(2)}) async-start(bf16[64,8,2048]{2,1,0:T(8,128)(2,1)} %bitcast.16), calls=%async_computation | async-start | bytes 4194304 | tf_op jit(solution)/shard_map/all_to_all | solution.py:306
  29.1 137.7 %reduce-scatter.2.cloned.1.call-start = ((), (), s32[]{:S(2)}) async-start(), calls=%async_computation.3 | async-start | bytes 5308416 | tf_op jit(solution)/shard_map/reduce_scatter | solution.py:313
  88.8 0.6 copy-start.3
  89.5 1.4 copy-start.1
  89.5 1.9 %copy-start.2 = (bf16[1,2048,384]{2,1,0:T(8,128)(2,1)S(1)}, bf16[1,2048,384]{2,1,0:T(8,128)(2,1)}, u32[]{:S(2)}) copy-start(bf16[1,2048,384]{2,1,0:T(8,128)(2,1)} %param.14) | copy-start | bytes 4718596
  91.3 0.8 copy-start.4
  94.1 77.0 %copy-start.5 = (s32[128]{0:T(128)S(1)}, s32[128]{0:T(128)}, u32[]{:S(2)}) copy-start(s32[128]{0:T(128)} %param.11) | copy-start | bytes 1540
  94.1 77.0 %copy-start.6 = (s32[128]{0:T(128)S(1)}, s32[128]{0:T(128)}, u32[]{:S(2)}) copy-start(s32[128]{0:T(128)} %param.12) | copy-start | bytes 1540
  94.1 77.0 %copy-start.7 = (bf16[128]{0:T(256)(128)(2,1)S(1)}, bf16[128]{0:T(256)(128)(2,1)}, u32[]{:S(2)}) copy-start(bf16[128]{0:T(256)(128)(2,1)} %param.10) | copy-start | bytes 772
  167.9 9.8 %collective-permute-start = (bf16[128,1152]{1,0:T(8,128)(2,1)S(1)}, bf16[128,1152]{1,0:T(8,128)(2,1)S(1)}, u32[]{:S(2)}, u32[]{:S(2)}) collective-permute-start(bf16[128,1152]{1,0:T(8,128)(2,1)S(1)} %get-tuple-element.25), channel_id=1, source_target_pairs={{0,8},{1,9},{2,10},{3,11},{4,12},{5,13},{6,14},{7,15},{8,0},{9,1},... | collective-permute-start | bytes 884744 | tf_op jit(solution)/shard_map/ppermute | solution.py:324
Sparse Core Ops, SparseCore 0:
  89.6 77.1 reduce-scatter.1

commit v4 on v3

--- a/solution.py
+++ b/solution.py
@@ -32,8 +32,8 @@
 
 
 def dispatch_kernel(
-    capacity, ids_hbm, slot_hbm, score_hbm, tokens_hbm, cotan_hbm, out_ref,
-    ids_ref, slot_ref, score_ref, rows_ref, sems,
+    capacity, ids_hbm, slot_hbm, score_hbm, tokens_hbm, cotan_hbm, out_hbm,
+    ids_ref, slot_ref, score_ref, rows_ref, out_ref, sems, out_sems,
 ):
     rows, (count, features) = out_ref.shape[0], tokens_hbm.shape
     chunk = features // CHUNKS
@@ -57,10 +57,15 @@
     pick_token = jnp.where(row == position, F32(1), F32(0))
     pick_cotan = jnp.where(row == position + capacity, score_ref[...].astype(F32), F32(0))
     pick = jnp.concatenate([pick_token, pick_cotan], axis=1).astype(BF16)
+    writes = []
     for i, c in enumerate(columns):
         copies[3 + 2 * i].wait()
         copies[4 + 2 * i].wait()
         out_ref[:, c] = dot(pick, rows_ref[:, c], 1, 0).astype(BF16)
+        writes.append(pltpu.make_async_copy(out_ref.at[:, c], out_hbm.at[:, c], out_sems.at[i]))
+        writes[-1].start()
+    for write in writes:
+        write.wait()
 
 
 def dispatch(expert_ids, slot_index, gate_scores, tokens, cotangent, experts, capacity):
@@ -69,14 +74,16 @@
     return pl.pallas_call(
         functools.partial(dispatch_kernel, capacity),
         in_specs=[ANYWHERE] * 5,
-        out_specs=ON_CHIP,
-        out_shape=pltpu.VMEM((rows, features), BF16),
+        out_specs=ANYWHERE,
+        out_shape=pltpu.HBM((rows, features), BF16),
         scratch_shapes=[
             pltpu.VMEM((1, count), jnp.int32),
             pltpu.VMEM((1, count), jnp.int32),
             pltpu.VMEM((1, count), BF16),
             pltpu.VMEM((2 * count, features), BF16),
+            pltpu.VMEM((rows, features), BF16),
             pltpu.SemaphoreType.DMA((3 + 2 * CHUNKS,)),
+            pltpu.SemaphoreType.DMA((CHUNKS,)),
         ],
         compiler_params=pltpu.CompilerParams(vmem_limit_bytes=24 * 2**20),
         name="dispatch",
@@ -99,13 +106,15 @@
 
 
 def expert_kernel(
-    capacity, ring, side_ref, recv_ref, gate_hbm, up_hbm, down_hbm, grads_hbm, inner_ref, score_ref,
-    gate_ref, up_ref, down_ref, inputs, scaled, hidden_sc, grads_ref, sems, out_sems,
+    capacity, ring, place_ref, recv_ref, gate_hbm, up_hbm, down_hbm,
+    gate_ref, up_ref, inner_ref, score_ref, *rest,
 ):
+    grads, scratch = rest[: 2 * ring], rest[2 * ring :]
+    down_ref, inputs, scaled, hidden_sc, stage, sems, out_sems = scratch
     rows, features = recv_ref.shape
     slots = rows // 2
     hidden_size = gate_ref.shape[1]
-    side = side_ref[0]
+    side, spot = place_ref[0], place_ref[1]
     copies = [
         pltpu.make_async_copy(source, target, sems.at[i])
         for i, (source, target) in enumerate(
@@ -136,53 +145,52 @@
 
     block = features // (2 * ring)
     writes = []
-    for step in range(ring):
+    for ahead in sorted(range(ring), key=lambda k: -min(k, ring - k)):
         for piece in range(2):
             owner = side if piece else 1 - side
-            columns = pl.ds(pl.multiple_of((owner * ring + step) * block, block), block)
-            first = (2 * step + piece) * block
-            grads_ref[first : first + block, : 2 * hidden_size] = dot(
+            column = owner * ring + lax.rem(spot + ahead, ring)
+            columns = pl.ds(pl.multiple_of(column * block, block), block)
+            which = 2 * ahead + piece
+            stage[which, :, : 2 * hidden_size] = dot(
                 inputs[:, columns], inner_ref[...], 0, 0
             ).astype(BF16)
-            grads_ref[first : first + block, 2 * hidden_size :] = dot(
+            stage[which, :, 2 * hidden_size :] = dot(
                 scaled[:, columns], hidden_sc[...], 0, 0
             ).astype(BF16)
-        done = slice(2 * step * block, 2 * (step + 1) * block)
-        writes.append(
-            pltpu.make_async_copy(grads_ref.at[done], grads_hbm.at[done], out_sems.at[step])
-        )
-        writes[-1].start()
+            writes.append(pltpu.make_async_copy(stage.at[which], grads[which], out_sems.at[which]))
+            writes[-1].start()
     for write in writes:
         write.wait()
 
 
-def expert_grads(side, ring, received, gate, up, down, capacity):
+def expert_grads(place, ring, received, gate, up, down, capacity):
     rows, features = received.shape
     hidden_size = gate.shape[1]
     slots = rows // 2
+    block = (features // (2 * ring), 3 * hidden_size)
     return pl.pallas_call(
         functools.partial(expert_kernel, capacity, ring),
         in_specs=[pl.BlockSpec(memory_space=pltpu.SMEM), ON_CHIP, ANYWHERE, ANYWHERE, ANYWHERE],
-        out_specs=[ANYWHERE, ON_CHIP, ON_CHIP],
+        out_specs=[ON_CHIP] * 4 + [ANYWHERE] * (2 * ring),
         out_shape=[
-            pltpu.HBM((features, 3 * hidden_size), BF16),
+            pltpu.VMEM(gate.shape, BF16),
+            pltpu.VMEM(up.shape, BF16),
             pltpu.VMEM((slots, 2 * hidden_size), BF16),
             pltpu.VMEM((slots, LANES), BF16),
-        ],
+        ]
+        + [pltpu.HBM(block, BF16)] * (2 * ring),
         scratch_shapes=[
-            pltpu.VMEM(gate.shape, BF16),
-            pltpu.VMEM(up.shape, BF16),
             pltpu.VMEM(down.shape, BF16),
             pltpu.VMEM((slots, features), BF16),
             pltpu.VMEM((slots, features), BF16),
             pltpu.VMEM((slots, hidden_size), BF16),
-            pltpu.VMEM((features, 3 * hidden_size), BF16),
+            pltpu.VMEM((2 * ring, *block), BF16),
             pltpu.SemaphoreType.DMA((3,)),
-            pltpu.SemaphoreType.DMA((ring,)),
+            pltpu.SemaphoreType.DMA((2 * ring,)),
         ],
-        compiler_params=pltpu.CompilerParams(vmem_limit_bytes=40 * 2**20),
+        compiler_params=pltpu.CompilerParams(vmem_limit_bytes=28 * 2**20),
         name="expert_grads",
-    )(side, *on_chip(received), *in_hbm(gate, up, down))
+    )(place, *on_chip(received), *in_hbm(gate, up, down))
 
 
 def return_kernel(capacity, inner_ref, score_ref, gate_ref, up_ref, out_ref):
@@ -209,9 +217,9 @@
     return pl.pallas_call(
         functools.partial(return_kernel, capacity),
         out_shape=jax.ShapeDtypeStruct((2 * slots, half + LANES), BF16),
-        compiler_params=pltpu.CompilerParams(vmem_limit_bytes=40 * 2**20),
+        compiler_params=pltpu.CompilerParams(vmem_limit_bytes=24 * 2**20),
         name="return_rows",
-    )(*on_chip(inner, score), gate, up)
+    )(*on_chip(inner, score, gate, up))
 
 
 def combine_kernel(capacity, ids_ref, slot_ref, score_ref, rows_ref, token_ref, grad_ref):
@@ -241,58 +249,77 @@
         compiler_params=pltpu.CompilerParams(vmem_limit_bytes=24 * 2**20),
         name="combine",
     )(
-        expert_ids.reshape(1, count),
-        slot_index.reshape(1, count),
-        gate_scores.reshape(1, count),
-        rows,
-    )
-
-
-def halves_kernel(summed_hbm, sent_ref, kept_ref, sems):
-    block = sent_ref.shape[0]
-    copies = [
-        pltpu.make_async_copy(summed_hbm.at[:block], sent_ref, sems.at[0]),
-        pltpu.make_async_copy(summed_hbm.at[block:], kept_ref, sems.at[1]),
-    ]
-    for copy in copies:
-        copy.start()
-    for copy in copies:
-        copy.wait()
-
-
-def halves(summed):
-    half = (summed.shape[0] // 2, summed.shape[1])
-    return pl.pallas_call(
-        halves_kernel,
-        in_specs=[ANYWHERE],
-        out_specs=[ON_CHIP, ON_CHIP],
-        out_shape=[pltpu.VMEM(half, BF16), pltpu.VMEM(half, BF16)],
-        scratch_shapes=[pltpu.SemaphoreType.DMA((2,))],
-        name="halves",
-    )(*in_hbm(summed))
-
-
-def split_kernel(kept_ref, arrived_ref, gate_ref, up_ref, down_ref):
+        *in_hbm(
+            expert_ids.reshape(1, count),
+            slot_index.reshape(1, count),
+            gate_scores.reshape(1, count),
+        ),
+        *on_chip(rows),
+    )
+
+
+def add_kernel(*refs):
+    total = refs[0][...].astype(F32)
+    for ref in refs[1:-1]:
+        total += ref[...].astype(F32)
+    refs[-1][...] = total.astype(BF16)
+
+
+def add(*arrays):
+    return pl.pallas_call(
+        add_kernel,
+        in_specs=[ON_CHIP] * len(arrays),
+        out_specs=ON_CHIP,
+        out_shape=pltpu.VMEM(arrays[0].shape, BF16),
+        compiler_params=pltpu.CompilerParams(vmem_limit_bytes=6 * 2**20),
+        name="add",
+    )(*on_chip(*arrays))
+
+
+def split_kernel(own_ref, up_way_ref, down_way_ref, other_ref, gate_ref, up_ref, down_ref):
     hidden_size = gate_ref.shape[1]
-    total = kept_ref[...].astype(F32) + arrived_ref[...].astype(F32)
+    total = own_ref[...].astype(F32) + up_way_ref[...].astype(F32)
+    total += down_way_ref[...].astype(F32) + other_ref[...].astype(F32)
     gate_ref[...] = total[:, :hidden_size].astype(BF16)
     up_ref[...] = total[:, hidden_size : 2 * hidden_size].astype(BF16)
     down_ref[...] = total[:, 2 * hidden_size :].T.astype(BF16)
 
 
-def split_grads(kept, arrived):
-    block, width = arrived.shape
+def split_grads(*parts):
+    block, width = parts[0].shape
     hidden_size = width // 3
     return pl.pallas_call(
         split_kernel,
-        in_specs=[ON_CHIP, ON_CHIP],
+        in_specs=[ON_CHIP] * 4,
         out_shape=[
             jax.ShapeDtypeStruct((block, hidden_size), BF16),
             jax.ShapeDtypeStruct((block, hidden_size), BF16),
             jax.ShapeDtypeStruct((hidden_size, block), BF16),
         ],
         name="split_grads",
-    )(*on_chip(kept, arrived))
+    )(*on_chip(*parts))
+
+
+def ring_sums(grads, ring):
+    far = ring // 2
+    moves = {
+        way: [(s * ring + i, s * ring + (i + way) % ring) for s in range(2) for i in range(ring)]
+        for way in (1, -1)
+    }
+    block = lambda ahead, piece: grads[2 * (ahead % ring) + piece]
+    carried = {}
+    for hop in range(far, 0, -1):
+        for piece in range(2):
+            for way in (1, -1):
+                if hop == far and piece != (0 if way == 1 else 1):
+                    continue
+                own = block(way * hop, piece)
+                if (way, piece) in carried:
+                    own = add(own, carried[way, piece])
+                carried[way, piece] = lax.ppermute(own, "dp", moves[way])
+    return [
+        (block(0, piece), carried[1, piece], carried[-1, piece]) for piece in range(2)
+    ]
 
 
 def on_device(
@@ -308,24 +335,23 @@
         "expert", split_axis=0, concat_axis=0, tiled=True,
     ).reshape(send.shape)
     ring = lax.axis_size("dp") // 2
-    side = (lax.axis_index("dp") >= ring).astype(jnp.int32).reshape(1)
-    grads, inner, score = expert_grads(side, ring, received, gate, up, down, capacity)
-    summed = lax.psum_scatter(
-        grads, "dp", scatter_dimension=0, tiled=True,
-        axis_index_groups=[[s * ring + i for i in range(ring)] for s in range(2)],
-    )
+    index = lax.axis_index("dp")
+    side = (index >= ring).astype(jnp.int32)
+    place = jnp.stack([side, index - side * ring])
+    gate, up, inner, score, *grads = expert_grads(place, ring, received, gate, up, down, capacity)
     back = return_rows(inner, score, gate, up, capacity)
     returned = lax.all_to_all(
         back.reshape(experts, 2 * capacity, back.shape[1]),
         "expert", split_axis=0, concat_axis=0, tiled=True,
     ).reshape(back.shape)
-    summed, returned = lax.optimization_barrier((summed, returned))
-    sent, kept = halves(summed)
-    arrived = lax.ppermute(sent, "dp", [(i, (i + ring) % (2 * ring)) for i in range(2 * ring)])
+    for_other, kept = ring_sums(grads, ring)
+    other = lax.ppermute(
+        add(*for_other), "dp", [(i, (i + ring) % (2 * ring)) for i in range(2 * ring)]
+    )
     token_grad, score_grad = combine(
         expert_ids, slot_index, gate_scores, returned, features, capacity
     )
-    grad_gate, grad_up, grad_down = split_grads(kept, arrived)
+    grad_gate, grad_up, grad_down = split_grads(*kept, other)
     return token_grad, score_grad.reshape(count), grad_gate[None], grad_up[None], grad_down[None]
 
 

time: 186 us -> 172 us (0.925)
  the two profiles are of different devices: /device:TPU:1 before, /device:TPU:2 now
where the time goes in v4:
time: 172 us; the launch traced here: 171 us
  starting transfers between devices  89.8 us (52%)
  waiting for transfers between devices  63.1 us (37%)
  Pallas kernels  16.7 us (10%)
    ppermute x14, starting transfers between devices, ring_sums(): carried[way, piece] = lax.ppermute(own, 'dp', moves[way])  59.7 us
    all_to_all x1, waiting for transfers between devices, on_device(): lax.all_to_all(send.reshape(experts, 2 * capacity, features), 'expert', s...  50.5 us
    all_to_all x1, starting transfers between devices, on_device(): lax.all_to_all(send.reshape(experts, 2 * capacity, features), 'expert', s...  17.3 us
    all_to_all x1, starting transfers between devices, on_device(): lax.all_to_all(back.reshape(experts, 2 * capacity, back.shape[1]), 'exper...  10.9 us
    ppermute x14, waiting for transfers between devices, ring_sums(): carried[way, piece] = lax.ppermute(own, 'dp', moves[way])  6.97 us
    pallas_call x1, Pallas kernels, expert_grads(): pl.pallas_call(functools.partial(expert_kernel, capacity, ring), in_specs...  6.93 us
    ppermute x1, waiting for transfers between devices, on_device(): lax.ppermute(add(*for_other), 'dp', [(i, (i + ring) % (2 * ring)) for i i...  5.57 us
  transfers between devices with their start and end apart: 17, of which 5 were waited for; matrix products, arithmetic and copies ran while one was open for 0% of the time, Pallas kernels for 1%

profile of v4, /device:TPU:2, one launch (start us, length us, event | category | flops | bytes accessed | tf_op | source)
XLA Modules:
  0.0 170.9 jit_solution(16278961459802919115)
XLA Ops:
  0.6 3.2 %dispatch.1 = bf16[512,2048]{1,0:T(8,128)(2,1)} custom-call(s32[1,128]{1,0:T(1,128)} %bitcast.22, s32[1,128]{1,0:T(1,128)} %bitcast.24, bf16[1,128]{1,0:T(2,128)(2,1)} %bitcast.26, bf16[128,2048]{1,0:T(8,128)(2,1)} %tokens_hbm.1, bf16[128,2048]{1,0:T(8,128)(2,1)} %cotan_hbm.1), custom_call_target="tpu_custom_call" | custom-call | tf_op jit(solution)/shard_map/dispatch/pallas_call | solution.py:74
  3.8 17.3 %all-to-all-start = ((bf16[64,8,2048]{2,1,0:T(8,128)(2,1)}), bf16[64,8,2048]{2,1,0:T(8,128)(2,1)S(1)}, u32[]{:S(2)}, u32[]{:S(2)}) async-start(bf16[64,8,2048]{2,1,0:T(8,128)(2,1)} %bitcast.18), calls=%async_computation | async-start | bytes 4194304 | tf_op jit(solution)/shard_map/all_to_all | solution.py:333
  21.2 0.1 pad_add_fusion.place_ref
  21.3 50.5 %all-to-all-done = bf16[64,8,2048]{2,1,0:T(8,128)(2,1)S(1)} async-done(((bf16[64,8,2048]{2,1,0:T(8,128)(2,1)}), bf16[64,8,2048]{2,1,0:T(8,128)(2,1)S(1)}, u32[]{:S(2)}, u32[]{:S(2)}) %all-to-all-start) | async-done | bytes 2097184 | tf_op jit(solution)/shard_map/all_to_all | solution.py:333
  71.8 6.9 %expert_grads.1 = (bf16[2048,384]{1,0:T(8,128)(2,1)S(1)}, bf16[2048,384]{1,0:T(8,128)(2,1)S(1)}, bf16[256,768]{1,0:T(8,128)(2,1)S(1)}, bf16[256,128]{1,0:T(8,128...) custom-call(s32[2]{0:T(128)S(1)} %pad_add_fusion.place_ref, ...), custom_call_target="tpu_custom_call" | custom-call | tf_op jit(solution)/shard_map/expert_grads/pallas_call | solution.py:171
  78.7 2.9 %return_rows.1 = bf16[512,1152]{1,0:T(8,128)(2,1)} custom-call(bf16[256,768]{1,0:T(8,128)(2,1)S(1)} %get-tuple-element.30.inner_ref, bf16[256,128]{1,0:T(8,128)(2,1)S(1)} %get-tuple-element.31.score_ref, bf16[2048,384]{1,0:T(8,128)(2,1)S(1)} %get-tuple-element.32.gate_ref, bf16[2048,384]{1,0:T(8,128)(2,1)S(1)} %get-tuple-element.33.up_ref), custom_call_target="tpu_custom_call" | custom-call | tf_op jit(solution)/shard_map/return_rows/pallas_call | solution.py:217
  81.7 10.9 %all-to-all-start.1 = ((bf16[64,8,1152]{2,1,0:T(8,128)(2,1)}), bf16[64,8,1152]{2,1,0:T(8,128)(2,1)S(1)}, u32[]{:S(2)}, u32[]{:S(2)}) async-start(bf16[64,8,1152]{2,1,0:T(8,128)(2,1)} %bitcast.10), calls=%async_computation.1 | async-start | bytes 2359296 | tf_op jit(solution)/shard_map/all_to_all | solution.py:343
  92.6 3.6 %collective-permute-start.7 = (bf16[128,1152]{1,0:T(8,128)(2,1)S(1)}, bf16[128,1152]{1,0:T(8,128)(2,1)S(1)}, u32[]{:S(2)}, u32[]{:S(2)}) collective-permute-start(bf16[128,1152]{1,0:T(8,128)(2,1)S(1)} %copy-done.15), channel_id=1, source_target_pairs={{0,1},{1,2},{2,3},{3,4},{4,5},{5,6},{6,7},{7,0},{8,9},{9,10},{10,1... | collective-permute-start | bytes 884744 | tf_op jit(solution)/shard_map/ppermute | solution.py:319
  96.2 14.1 %collective-permute-start.3 = (bf16[128,1152]{1,0:T(8,128)(2,1)S(1)}, bf16[128,1152]{1,0:T(8,128)(2,1)S(1)}, u32[]{:S(2)}, u32[]{:S(2)}) collective-permute-start(bf16[128,1152]{1,0:T(8,128)(2,1)S(1)} %copy-done.14), channel_id=1, source_target_pairs={{0,7},{1,0},{2,1},{3,2},{4,3},{5,4},{6,5},{7,6},{8,15},{9,8},{10,9... | collective-permute-start | bytes 884744 | tf_op jit(solution)/shard_map/ppermute | solution.py:319
  110.3 6.9 %collective-permute-start.11 = (bf16[128,1152]{1,0:T(8,128)(2,1)S(1)}, bf16[128,1152]{1,0:T(8,128)(2,1)S(1)}, u32[]{:S(2)}, u32[]{:S(2)}) collective-permute-start(bf16[128,1152]{1,0:T(8,128)(2,1)S(1)} %copy-done.13), channel_id=1, source_target_pairs={{0,7},{1,0},{2,1},{3,2},{4,3},{5,4},{6,5},{7,6},{8,15},{9,8},{10,9... | collective-permute-start | bytes 884744 | tf_op jit(solution)/shard_map/ppermute | solution.py:319
  117.2 0.0 collective-permute-done.7.refs_1_
  117.3 0.1 add.18
  117.3 1.9 %collective-permute-start.8 = (bf16[128,1152]{1,0:T(8,128)(2,1)S(1)}, bf16[128,1152]{1,0:T(8,128)(2,1)S(1)}, u32[]{:S(2)}, u32[]{:S(2)}) collective-permute-start(bf16[128,1152]{1,0:T(8,128)(2,1)S(1)} %add.18), channel_id=1, source_target_pairs={{0,1},{1,2},{2,3},{3,4},{4,5},{5,6},{6,7},{7,0},{8,9},{9,10},{10,1... | collective-permute-start | bytes 884744 | tf_op jit(solution)/shard_map/ppermute | solution.py:319
  119.3 1.9 %collective-permute-start = (bf16[128,1152]{1,0:T(8,128)(2,1)S(1)}, bf16[128,1152]{1,0:T(8,128)(2,1)S(1)}, u32[]{:S(2)}, u32[]{:S(2)}) collective-permute-start(bf16[128,1152]{1,0:T(8,128)(2,1)S(1)} %copy-done.12), channel_id=1, source_target_pairs={{0,1},{1,2},{2,3},{3,4},{4,5},{5,6},{6,7},{7,0},{8,9},{9,10},{10,1... | collective-permute-start | bytes 884744 | tf_op jit(solution)/shard_map/ppermute | solution.py:319
  121.2 0.0 collective-permute-done.3.refs_1_
  121.2 0.1 add.15
  121.3 5.3 %collective-permute-start.4 = (bf16[128,1152]{1,0:T(8,128)(2,1)S(1)}, bf16[128,1152]{1,0:T(8,128)(2,1)S(1)}, u32[]{:S(2)}, u32[]{:S(2)}) collective-permute-start(bf16[128,1152]{1,0:T(8,128)(2,1)S(1)} %add.15), channel_id=1, source_target_pairs={{0,7},{1,0},{2,1},{3,2},{4,3},{5,4},{6,5},{7,6},{8,15},{9,8},{10,9... | collective-permute-start | bytes 884744 | tf_op jit(solution)/shard_map/ppermute | solution.py:319
  126.7 0.1 add.21
  126.8 3.9 %collective-permute-start.12 = (bf16[128,1152]{1,0:T(8,128)(2,1)S(1)}, bf16[128,1152]{1,0:T(8,128)(2,1)S(1)}, u32[]{:S(2)}, u32[]{:S(2)}) collective-permute-start(bf16[128,1152]{1,0:T(8,128)(2,1)S(1)} %add.21), channel_id=1, source_target_pairs={{0,7},{1,0},{2,1},{3,2},{4,3},{5,4},{6,5},{7,6},{8,15},{9,8},{10,9... | collective-permute-start | bytes 884744 | tf_op jit(solution)/shard_map/ppermute | solution.py:319
  130.7 0.0 collective-permute-done.8.refs_1_
  130.7 0.1 add.19
  130.8 1.9 %collective-permute-start.9 = (bf16[128,1152]{1,0:T(8,128)(2,1)S(1)}, bf16[128,1152]{1,0:T(8,128)(2,1)S(1)}, u32[]{:S(2)}, u32[]{:S(2)}) collective-permute-start(bf16[128,1152]{1,0:T(8,128)(2,1)S(1)} %add.19), channel_id=1, source_target_pairs={{0,1},{1,2},{2,3},{3,4},{4,5},{5,6},{6,7},{7,0},{8,9},{9,10},{10,1... | collective-permute-start | bytes 884744 | tf_op jit(solution)/shard_map/ppermute | solution.py:319
  132.7 3.5 %collective-permute-done.refs_1_ = bf16[128,1152]{1,0:T(8,128)(2,1)S(1)} collective-permute-done((bf16[128,1152]{1,0:T(8,128)(2,1)S(1)}, bf16[128,1152]{1,0:T(8,128)(2,1)S(1)}, u32[]{:S(2)}, u32[]{:S(2)}) %collective-permute-start) | collective-permute-done | bytes 294944 | tf_op jit(solution)/shard_map/ppermute | solution.py:319
  136.2 0.1 add.13
  136.3 1.9 %collective-permute-start.1 = (bf16[128,1152]{1,0:T(8,128)(2,1)S(1)}, bf16[128,1152]{1,0:T(8,128)(2,1)S(1)}, u32[]{:S(2)}, u32[]{:S(2)}) collective-permute-start(bf16[128,1152]{1,0:T(8,128)(2,1)S(1)} %add.13), channel_id=1, source_target_pairs={{0,1},{1,2},{2,3},{3,4},{4,5},{5,6},{6,7},{7,0},{8,9},{9,10},{10,1... | collective-permute-start | bytes 884744 | tf_op jit(solution)/shard_map/ppermute | solution.py:319
  138.2 0.1 add.16
  138.3 5.1 %collective-permute-start.5 = (bf16[128,1152]{1,0:T(8,128)(2,1)S(1)}, bf16[128,1152]{1,0:T(8,128)(2,1)S(1)}, u32[]{:S(2)}, u32[]{:S(2)}) collective-permute-start(bf16[128,1152]{1,0:T(8,128)(2,1)S(1)} %add.16), channel_id=1, source_target_pairs={{0,7},{1,0},{2,1},{3,2},{4,3},{5,4},{6,5},{7,6},{8,15},{9,8},{10,9... | collective-permute-start | bytes 884744 | tf_op jit(solution)/shard_map/ppermute | solution.py:319
  143.5 0.0 copy-start.11
  143.5 0.1 add.22
  143.6 3.2 %collective-permute-start.13 = (bf16[128,1152]{1,0:T(8,128)(2,1)S(1)}, bf16[128,1152]{1,0:T(8,128)(2,1)S(1)}, u32[]{:S(2)}, u32[]{:S(2)}) collective-permute-start(bf16[128,1152]{1,0:T(8,128)(2,1)S(1)} %add.22), channel_id=1, source_target_pairs={{0,7},{1,0},{2,1},{3,2},{4,3},{5,4},{6,5},{7,6},{8,15},{9,8},{10,9... | collective-permute-start | bytes 884744 | tf_op jit(solution)/shard_map/ppermute | solution.py:319
  146.7 0.0 collective-permute-done.9.refs_1_
  146.8 0.1 add.20
  146.9 2.8 %collective-permute-start.10 = (bf16[128,1152]{1,0:T(8,128)(2,1)S(1)}, bf16[128,1152]{1,0:T(8,128)(2,1)S(1)}, u32[]{:S(2)}, u32[]{:S(2)}) collective-permute-start(bf16[128,1152]{1,0:T(8,128)(2,1)S(1)} %add.20), channel_id=1, source_target_pairs={{0,1},{1,2},{2,3},{3,4},{4,5},{5,6},{6,7},{7,0},{8,9},{9,10},{10,1... | collective-permute-start | bytes 884744 | tf_op jit(solution)/shard_map/ppermute | solution.py:319
  149.7 0.0 collective-permute-done.1.refs_1_
  149.7 0.1 add.14
  149.8 1.9 %collective-permute-start.2 = (bf16[128,1152]{1,0:T(8,128)(2,1)S(1)}, bf16[128,1152]{1,0:T(8,128)(2,1)S(1)}, u32[]{:S(2)}, u32[]{:S(2)}) collective-permute-start(bf16[128,1152]{1,0:T(8,128)(2,1)S(1)} %add.14), channel_id=1, source_target_pairs={{0,1},{1,2},{2,3},{3,4},{4,5},{5,6},{6,7},{7,0},{8,9},{9,10},{10,1... | collective-permute-start | bytes 884744 | tf_op jit(solution)/shard_map/ppermute | solution.py:319
  151.7 0.0 collective-permute-done.5.refs_1_
  151.7 0.1 add.17
  151.8 5.1 %collective-permute-start.6 = (bf16[128,1152]{1,0:T(8,128)(2,1)S(1)}, bf16[128,1152]{1,0:T(8,128)(2,1)S(1)}, u32[]{:S(2)}, u32[]{:S(2)}) collective-permute-start(bf16[128,1152]{1,0:T(8,128)(2,1)S(1)} %add.17), channel_id=1, source_target_pairs={{0,7},{1,0},{2,1},{3,2},{4,3},{5,4},{6,5},{7,6},{8,15},{9,8},{10,9... | collective-permute-start | bytes 884744 | tf_op jit(solution)/shard_map/ppermute | solution.py:319
  156.9 0.0 collective-permute-done.13.refs_2_
  157.0 2.4 %collective-permute-done.10.refs_1_ = bf16[128,1152]{1,0:T(8,128)(2,1)S(1)} collective-permute-done((bf16[128,1152]{1,0:T(8,128)(2,1)S(1)}, bf16[128,1152]{1,0:T(8,128)(2,1)S(1)}, u32[]{:S(2)}, u32[]{:S(2)}) %collective-permute-start.10) | collective-permute-done | bytes 294944 | tf_op jit(solution)/shard_map/ppermute | solution.py:319
  159.3 0.1 add.23
  159.4 1.9 %collective-permute-start.14 = (bf16[128,1152]{1,0:T(8,128)(2,1)S(1)}, bf16[128,1152]{1,0:T(8,128)(2,1)S(1)}, u32[]{:S(2)}, u32[]{:S(2)}) collective-permute-start(bf16[128,1152]{1,0:T(8,128)(2,1)S(1)} %add.23), channel_id=1, source_target_pairs={{0,8},{1,9},{2,10},{3,11},{4,12},{5,13},{6,14},{7,15},{8,0},{9,1},... | collective-permute-start | bytes 884744 | tf_op jit(solution)/shard_map/ppermute | solution.py:348
  161.4 1.1 collective-permute-done.2.up_way_ref
  162.5 0.0 collective-permute-done.6.down_way_ref
  162.5 5.6 %collective-permute-done.14.other_ref = bf16[128,1152]{1,0:T(8,128)(2,1)S(1)} collective-permute-done((bf16[128,1152]{1,0:T(8,128)(2,1)S(1)}, bf16[128,1152]{1,0:T(8,128)(2,1)S(1)}, u32[]{:S(2)}, u32[]{:S(2)}) %collective-permute-start.14) | collective-permute-done | bytes 294944 | tf_op jit(solution)/shard_map/ppermute | solution.py:348
  168.0 0.8 split_grads.1
  168.9 2.0 %combine.1 = (bf16[128,2048]{1,0:T(8,128)(2,1)}, bf16[1,128]{1,0:T(2,128)(2,1)}) custom-call(s32[1,128]{1,0:T(1,128)} %bitcast.23, s32[1,128]{1,0:T(1,128)} %bitcast.25, bf16[1,128]{1,0:T(2,128)(2,1)} %bitcast.27, bf16[512,1152]{1,0:T(8,128)(2,1)S(1)} %bitcast.17), custom_call_target="tpu_custom_call" | custom-call | tf_op jit(solution)/shard_map/combine/pallas_call | solution.py:243
  (35 shorter events, 0.1 us)
Async XLA Ops:
  3.8 68.0 %all-to-all-start = ((bf16[64,8,2048]{2,1,0:T(8,128)(2,1)}), bf16[64,8,2048]{2,1,0:T(8,128)(2,1)S(1)}, u32[]{:S(2)}, u32[]{:S(2)}) async-start(bf16[64,8,2048]{2,1,0:T(8,128)(2,1)} %bitcast.18), calls=%async_computation | async-start | bytes 4194304 | tf_op jit(solution)/shard_map/all_to_all | solution.py:333
  81.6 10.9 %copy-start.15 = (bf16[128,1152]{1,0:T(8,128)(2,1)S(1)}, bf16[128,1152]{1,0:T(8,128)(2,1)}, u32[]{:S(2)}) copy-start(bf16[128,1152]{1,0:T(8,128)(2,1)} %get-tuple-element.48) | copy-start | bytes 884740
  81.6 14.6 %copy-start.14 = (bf16[128,1152]{1,0:T(8,128)(2,1)S(1)}, bf16[128,1152]{1,0:T(8,128)(2,1)}, u32[]{:S(2)}) copy-start(bf16[128,1152]{1,0:T(8,128)(2,1)} %get-tuple-element.43) | copy-start | bytes 884740
  81.7 28.6 %copy-start.13 = (bf16[128,1152]{1,0:T(8,128)(2,1)S(1)}, bf16[128,1152]{1,0:T(8,128)(2,1)}, u32[]{:S(2)}) copy-start(bf16[128,1152]{1,0:T(8,128)(2,1)} %get-tuple-element.51) | copy-start | bytes 884740
  81.7 35.6 %copy-start.9 = (bf16[128,1152]{1,0:T(8,128)(2,1)S(1)}, bf16[128,1152]{1,0:T(8,128)(2,1)}, u32[]{:S(2)}) copy-start(bf16[128,1152]{1,0:T(8,128)(2,1)} %get-tuple-element.47.refs_0_) | copy-start | bytes 884740
  81.7 37.6 %copy-start.12 = (bf16[128,1152]{1,0:T(8,128)(2,1)S(1)}, bf16[128,1152]{1,0:T(8,128)(2,1)}, u32[]{:S(2)}) copy-start(bf16[128,1152]{1,0:T(8,128)(2,1)} %get-tuple-element.39) | copy-start | bytes 884740
  81.7 39.6 %copy-start.8 = (bf16[128,1152]{1,0:T(8,128)(2,1)S(1)}, bf16[128,1152]{1,0:T(8,128)(2,1)}, u32[]{:S(2)}) copy-start(bf16[128,1152]{1,0:T(8,128)(2,1)} %get-tuple-element.42.refs_0_) | copy-start | bytes 884740
  81.7 45.0 %copy-start.7 = (bf16[128,1152]{1,0:T(8,128)(2,1)S(1)}, bf16[128,1152]{1,0:T(8,128)(2,1)}, u32[]{:S(2)}) copy-start(bf16[128,1152]{1,0:T(8,128)(2,1)} %get-tuple-element.50.refs_0_) | copy-start | bytes 884740
  81.7 87.2 %all-to-all-start.1 = ((bf16[64,8,1152]{2,1,0:T(8,128)(2,1)}), bf16[64,8,1152]{2,1,0:T(8,128)(2,1)S(1)}, u32[]{:S(2)}, u32[]{:S(2)}) async-start(bf16[64,8,1152]{2,1,0:T(8,128)(2,1)} %bitcast.10), calls=%async_computation.1 | async-start | bytes 2359296 | tf_op jit(solution)/shard_map/all_to_all | solution.py:343
  92.5 38.1 %copy-start.6 = (bf16[128,1152]{1,0:T(8,128)(2,1)S(1)}, bf16[128,1152]{1,0:T(8,128)(2,1)}, u32[]{:S(2)}) copy-start(bf16[128,1152]{1,0:T(8,128)(2,1)} %get-tuple-element.46.refs_0_) | copy-start | bytes 884740
  92.6 24.7 %collective-permute-start.7 = (bf16[128,1152]{1,0:T(8,128)(2,1)S(1)}, bf16[128,1152]{1,0:T(8,128)(2,1)S(1)}, u32[]{:S(2)}, u32[]{:S(2)}) collective-permute-start(bf16[128,1152]{1,0:T(8,128)(2,1)S(1)} %copy-done.15), channel_id=1, source_target_pairs={{0,1},{1,2},{2,3},{3,4},{4,5},{5,6},{6,7},{7,0},{8,9},{9,10},{10,1... | collective-permute-start | bytes 884744 | tf_op jit(solution)/shard_map/ppermute | solution.py:319
  96.2 25.0 %collective-permute-start.3 = (bf16[128,1152]{1,0:T(8,128)(2,1)S(1)}, bf16[128,1152]{1,0:T(8,128)(2,1)S(1)}, u32[]{:S(2)}, u32[]{:S(2)}) collective-permute-start(bf16[128,1152]{1,0:T(8,128)(2,1)S(1)} %copy-done.14), channel_id=1, source_target_pairs={{0,7},{1,0},{2,1},{3,2},{4,3},{5,4},{6,5},{7,6},{8,15},{9,8},{10,9... | collective-permute-start | bytes 884744 | tf_op jit(solution)/shard_map/ppermute | solution.py:319
  110.3 16.4 %collective-permute-start.11 = (bf16[128,1152]{1,0:T(8,128)(2,1)S(1)}, bf16[128,1152]{1,0:T(8,128)(2,1)S(1)}, u32[]{:S(2)}, u32[]{:S(2)}) collective-permute-start(bf16[128,1152]{1,0:T(8,128)(2,1)S(1)} %copy-done.13), channel_id=1, source_target_pairs={{0,7},{1,0},{2,1},{3,2},{4,3},{5,4},{6,5},{7,6},{8,15},{9,8},{10,9... | collective-permute-start | bytes 884744 | tf_op jit(solution)/shard_map/ppermute | solution.py:319
  117.2 19.0 %copy-start.5 = (bf16[128,1152]{1,0:T(8,128)(2,1)S(1)}, bf16[128,1152]{1,0:T(8,128)(2,1)}, u32[]{:S(2)}) copy-start(bf16[128,1152]{1,0:T(8,128)(2,1)} %get-tuple-element.38.refs_0_) | copy-start | bytes 884740
  117.3 13.3 %collective-permute-start.8 = (bf16[128,1152]{1,0:T(8,128)(2,1)S(1)}, bf16[128,1152]{1,0:T(8,128)(2,1)S(1)}, u32[]{:S(2)}, u32[]{:S(2)}) collective-permute-start(bf16[128,1152]{1,0:T(8,128)(2,1)S(1)} %add.18), channel_id=1, source_target_pairs={{0,1},{1,2},{2,3},{3,4},{4,5},{5,6},{6,7},{7,0},{8,9},{9,10},{10,1... | collective-permute-start | bytes 884744 | tf_op jit(solution)/shard_map/ppermute | solution.py:319
  119.3 16.9 %collective-permute-start = (bf16[128,1152]{1,0:T(8,128)(2,1)S(1)}, bf16[128,1152]{1,0:T(8,128)(2,1)S(1)}, u32[]{:S(2)}, u32[]{:S(2)}) collective-permute-start(bf16[128,1152]{1,0:T(8,128)(2,1)S(1)} %copy-done.12), channel_id=1, source_target_pairs={{0,1},{1,2},{2,3},{3,4},{4,5},{5,6},{6,7},{7,0},{8,9},{9,10},{10,1... | collective-permute-start | bytes 884744 | tf_op jit(solution)/shard_map/ppermute | solution.py:319
  121.2 17.0 %copy-start.4 = (bf16[128,1152]{1,0:T(8,128)(2,1)S(1)}, bf16[128,1152]{1,0:T(8,128)(2,1)}, u32[]{:S(2)}) copy-start(bf16[128,1152]{1,0:T(8,128)(2,1)} %get-tuple-element.41.refs_0_) | copy-start | bytes 884740
  121.3 16.9 %collective-permute-start.4 = (bf16[128,1152]{1,0:T(8,128)(2,1)S(1)}, bf16[128,1152]{1,0:T(8,128)(2,1)S(1)}, u32[]{:S(2)}, u32[]{:S(2)}) collective-permute-start(bf16[128,1152]{1,0:T(8,128)(2,1)S(1)} %add.15), channel_id=1, source_target_pairs={{0,7},{1,0},{2,1},{3,2},{4,3},{5,4},{6,5},{7,6},{8,15},{9,8},{10,9... | collective-permute-start | bytes 884744 | tf_op jit(solution)/shard_map/ppermute | solution.py:319
  126.7 16.8 %copy-start.3 = (bf16[128,1152]{1,0:T(8,128)(2,1)S(1)}, bf16[128,1152]{1,0:T(8,128)(2,1)}, u32[]{:S(2)}) copy-start(bf16[128,1152]{1,0:T(8,128)(2,1)} %get-tuple-element.49.refs_0_) | copy-start | bytes 884740
  126.8 16.7 %collective-permute-start.12 = (bf16[128,1152]{1,0:T(8,128)(2,1)S(1)}, bf16[128,1152]{1,0:T(8,128)(2,1)S(1)}, u32[]{:S(2)}, u32[]{:S(2)}) collective-permute-start(bf16[128,1152]{1,0:T(8,128)(2,1)S(1)} %add.21), channel_id=1, source_target_pairs={{0,7},{1,0},{2,1},{3,2},{4,3},{5,4},{6,5},{7,6},{8,15},{9,8},{10,9... | collective-permute-start | bytes 884744 | tf_op jit(solution)/shard_map/ppermute | solution.py:319
  130.7 16.1 %copy-start.2 = (bf16[128,1152]{1,0:T(8,128)(2,1)S(1)}, bf16[128,1152]{1,0:T(8,128)(2,1)}, u32[]{:S(2)}) copy-start(bf16[128,1152]{1,0:T(8,128)(2,1)} %get-tuple-element.45.refs_0_) | copy-start | bytes 884740
  130.8 16.0 %collective-permute-start.9 = (bf16[128,1152]{1,0:T(8,128)(2,1)S(1)}, bf16[128,1152]{1,0:T(8,128)(2,1)S(1)}, u32[]{:S(2)}, u32[]{:S(2)}) collective-permute-start(bf16[128,1152]{1,0:T(8,128)(2,1)S(1)} %add.19), channel_id=1, source_target_pairs={{0,1},{1,2},{2,3},{3,4},{4,5},{5,6},{6,7},{7,0},{8,9},{9,10},{10,1... | collective-permute-start | bytes 884744 | tf_op jit(solution)/shard_map/ppermute | solution.py:319
  136.2 13.5 %copy-start.1 = (bf16[128,1152]{1,0:T(8,128)(2,1)S(1)}, bf16[128,1152]{1,0:T(8,128)(2,1)}, u32[]{:S(2)}) copy-start(bf16[128,1152]{1,0:T(8,128)(2,1)} %get-tuple-element.37.refs_0_) | copy-start | bytes 884740
  136.3 13.4 %collective-permute-start.1 = (bf16[128,1152]{1,0:T(8,128)(2,1)S(1)}, bf16[128,1152]{1,0:T(8,128)(2,1)S(1)}, u32[]{:S(2)}, u32[]{:S(2)}) collective-permute-start(bf16[128,1152]{1,0:T(8,128)(2,1)S(1)} %add.13), channel_id=1, source_target_pairs={{0,1},{1,2},{2,3},{3,4},{4,5},{5,6},{6,7},{7,0},{8,9},{9,10},{10,1... | collective-permute-start | bytes 884744 | tf_op jit(solution)/shard_map/ppermute | solution.py:319
  138.2 13.5 %copy-start = (bf16[128,1152]{1,0:T(8,128)(2,1)S(1)}, bf16[128,1152]{1,0:T(8,128)(2,1)}, u32[]{:S(2)}) copy-start(bf16[128,1152]{1,0:T(8,128)(2,1)} %get-tuple-element.40.refs_0_) | copy-start | bytes 884740
  138.3 13.4 %collective-permute-start.5 = (bf16[128,1152]{1,0:T(8,128)(2,1)S(1)}, bf16[128,1152]{1,0:T(8,128)(2,1)S(1)}, u32[]{:S(2)}, u32[]{:S(2)}) collective-permute-start(bf16[128,1152]{1,0:T(8,128)(2,1)S(1)} %add.16), channel_id=1, source_target_pairs={{0,7},{1,0},{2,1},{3,2},{4,3},{5,4},{6,5},{7,6},{8,15},{9,8},{10,9... | collective-permute-start | bytes 884744 | tf_op jit(solution)/shard_map/ppermute | solution.py:319
  143.5 15.8 %copy-start.11 = (bf16[128,1152]{1,0:T(8,128)(2,1)S(1)}, bf16[128,1152]{1,0:T(8,128)(2,1)}, u32[]{:S(2)}) copy-start(bf16[128,1152]{1,0:T(8,128)(2,1)} %get-tuple-element.44.refs_0_) | copy-start | bytes 884740
  143.6 13.4 %collective-permute-start.13 = (bf16[128,1152]{1,0:T(8,128)(2,1)S(1)}, bf16[128,1152]{1,0:T(8,128)(2,1)S(1)}, u32[]{:S(2)}, u32[]{:S(2)}) collective-permute-start(bf16[128,1152]{1,0:T(8,128)(2,1)S(1)} %add.22), channel_id=1, source_target_pairs={{0,7},{1,0},{2,1},{3,2},{4,3},{5,4},{6,5},{7,6},{8,15},{9,8},{10,9... | collective-permute-start | bytes 884744 | tf_op jit(solution)/shard_map/ppermute | solution.py:319
  146.8 21.2 %copy-start.10 = (bf16[128,1152]{1,0:T(8,128)(2,1)S(1)}, bf16[128,1152]{1,0:T(8,128)(2,1)}, u32[]{:S(2)}) copy-start(bf16[128,1152]{1,0:T(8,128)(2,1)} %get-tuple-element.36.own_ref) | copy-start | bytes 884740
  146.9 12.5 %collective-permute-start.10 = (bf16[128,1152]{1,0:T(8,128)(2,1)S(1)}, bf16[128,1152]{1,0:T(8,128)(2,1)S(1)}, u32[]{:S(2)}, u32[]{:S(2)}) collective-permute-start(bf16[128,1152]{1,0:T(8,128)(2,1)S(1)} %add.20), channel_id=1, source_target_pairs={{0,1},{1,2},{2,3},{3,4},{4,5},{5,6},{6,7},{7,0},{8,9},{9,10},{10,1... | collective-permute-start | bytes 884744 | tf_op jit(solution)/shard_map/ppermute | solution.py:319
  149.8 12.7 %collective-permute-start.2 = (bf16[128,1152]{1,0:T(8,128)(2,1)S(1)}, bf16[128,1152]{1,0:T(8,128)(2,1)S(1)}, u32[]{:S(2)}, u32[]{:S(2)}) collective-permute-start(bf16[128,1152]{1,0:T(8,128)(2,1)S(1)} %add.14), channel_id=1, source_target_pairs={{0,1},{1,2},{2,3},{3,4},{4,5},{5,6},{6,7},{7,0},{8,9},{9,10},{10,1... | collective-permute-start | bytes 884744 | tf_op jit(solution)/shard_map/ppermute | solution.py:319
  151.8 10.7 %collective-permute-start.6 = (bf16[128,1152]{1,0:T(8,128)(2,1)S(1)}, bf16[128,1152]{1,0:T(8,128)(2,1)S(1)}, u32[]{:S(2)}, u32[]{:S(2)}) collective-permute-start(bf16[128,1152]{1,0:T(8,128)(2,1)S(1)} %add.17), channel_id=1, source_target_pairs={{0,7},{1,0},{2,1},{3,2},{4,3},{5,4},{6,5},{7,6},{8,15},{9,8},{10,9... | collective-permute-start | bytes 884744 | tf_op jit(solution)/shard_map/ppermute | solution.py:319
  159.4 8.6 %collective-permute-start.14 = (bf16[128,1152]{1,0:T(8,128)(2,1)S(1)}, bf16[128,1152]{1,0:T(8,128)(2,1)S(1)}, u32[]{:S(2)}, u32[]{:S(2)}) collective-permute-start(bf16[128,1152]{1,0:T(8,128)(2,1)S(1)} %add.23), channel_id=1, source_target_pairs={{0,8},{1,9},{2,10},{3,11},{4,12},{5,13},{6,14},{7,15},{8,0},{9,1},... | collective-permute-start | bytes 884744 | tf_op jit(solution)/shard_map/ppermute | solution.py:348

commit v5 on v4

--- a/solution.py
+++ b/solution.py
@@ -105,16 +105,40 @@
     return jnp.where(row == wanted, F32(1), F32(0)).astype(BF16)
 
 
+def early_blocks(ring):
+    return [(ring // 2, 0), (2, 0), (ring - 2, 0)]
+
+
+def late_blocks(ring):
+    far = sorted(range(ring), key=lambda k: -min(k, ring - k))
+    return [(k, p) for k in far for p in range(2) if (k, p) not in early_blocks(ring)]
+
+
+def write_blocks(blocks, ring, place_ref, inputs, scaled, inner, hidden, stage, outs, sems):
+    side, spot = place_ref[0], place_ref[1]
+    block = inputs.shape[1] // (2 * ring)
+    hidden_size = hidden.shape[1]
+    writes = []
+    for i, (ahead, piece) in enumerate(blocks):
+        owner = side if piece else 1 - side
+        column = owner * ring + lax.rem(spot + ahead, ring)
+        columns = pl.ds(pl.multiple_of(column * block, block), block)
+        stage[i, :, : 2 * hidden_size] = dot(inputs[:, columns], inner[...], 0, 0).astype(BF16)
+        stage[i, :, 2 * hidden_size :] = dot(scaled[:, columns], hidden[...], 0, 0).astype(BF16)
+        writes.append(pltpu.make_async_copy(stage.at[i], outs[i], sems.at[i]))
+        writes[-1].start()
+    return writes
+
+
 def expert_kernel(
     capacity, ring, place_ref, recv_ref, gate_hbm, up_hbm, down_hbm,
-    gate_ref, up_ref, inner_ref, score_ref, *rest,
+    gate_ref, up_ref, inner_ref, score_ref, inputs, scaled, hidden_ref, *rest,
 ):
-    grads, scratch = rest[: 2 * ring], rest[2 * ring :]
-    down_ref, inputs, scaled, hidden_sc, stage, sems, out_sems = scratch
+    blocks = early_blocks(ring)
+    grads, (down_ref, stage, sems, out_sems) = rest[: len(blocks)], rest[len(blocks) :]
     rows, features = recv_ref.shape
     slots = rows // 2
     hidden_size = gate_ref.shape[1]
-    side, spot = place_ref[0], place_ref[1]
     copies = [
         pltpu.make_async_copy(source, target, sems.at[i])
         for i, (source, target) in enumerate(
@@ -135,69 +159,63 @@
     sigmoid = jax.nn.sigmoid(pre_gate)
     activated = pre_gate * sigmoid
     hidden = (activated * pre_up).astype(BF16)
-    hidden_sc[...] = hidden
+    hidden_ref[...] = hidden
     inner_ref[:, :hidden_size] = (
         hidden_grad * pre_up * sigmoid * (1.0 + pre_gate * (1.0 - sigmoid))
     ).astype(BF16)
     inner_ref[:, hidden_size:] = (hidden_grad * activated).astype(BF16)
     score = jnp.sum(hidden.astype(F32) * hidden_grad, axis=1, keepdims=True)
     score_ref[...] = jnp.broadcast_to(score, score_ref.shape).astype(BF16)
-
-    block = features // (2 * ring)
-    writes = []
-    for ahead in sorted(range(ring), key=lambda k: -min(k, ring - k)):
-        for piece in range(2):
-            owner = side if piece else 1 - side
-            column = owner * ring + lax.rem(spot + ahead, ring)
-            columns = pl.ds(pl.multiple_of(column * block, block), block)
-            which = 2 * ahead + piece
-            stage[which, :, : 2 * hidden_size] = dot(
-                inputs[:, columns], inner_ref[...], 0, 0
-            ).astype(BF16)
-            stage[which, :, 2 * hidden_size :] = dot(
-                scaled[:, columns], hidden_sc[...], 0, 0
-            ).astype(BF16)
-            writes.append(pltpu.make_async_copy(stage.at[which], grads[which], out_sems.at[which]))
-            writes[-1].start()
-    for write in writes:
+    for write in write_blocks(
+        blocks, ring, place_ref, inputs, scaled, inner_ref, hidden_ref, stage, grads, out_sems
+    ):
         write.wait()
 
 
-def expert_grads(place, ring, received, gate, up, down, capacity):
+def expert_first(place, ring, received, gate, up, down, capacity):
     rows, features = received.shape
     hidden_size = gate.shape[1]
     slots = rows // 2
     block = (features // (2 * ring), 3 * hidden_size)
+    count = len(early_blocks(ring))
     return pl.pallas_call(
         functools.partial(expert_kernel, capacity, ring),
         in_specs=[pl.BlockSpec(memory_space=pltpu.SMEM), ON_CHIP, ANYWHERE, ANYWHERE, ANYWHERE],
-        out_specs=[ON_CHIP] * 4 + [ANYWHERE] * (2 * ring),
+        out_specs=[ON_CHIP] * 7 + [ANYWHERE] * count,
         out_shape=[
             pltpu.VMEM(gate.shape, BF16),
             pltpu.VMEM(up.shape, BF16),
             pltpu.VMEM((slots, 2 * hidden_size), BF16),
             pltpu.VMEM((slots, LANES), BF16),
-        ]
-        + [pltpu.HBM(block, BF16)] * (2 * ring),
-        scratch_shapes=[
-            pltpu.VMEM(down.shape, BF16),
             pltpu.VMEM((slots, features), BF16),
             pltpu.VMEM((slots, features), BF16),
             pltpu.VMEM((slots, hidden_size), BF16),
-            pltpu.VMEM((2 * ring, *block), BF16),
+        ]
+        + [pltpu.HBM(block, BF16)] * count,
+        scratch_shapes=[
+            pltpu.VMEM(down.shape, BF16),
+            pltpu.VMEM((count, *block), BF16),
             pltpu.SemaphoreType.DMA((3,)),
-            pltpu.SemaphoreType.DMA((2 * ring,)),
+            pltpu.SemaphoreType.DMA((count,)),
         ],
-        compiler_params=pltpu.CompilerParams(vmem_limit_bytes=28 * 2**20),
-        name="expert_grads",
+        compiler_params=pltpu.CompilerParams(vmem_limit_bytes=24 * 2**20),
+        name="expert_first",
     )(place, *on_chip(received), *in_hbm(gate, up, down))
 
 
-def return_kernel(capacity, inner_ref, score_ref, gate_ref, up_ref, out_ref):
+def late_kernel(
+    capacity, ring, place_ref, gate_ref, up_ref, inner_ref, score_ref, inputs, scaled, hidden_ref,
+    back_hbm, *rest,
+):
+    blocks = late_blocks(ring)
+    grads, (stage, back, out_sems) = rest[: len(blocks)], rest[len(blocks) :]
     slots = inner_ref.shape[0]
-    rows = out_ref.shape[0]
+    rows = back.shape[0]
     hidden_size = gate_ref.shape[1]
     half = gate_ref.shape[0] // 2
+    writes = write_blocks(
+        blocks, ring, place_ref, inputs, scaled, inner_ref, hidden_ref, stage, grads, out_sems
+    )
     total = jnp.zeros((rows, half), F32)
     for part in range(2):
         piece = pl.ds(part * half, half)
@@ -207,19 +225,36 @@
         spread = pick_rows(slots, rows, capacity, part)
         total += dot(spread, input_grad.astype(BF16), 0, 0)
         if part == 0:
-            out_ref[:, half:] = dot(spread, score_ref[...], 0, 0).astype(BF16)
-    out_ref[:, :half] = total.astype(BF16)
-
-
-def return_rows(inner, score, gate, up, capacity):
-    slots = inner.shape[0]
-    half = gate.shape[0] // 2
-    return pl.pallas_call(
-        functools.partial(return_kernel, capacity),
-        out_shape=jax.ShapeDtypeStruct((2 * slots, half + LANES), BF16),
+            back[:, half:] = dot(spread, score_ref[...], 0, 0).astype(BF16)
+    back[:, :half] = total.astype(BF16)
+    writes.append(pltpu.make_async_copy(back, back_hbm, out_sems.at[len(blocks)]))
+    writes[-1].start()
+    for write in writes:
+        write.wait()
+
+
+def expert_late(place, ring, gate, up, inner, score, inputs, scaled, hidden, capacity):
+    slots, features = inputs.shape
+    hidden_size = gate.shape[1]
+    block = (features // (2 * ring), 3 * hidden_size)
+    count = len(late_blocks(ring))
+    back = (2 * slots, features // 2 + LANES)
+    return pl.pallas_call(
+        functools.partial(late_kernel, capacity, ring),
+        in_specs=[pl.BlockSpec(memory_space=pltpu.SMEM)] + [ON_CHIP] * 7,
+        out_specs=[ANYWHERE] * (1 + count),
+        out_shape=[pltpu.HBM(back, BF16)] + [pltpu.HBM(block, BF16)] * count,
+        scratch_shapes=[
+            pltpu.VMEM((count, *block), BF16),
+            pltpu.VMEM(back, BF16),
+            pltpu.SemaphoreType.DMA((count + 1,)),
+        ],
         compiler_params=pltpu.CompilerParams(vmem_limit_bytes=24 * 2**20),
-        name="return_rows",
-    )(*on_chip(inner, score, gate, up))
+        cost_estimate=pl.CostEstimate(
+            flops=2 * slots * features * 6 * hidden_size, bytes_accessed=2**23, transcendentals=0
+        ),
+        name="expert_late",
+    )(place, *on_chip(gate, up, inner, score, inputs, scaled, hidden))
 
 
 def combine_kernel(capacity, ids_ref, slot_ref, score_ref, rows_ref, token_ref, grad_ref):
@@ -306,20 +341,25 @@
         way: [(s * ring + i, s * ring + (i + way) % ring) for s in range(2) for i in range(ring)]
         for way in (1, -1)
     }
-    block = lambda ahead, piece: grads[2 * (ahead % ring) + piece]
+    across = lambda block: lax.ppermute(
+        block, "dp", [(i, (i + ring) % (2 * ring)) for i in range(2 * ring)]
+    )
+    block = lambda ahead, piece: grads[ahead % ring, piece]
+    joined = {k % ring: add(block(k, 1), across(block(k, 0))) for k in (far, far - 1, 1 - far)}
     carried = {}
     for hop in range(far, 0, -1):
         for piece in range(2):
             for way in (1, -1):
-                if hop == far and piece != (0 if way == 1 else 1):
+                if piece == 0 and hop > 2 or hop == far and way == -1:
                     continue
                 own = block(way * hop, piece)
+                if piece == 1:
+                    own = joined.get(way * hop % ring, own)
                 if (way, piece) in carried:
                     own = add(own, carried[way, piece])
                 carried[way, piece] = lax.ppermute(own, "dp", moves[way])
-    return [
-        (block(0, piece), carried[1, piece], carried[-1, piece]) for piece in range(2)
-    ]
+    other = across(add(block(0, 0), carried[1, 0], carried[-1, 0]))
+    return block(0, 1), carried[1, 1], carried[-1, 1], other
 
 
 def on_device(
@@ -338,20 +378,20 @@
     index = lax.axis_index("dp")
     side = (index >= ring).astype(jnp.int32)
     place = jnp.stack([side, index - side * ring])
-    gate, up, inner, score, *grads = expert_grads(place, ring, received, gate, up, down, capacity)
-    back = return_rows(inner, score, gate, up, capacity)
+    held = expert_first(place, ring, received, gate, up, down, capacity)
+    held, early = held[:7], held[7:]
+    back, *late = expert_late(place, ring, *held, capacity)
+    grads = dict(zip(early_blocks(ring) + late_blocks(ring), [*early, *late]))
     returned = lax.all_to_all(
         back.reshape(experts, 2 * capacity, back.shape[1]),
         "expert", split_axis=0, concat_axis=0, tiled=True,
     ).reshape(back.shape)
-    for_other, kept = ring_sums(grads, ring)
-    other = lax.ppermute(
-        add(*for_other), "dp", [(i, (i + ring) % (2 * ring)) for i in range(2 * ring)]
-    )
+    *parts, other = ring_sums(grads, ring)
     token_grad, score_grad = combine(
         expert_ids, slot_index, gate_scores, returned, features, capacity
     )
-    grad_gate, grad_up, grad_down = split_grads(*kept, other)
+    other, score_grad = lax.optimization_barrier((other, score_grad))
+    grad_gate, grad_up, grad_down = split_grads(*parts, other)
     return token_grad, score_grad.reshape(count), grad_gate[None], grad_up[None], grad_down[None]
 
 

time: 172 us -> 193 us (1.12)
  the two profiles are of different devices: /device:TPU:2 before, /device:TPU:18 now
where the time goes in v5:
time: 193 us; the launch traced here: 192 us
  starting transfers between devices  87.1 us (45%)
  waiting for transfers between devices  86.7 us (45%)
  Pallas kernels  17.2 us (9%)
    all_to_all x1, waiting for transfers between devices, on_device(): lax.all_to_all(send.reshape(experts, 2 * capacity, features), 'expert', s...  50.8 us
    ppermute x11, starting transfers between devices, ring_sums(): carried[way, piece] = lax.ppermute(own, 'dp', moves[way])  49.1 us
    ppermute x4, waiting for transfers between devices, ring_sums(): lax.ppermute(block, 'dp', [(i, (i + ring) % (2 * ring)) for i in range(2...  25 us
    all_to_all x1, starting transfers between devices, on_device(): lax.all_to_all(back.reshape(experts, 2 * capacity, back.shape[1]), 'exper...  13.4 us
    all_to_all x1, starting transfers between devices, on_device(): lax.all_to_all(send.reshape(experts, 2 * capacity, features), 'expert', s...  12.7 us
    ppermute x4, starting transfers between devices, ring_sums(): lax.ppermute(block, 'dp', [(i, (i + ring) % (2 * ring)) for i in range(2...  12 us
    ppermute x11, waiting for transfers between devices, ring_sums(): carried[way, piece] = lax.ppermute(own, 'dp', moves[way])  10.9 us
    pallas_call x1, Pallas kernels, expert_first(): pl.pallas_call(functools.partial(expert_kernel, capacity, ring), in_specs...  5.49 us
  transfers between devices with their start and end apart: 17, of which 7 were waited for; matrix products, arithmetic and copies ran while one was open for 0% of the time, Pallas kernels for 1%

profile of v5, /device:TPU:18, one launch (start us, length us, event | category | flops | bytes accessed | tf_op | source)
XLA Modules:
  0.0 192.3 jit_solution(5493122862224688327)
XLA Ops:
  0.6 3.2 %dispatch.1 = bf16[512,2048]{1,0:T(8,128)(2,1)} custom-call(s32[1,128]{1,0:T(1,128)} %bitcast.23, s32[1,128]{1,0:T(1,128)} %bitcast.25, bf16[1,128]{1,0:T(2,128)(2,1)} %bitcast.27, bf16[128,2048]{1,0:T(8,128)(2,1)} %tokens_hbm.1, bf16[128,2048]{1,0:T(8,128)(2,1)} %cotan_hbm.1), custom_call_target="tpu_custom_call" | custom-call | tf_op jit(solution)/shard_map/dispatch/pallas_call | solution.py:74
  3.8 12.7 %all-to-all-start = ((bf16[64,8,2048]{2,1,0:T(8,128)(2,1)}), bf16[64,8,2048]{2,1,0:T(8,128)(2,1)S(1)}, u32[]{:S(2)}, u32[]{:S(2)}) async-start(bf16[64,8,2048]{2,1,0:T(8,128)(2,1)} %bitcast.18), calls=%async_computation | async-start | bytes 4194304 | tf_op jit(solution)/shard_map/all_to_all | solution.py:373
  16.5 0.1 pad_add_fusion.place_ref
  16.6 50.8 %all-to-all-done = bf16[64,8,2048]{2,1,0:T(8,128)(2,1)S(1)} async-done(((bf16[64,8,2048]{2,1,0:T(8,128)(2,1)}), bf16[64,8,2048]{2,1,0:T(8,128)(2,1)S(1)}, u32[]{:S(2)}, u32[]{:S(2)}) %all-to-all-start) | async-done | bytes 2097184 | tf_op jit(solution)/shard_map/all_to_all | solution.py:373
  67.5 5.5 %expert_first.1 = (bf16[2048,384]{1,0:T(8,128)(2,1)S(1)}, bf16[2048,384]{1,0:T(8,128)(2,1)S(1)}, bf16[256,768]{1,0:T(8,128)(2,1)S(1)}, bf16[256,128]{1,0:T(8,128...) custom-call(s32[2]{0:T(128)S(1)} %pad_add_fusion.place_ref, ...), custom_call_target="tpu_custom_call" | custom-call | tf_op jit(solution)/shard_map/expert_first/pallas_call | solution.py:181
  73.0 4.8 %expert_late.1 = (bf16[512,1152]{1,0:T(8,128)(2,1)}, bf16[128,1152]{1,0:T(8,128)(2,1)}, bf16[128,1152]{1,0:T(8,128)(2,1)}, bf16[128,1152]{1,0:T(8,128)(2,1)}, bf...) custom-call(s32[2]{0:T(128)S(1)} %pad_add_fusion.place_ref, ...), custom_call_target="tpu_custom_call" | custom-call | flops 2415919104 | bytes 8388608 | tf_op jit(solution)/shard_map/expert_late/pallas_call | solution.py:242
  77.8 0.0 copy-start.15
  77.9 13.4 %all-to-all-start.1 = ((bf16[64,8,1152]{2,1,0:T(8,128)(2,1)}), bf16[64,8,1152]{2,1,0:T(8,128)(2,1)S(1)}, u32[]{:S(2)}, u32[]{:S(2)}) async-start(bf16[64,8,1152]{2,1,0:T(8,128)(2,1)} %bitcast.22), calls=%async_computation.1 | async-start | bytes 2359296 | tf_op jit(solution)/shard_map/all_to_all | solution.py:385
  91.3 4.1 %collective-permute-start.6 = (bf16[128,1152]{1,0:T(8,128)(2,1)S(1)}, bf16[128,1152]{1,0:T(8,128)(2,1)S(1)}, u32[]{:S(2)}, u32[]{:S(2)}) collective-permute-start(bf16[128,1152]{1,0:T(8,128)(2,1)S(1)} %copy-done.15), channel_id=1, source_target_pairs={{0,8},{1,9},{2,10},{3,11},{4,12},{5,13},{6,14},{7,15},{8,0},{9,1},... | collective-permute-start | bytes 884744 | tf_op jit(solution)/shard_map/ppermute | solution.py:344
  95.3 1.9 collective-permute-start.11
  97.3 3.9 %collective-permute-start.5 = (bf16[128,1152]{1,0:T(8,128)(2,1)S(1)}, bf16[128,1152]{1,0:T(8,128)(2,1)S(1)}, u32[]{:S(2)}, u32[]{:S(2)}) collective-permute-start(bf16[128,1152]{1,0:T(8,128)(2,1)S(1)} %copy-done.13), channel_id=1, source_target_pairs={{0,8},{1,9},{2,10},{3,11},{4,12},{5,13},{6,14},{7,15},{8,0},{9,1},... | collective-permute-start | bytes 884744 | tf_op jit(solution)/shard_map/ppermute | solution.py:344
  101.2 25.0 %collective-permute-done.6.refs_1_ = bf16[128,1152]{1,0:T(8,128)(2,1)S(1)} collective-permute-done((bf16[128,1152]{1,0:T(8,128)(2,1)S(1)}, bf16[128,1152]{1,0:T(8,128)(2,1)S(1)}, u32[]{:S(2)}, u32[]{:S(2)}) %collective-permute-start.6) | collective-permute-done | bytes 294944 | tf_op jit(solution)/shard_map/ppermute | solution.py:344
  126.2 0.1 add.17
  126.3 4.0 %collective-permute-start.7 = (bf16[128,1152]{1,0:T(8,128)(2,1)S(1)}, bf16[128,1152]{1,0:T(8,128)(2,1)S(1)}, u32[]{:S(2)}, u32[]{:S(2)}) collective-permute-start(bf16[128,1152]{1,0:T(8,128)(2,1)S(1)} %add.17), channel_id=1, source_target_pairs={{0,1},{1,2},{2,3},{3,4},{4,5},{5,6},{6,7},{7,0},{8,9},{9,10},{10,1... | collective-permute-start | bytes 884744 | tf_op jit(solution)/shard_map/ppermute | solution.py:360
  130.3 9.5 %collective-permute-start = (bf16[128,1152]{1,0:T(8,128)(2,1)S(1)}, bf16[128,1152]{1,0:T(8,128)(2,1)S(1)}, u32[]{:S(2)}, u32[]{:S(2)}) collective-permute-start(bf16[128,1152]{1,0:T(8,128)(2,1)S(1)} %copy-done.12), channel_id=1, source_target_pairs={{0,1},{1,2},{2,3},{3,4},{4,5},{5,6},{6,7},{7,0},{8,9},{9,10},{10,1... | collective-permute-start | bytes 884744 | tf_op jit(solution)/shard_map/ppermute | solution.py:360
  139.8 6.5 %collective-permute-start.2 = (bf16[128,1152]{1,0:T(8,128)(2,1)S(1)}, bf16[128,1152]{1,0:T(8,128)(2,1)S(1)}, u32[]{:S(2)}, u32[]{:S(2)}) collective-permute-start(bf16[128,1152]{1,0:T(8,128)(2,1)S(1)} %copy-done.11), channel_id=1, source_target_pairs={{0,7},{1,0},{2,1},{3,2},{4,3},{5,4},{6,5},{7,6},{8,15},{9,8},{10,9... | collective-permute-start | bytes 884744 | tf_op jit(solution)/shard_map/ppermute | solution.py:360
  146.3 0.0 collective-permute-done.11.refs_1_
  146.3 0.1 add.21
  146.4 5.8 %collective-permute-start.12 = (bf16[128,1152]{1,0:T(8,128)(2,1)S(1)}, bf16[128,1152]{1,0:T(8,128)(2,1)S(1)}, u32[]{:S(2)}, u32[]{:S(2)}) collective-permute-start(bf16[128,1152]{1,0:T(8,128)(2,1)S(1)} %add.21), channel_id=1, source_target_pairs={{0,7},{1,0},{2,1},{3,2},{4,3},{5,4},{6,5},{7,6},{8,15},{9,8},{10,9... | collective-permute-start | bytes 884744 | tf_op jit(solution)/shard_map/ppermute | solution.py:360
  152.2 0.0 collective-permute-done.5.refs_1_
  152.2 0.1 add.16.refs_0_
  152.3 0.0 collective-permute-done.7.refs_1_
  152.3 0.1 add.18
  152.4 1.9 collective-permute-start.8
  154.3 1.2 collective-permute-done.refs_1_
  155.5 0.1 add.13
  155.6 1.9 collective-permute-start.1
  157.6 0.1 add.14
  157.7 6.0 %collective-permute-start.3 = (bf16[128,1152]{1,0:T(8,128)(2,1)S(1)}, bf16[128,1152]{1,0:T(8,128)(2,1)S(1)}, u32[]{:S(2)}, u32[]{:S(2)}) collective-permute-start(bf16[128,1152]{1,0:T(8,128)(2,1)S(1)} %add.14), channel_id=1, source_target_pairs={{0,7},{1,0},{2,1},{3,2},{4,3},{5,4},{6,5},{7,6},{8,15},{9,8},{10,9... | collective-permute-start | bytes 884744 | tf_op jit(solution)/shard_map/ppermute | solution.py:360
  163.7 0.0 collective-permute-done.12.refs_1_
  163.7 0.1 add.22
  163.8 4.1 %collective-permute-start.13 = (bf16[128,1152]{1,0:T(8,128)(2,1)S(1)}, bf16[128,1152]{1,0:T(8,128)(2,1)S(1)}, u32[]{:S(2)}, u32[]{:S(2)}) collective-permute-start(bf16[128,1152]{1,0:T(8,128)(2,1)S(1)} %add.22), channel_id=1, source_target_pairs={{0,7},{1,0},{2,1},{3,2},{4,3},{5,4},{6,5},{7,6},{8,15},{9,8},{10,9... | collective-permute-start | bytes 884744 | tf_op jit(solution)/shard_map/ppermute | solution.py:360
  167.9 0.1 add.19
  168.0 1.9 collective-permute-start.9
  169.9 0.0 collective-permute-done.1.refs_1_
  170.0 1.2 collective-permute-done.3.refs_2_
  171.1 0.1 add.15
  171.3 2.1 %collective-permute-start.4 = (bf16[128,1152]{1,0:T(8,128)(2,1)S(1)}, bf16[128,1152]{1,0:T(8,128)(2,1)S(1)}, u32[]{:S(2)}, u32[]{:S(2)}) collective-permute-start(bf16[128,1152]{1,0:T(8,128)(2,1)S(1)} %add.15), channel_id=1, source_target_pairs={{0,8},{1,9},{2,10},{3,11},{4,12},{5,13},{6,14},{7,15},{8,0},{9,1},... | collective-permute-start | bytes 884744 | tf_op jit(solution)/shard_map/ppermute | solution.py:344
  173.3 2.3 %collective-permute-done.13.refs_1_ = bf16[128,1152]{1,0:T(8,128)(2,1)S(1)} collective-permute-done((bf16[128,1152]{1,0:T(8,128)(2,1)S(1)}, bf16[128,1152]{1,0:T(8,128)(2,1)S(1)}, u32[]{:S(2)}, u32[]{:S(2)}) %collective-permute-start.13) | collective-permute-done | bytes 294944 | tf_op jit(solution)/shard_map/ppermute | solution.py:360
  175.7 0.1 add.23
  175.7 5.6 %collective-permute-start.14 = (bf16[128,1152]{1,0:T(8,128)(2,1)S(1)}, bf16[128,1152]{1,0:T(8,128)(2,1)S(1)}, u32[]{:S(2)}, u32[]{:S(2)}) collective-permute-start(bf16[128,1152]{1,0:T(8,128)(2,1)S(1)} %add.23), channel_id=1, source_target_pairs={{0,7},{1,0},{2,1},{3,2},{4,3},{5,4},{6,5},{7,6},{8,15},{9,8},{10,9... | collective-permute-start | bytes 884744 | tf_op jit(solution)/shard_map/ppermute | solution.py:360
  181.4 0.1 add.20
  181.5 1.9 collective-permute-start.10
  183.4 2.0 %combine.1 = (bf16[128,2048]{1,0:T(8,128)(2,1)}, bf16[1,128]{1,0:T(2,128)(2,1)}) custom-call(s32[1,128]{1,0:T(1,128)} %bitcast.24, s32[1,128]{1,0:T(1,128)} %bitcast.26, bf16[1,128]{1,0:T(2,128)(2,1)} %bitcast.28, bf16[512,1152]{1,0:T(8,128)(2,1)S(1)} %bitcast.17), custom_call_target="tpu_custom_call" | custom-call | tf_op jit(solution)/shard_map/combine/pallas_call | solution.py:278
  185.4 0.0 collective-permute-done.4.other_ref
  185.4 0.7 collective-permute-done.14.down_way_ref
  186.1 5.4 %collective-permute-done.10.up_way_ref = bf16[128,1152]{1,0:T(8,128)(2,1)S(1)} collective-permute-done((bf16[128,1152]{1,0:T(8,128)(2,1)S(1)}, bf16[128,1152]{1,0:T(8,128)(2,1)S(1)}, u32[]{:S(2)}, u32[]{:S(2)}) %collective-permute-start.10) | collective-permute-done | bytes 294944 | tf_op jit(solution)/shard_map/ppermute | solution.py:360
  191.5 0.8 split_grads.1
  (35 shorter events, 0.1 us)
Async XLA Ops:
  3.8 63.6 %all-to-all-start = ((bf16[64,8,2048]{2,1,0:T(8,128)(2,1)}), bf16[64,8,2048]{2,1,0:T(8,128)(2,1)S(1)}, u32[]{:S(2)}, u32[]{:S(2)}) async-start(bf16[64,8,2048]{2,1,0:T(8,128)(2,1)} %bitcast.18), calls=%async_computation | async-start | bytes 4194304 | tf_op jit(solution)/shard_map/all_to_all | solution.py:373
  77.8 13.5 %copy-start.15 = (bf16[128,1152]{1,0:T(8,128)(2,1)S(1)}, bf16[128,1152]{1,0:T(8,128)(2,1)}, u32[]{:S(2)}) copy-start(bf16[128,1152]{1,0:T(8,128)(2,1)} %get-tuple-element.58) | copy-start | bytes 884740
  77.8 17.5 %copy-start.14 = (bf16[128,1152]{1,0:T(8,128)(2,1)S(1)}, bf16[128,1152]{1,0:T(8,128)(2,1)}, u32[]{:S(2)}) copy-start(bf16[128,1152]{1,0:T(8,128)(2,1)} %get-tuple-element.62) | copy-start | bytes 884740
  77.8 19.5 %copy-start.13 = (bf16[128,1152]{1,0:T(8,128)(2,1)S(1)}, bf16[128,1152]{1,0:T(8,128)(2,1)}, u32[]{:S(2)}) copy-start(bf16[128,1152]{1,0:T(8,128)(2,1)} %get-tuple-element.56) | copy-start | bytes 884740
  77.8 48.4 %copy-start.8 = (bf16[128,1152]{1,0:T(8,128)(2,1)S(1)}, bf16[128,1152]{1,0:T(8,128)(2,1)}, u32[]{:S(2)}) copy-start(bf16[128,1152]{1,0:T(8,128)(2,1)} %get-tuple-element.57.refs_0_) | copy-start | bytes 884740
  77.8 52.4 %copy-start.12 = (bf16[128,1152]{1,0:T(8,128)(2,1)S(1)}, bf16[128,1152]{1,0:T(8,128)(2,1)}, u32[]{:S(2)}) copy-start(bf16[128,1152]{1,0:T(8,128)(2,1)} %get-tuple-element.47) | copy-start | bytes 884740
  77.8 61.9 %copy-start.11 = (bf16[128,1152]{1,0:T(8,128)(2,1)S(1)}, bf16[128,1152]{1,0:T(8,128)(2,1)}, u32[]{:S(2)}) copy-start(bf16[128,1152]{1,0:T(8,128)(2,1)} %get-tuple-element.49) | copy-start | bytes 884740
  77.8 68.4 %copy-start.7 = (bf16[128,1152]{1,0:T(8,128)(2,1)S(1)}, bf16[128,1152]{1,0:T(8,128)(2,1)}, u32[]{:S(2)}) copy-start(bf16[128,1152]{1,0:T(8,128)(2,1)} %get-tuple-element.61.refs_0_) | copy-start | bytes 884740
  77.9 74.3 %copy-start.6 = (bf16[128,1152]{1,0:T(8,128)(2,1)S(1)}, bf16[128,1152]{1,0:T(8,128)(2,1)}, u32[]{:S(2)}) copy-start(bf16[128,1152]{1,0:T(8,128)(2,1)} %get-tuple-element.55.refs_0_) | copy-start | bytes 884740
  77.9 105.5 %all-to-all-start.1 = ((bf16[64,8,1152]{2,1,0:T(8,128)(2,1)}), bf16[64,8,1152]{2,1,0:T(8,128)(2,1)S(1)}, u32[]{:S(2)}, u32[]{:S(2)}) async-start(bf16[64,8,1152]{2,1,0:T(8,128)(2,1)} %bitcast.22), calls=%async_computation.1 | async-start | bytes 2359296 | tf_op jit(solution)/shard_map/all_to_all | solution.py:385
  91.3 34.9 %collective-permute-start.6 = (bf16[128,1152]{1,0:T(8,128)(2,1)S(1)}, bf16[128,1152]{1,0:T(8,128)(2,1)S(1)}, u32[]{:S(2)}, u32[]{:S(2)}) collective-permute-start(bf16[128,1152]{1,0:T(8,128)(2,1)S(1)} %copy-done.15), channel_id=1, source_target_pairs={{0,8},{1,9},{2,10},{3,11},{4,12},{5,13},{6,14},{7,15},{8,0},{9,1},... | collective-permute-start | bytes 884744 | tf_op jit(solution)/shard_map/ppermute | solution.py:344
  95.3 50.9 %collective-permute-start.11 = (bf16[128,1152]{1,0:T(8,128)(2,1)S(1)}, bf16[128,1152]{1,0:T(8,128)(2,1)S(1)}, u32[]{:S(2)}, u32[]{:S(2)}) collective-permute-start(bf16[128,1152]{1,0:T(8,128)(2,1)S(1)} %copy-done.14), channel_id=1, source_target_pairs={{0,8},{1,9},{2,10},{3,11},{4,12},{5,13},{6,14},{7,15},{8,0},{9,1},... | collective-permute-start | bytes 884744 | tf_op jit(solution)/shard_map/ppermute | solution.py:344
  97.3 54.9 %collective-permute-start.5 = (bf16[128,1152]{1,0:T(8,128)(2,1)S(1)}, bf16[128,1152]{1,0:T(8,128)(2,1)S(1)}, u32[]{:S(2)}, u32[]{:S(2)}) collective-permute-start(bf16[128,1152]{1,0:T(8,128)(2,1)S(1)} %copy-done.13), channel_id=1, source_target_pairs={{0,8},{1,9},{2,10},{3,11},{4,12},{5,13},{6,14},{7,15},{8,0},{9,1},... | collective-permute-start | bytes 884744 | tf_op jit(solution)/shard_map/ppermute | solution.py:344
  126.2 29.3 %copy-start.5 = (bf16[128,1152]{1,0:T(8,128)(2,1)S(1)}, bf16[128,1152]{1,0:T(8,128)(2,1)}, u32[]{:S(2)}) copy-start(bf16[128,1152]{1,0:T(8,128)(2,1)} %get-tuple-element.46.refs_0_) | copy-start | bytes 884740
  126.3 26.0 %collective-permute-start.7 = (bf16[128,1152]{1,0:T(8,128)(2,1)S(1)}, bf16[128,1152]{1,0:T(8,128)(2,1)S(1)}, u32[]{:S(2)}, u32[]{:S(2)}) collective-permute-start(bf16[128,1152]{1,0:T(8,128)(2,1)S(1)} %add.17), channel_id=1, source_target_pairs={{0,1},{1,2},{2,3},{3,4},{4,5},{5,6},{6,7},{7,0},{8,9},{9,10},{10,1... | collective-permute-start | bytes 884744 | tf_op jit(solution)/shard_map/ppermute | solution.py:360
  130.3 25.3 %collective-permute-start = (bf16[128,1152]{1,0:T(8,128)(2,1)S(1)}, bf16[128,1152]{1,0:T(8,128)(2,1)S(1)}, u32[]{:S(2)}, u32[]{:S(2)}) collective-permute-start(bf16[128,1152]{1,0:T(8,128)(2,1)S(1)} %copy-done.12), channel_id=1, source_target_pairs={{0,1},{1,2},{2,3},{3,4},{4,5},{5,6},{6,7},{7,0},{8,9},{9,10},{10,1... | collective-permute-start | bytes 884744 | tf_op jit(solution)/shard_map/ppermute | solution.py:360
  139.8 17.8 %collective-permute-start.2 = (bf16[128,1152]{1,0:T(8,128)(2,1)S(1)}, bf16[128,1152]{1,0:T(8,128)(2,1)S(1)}, u32[]{:S(2)}, u32[]{:S(2)}) collective-permute-start(bf16[128,1152]{1,0:T(8,128)(2,1)S(1)} %copy-done.11), channel_id=1, source_target_pairs={{0,7},{1,0},{2,1},{3,2},{4,3},{5,4},{6,5},{7,6},{8,15},{9,8},{10,9... | collective-permute-start | bytes 884744 | tf_op jit(solution)/shard_map/ppermute | solution.py:360
  146.3 11.3 %copy-start.4 = (bf16[128,1152]{1,0:T(8,128)(2,1)S(1)}, bf16[128,1152]{1,0:T(8,128)(2,1)}, u32[]{:S(2)}) copy-start(bf16[128,1152]{1,0:T(8,128)(2,1)} %get-tuple-element.48.refs_0_) | copy-start | bytes 884740
  146.4 17.3 %collective-permute-start.12 = (bf16[128,1152]{1,0:T(8,128)(2,1)S(1)}, bf16[128,1152]{1,0:T(8,128)(2,1)S(1)}, u32[]{:S(2)}, u32[]{:S(2)}) collective-permute-start(bf16[128,1152]{1,0:T(8,128)(2,1)S(1)} %add.21), channel_id=1, source_target_pairs={{0,7},{1,0},{2,1},{3,2},{4,3},{5,4},{6,5},{7,6},{8,15},{9,8},{10,9... | collective-permute-start | bytes 884744 | tf_op jit(solution)/shard_map/ppermute | solution.py:360
  152.2 11.5 %copy-start.3 = (bf16[128,1152]{1,0:T(8,128)(2,1)S(1)}, bf16[128,1152]{1,0:T(8,128)(2,1)}, u32[]{:S(2)}) copy-start(bf16[128,1152]{1,0:T(8,128)(2,1)} %get-tuple-element.60.refs_0_) | copy-start | bytes 884740
  152.3 15.6 %copy-start.2 = (bf16[128,1152]{1,0:T(8,128)(2,1)S(1)}, bf16[128,1152]{1,0:T(8,128)(2,1)}, u32[]{:S(2)}) copy-start(bf16[128,1152]{1,0:T(8,128)(2,1)} %get-tuple-element.54.refs_0_) | copy-start | bytes 884740
  152.4 15.5 %collective-permute-start.8 = (bf16[128,1152]{1,0:T(8,128)(2,1)S(1)}, bf16[128,1152]{1,0:T(8,128)(2,1)S(1)}, u32[]{:S(2)}, u32[]{:S(2)}) collective-permute-start(bf16[128,1152]{1,0:T(8,128)(2,1)S(1)} %add.18), channel_id=1, source_target_pairs={{0,1},{1,2},{2,3},{3,4},{4,5},{5,6},{6,7},{7,0},{8,9},{9,10},{10,1... | collective-permute-start | bytes 884744 | tf_op jit(solution)/shard_map/ppermute | solution.py:360
  155.5 15.6 %copy-start.10 = (bf16[128,1152]{1,0:T(8,128)(2,1)S(1)}, bf16[128,1152]{1,0:T(8,128)(2,1)}, u32[]{:S(2)}) copy-start(bf16[128,1152]{1,0:T(8,128)(2,1)} %get-tuple-element.45.refs_0_) | copy-start | bytes 884740
  155.6 14.3 %collective-permute-start.1 = (bf16[128,1152]{1,0:T(8,128)(2,1)S(1)}, bf16[128,1152]{1,0:T(8,128)(2,1)S(1)}, u32[]{:S(2)}, u32[]{:S(2)}) collective-permute-start(bf16[128,1152]{1,0:T(8,128)(2,1)S(1)} %add.13), channel_id=1, source_target_pairs={{0,1},{1,2},{2,3},{3,4},{4,5},{5,6},{6,7},{7,0},{8,9},{9,10},{10,1... | collective-permute-start | bytes 884744 | tf_op jit(solution)/shard_map/ppermute | solution.py:360
  157.6 18.0 %copy-start.1 = (bf16[128,1152]{1,0:T(8,128)(2,1)S(1)}, bf16[128,1152]{1,0:T(8,128)(2,1)}, u32[]{:S(2)}) copy-start(bf16[128,1152]{1,0:T(8,128)(2,1)} %get-tuple-element.59.refs_0_) | copy-start | bytes 884740
  157.7 13.5 %collective-permute-start.3 = (bf16[128,1152]{1,0:T(8,128)(2,1)S(1)}, bf16[128,1152]{1,0:T(8,128)(2,1)S(1)}, u32[]{:S(2)}, u32[]{:S(2)}) collective-permute-start(bf16[128,1152]{1,0:T(8,128)(2,1)S(1)} %add.14), channel_id=1, source_target_pairs={{0,7},{1,0},{2,1},{3,2},{4,3},{5,4},{6,5},{7,6},{8,15},{9,8},{10,9... | collective-permute-start | bytes 884744 | tf_op jit(solution)/shard_map/ppermute | solution.py:360
  163.8 17.6 %copy-start = (bf16[128,1152]{1,0:T(8,128)(2,1)S(1)}, bf16[128,1152]{1,0:T(8,128)(2,1)}, u32[]{:S(2)}) copy-start(bf16[128,1152]{1,0:T(8,128)(2,1)} %get-tuple-element.53.refs_0_) | copy-start | bytes 884740
  163.8 11.9 %collective-permute-start.13 = (bf16[128,1152]{1,0:T(8,128)(2,1)S(1)}, bf16[128,1152]{1,0:T(8,128)(2,1)S(1)}, u32[]{:S(2)}, u32[]{:S(2)}) collective-permute-start(bf16[128,1152]{1,0:T(8,128)(2,1)S(1)} %add.22), channel_id=1, source_target_pairs={{0,7},{1,0},{2,1},{3,2},{4,3},{5,4},{6,5},{7,6},{8,15},{9,8},{10,9... | collective-permute-start | bytes 884744 | tf_op jit(solution)/shard_map/ppermute | solution.py:360
  168.0 13.4 %collective-permute-start.9 = (bf16[128,1152]{1,0:T(8,128)(2,1)S(1)}, bf16[128,1152]{1,0:T(8,128)(2,1)S(1)}, u32[]{:S(2)}, u32[]{:S(2)}) collective-permute-start(bf16[128,1152]{1,0:T(8,128)(2,1)S(1)} %add.19), channel_id=1, source_target_pairs={{0,1},{1,2},{2,3},{3,4},{4,5},{5,6},{6,7},{7,0},{8,9},{9,10},{10,1... | collective-permute-start | bytes 884744 | tf_op jit(solution)/shard_map/ppermute | solution.py:360
  171.3 20.2 %copy-start.9 = (bf16[128,1152]{1,0:T(8,128)(2,1)S(1)}, bf16[128,1152]{1,0:T(8,128)(2,1)}, u32[]{:S(2)}) copy-start(bf16[128,1152]{1,0:T(8,128)(2,1)} %get-tuple-element.52.own_ref) | copy-start | bytes 884740
  171.3 14.1 %collective-permute-start.4 = (bf16[128,1152]{1,0:T(8,128)(2,1)S(1)}, bf16[128,1152]{1,0:T(8,128)(2,1)S(1)}, u32[]{:S(2)}, u32[]{:S(2)}) collective-permute-start(bf16[128,1152]{1,0:T(8,128)(2,1)S(1)} %add.15), channel_id=1, source_target_pairs={{0,8},{1,9},{2,10},{3,11},{4,12},{5,13},{6,14},{7,15},{8,0},{9,1},... | collective-permute-start | bytes 884744 | tf_op jit(solution)/shard_map/ppermute | solution.py:344
  175.7 10.3 %collective-permute-start.14 = (bf16[128,1152]{1,0:T(8,128)(2,1)S(1)}, bf16[128,1152]{1,0:T(8,128)(2,1)S(1)}, u32[]{:S(2)}, u32[]{:S(2)}) collective-permute-start(bf16[128,1152]{1,0:T(8,128)(2,1)S(1)} %add.23), channel_id=1, source_target_pairs={{0,7},{1,0},{2,1},{3,2},{4,3},{5,4},{6,5},{7,6},{8,15},{9,8},{10,9... | collective-permute-start | bytes 884744 | tf_op jit(solution)/shard_map/ppermute | solution.py:360
  181.5 10.0 %collective-permute-start.10 = (bf16[128,1152]{1,0:T(8,128)(2,1)S(1)}, bf16[128,1152]{1,0:T(8,128)(2,1)S(1)}, u32[]{:S(2)}, u32[]{:S(2)}) collective-permute-start(bf16[128,1152]{1,0:T(8,128)(2,1)S(1)} %add.20), channel_id=1, source_target_pairs={{0,1},{1,2},{2,3},{3,4},{4,5},{5,6},{6,7},{7,0},{8,9},{9,10},{10,1... | collective-permute-start | bytes 884744 | tf_op jit(solution)/shard_map/ppermute | solution.py:360

commit v6 on v5

--- a/solution.py
+++ b/solution.py
@@ -106,7 +106,8 @@
 
 
 def early_blocks(ring):
-    return [(ring // 2, 0), (2, 0), (ring - 2, 0)]
+    far = ring // 2
+    return [(far, 0), (far, 1), (far - 1, 1), (far + 1, 0)]
 
 
 def late_blocks(ring):
@@ -335,31 +336,30 @@
     )(*on_chip(*parts))
 
 
-def ring_sums(grads, ring):
+def ring_sums(grads, ring, back):
     far = ring // 2
     moves = {
         way: [(s * ring + i, s * ring + (i + way) % ring) for s in range(2) for i in range(ring)]
         for way in (1, -1)
     }
-    across = lambda block: lax.ppermute(
-        block, "dp", [(i, (i + ring) % (2 * ring)) for i in range(2 * ring)]
-    )
     block = lambda ahead, piece: grads[ahead % ring, piece]
-    joined = {k % ring: add(block(k, 1), across(block(k, 0))) for k in (far, far - 1, 1 - far)}
     carried = {}
     for hop in range(far, 0, -1):
         for piece in range(2):
             for way in (1, -1):
-                if piece == 0 and hop > 2 or hop == far and way == -1:
+                if hop == far and piece != (0 if way == 1 else 1):
                     continue
                 own = block(way * hop, piece)
-                if piece == 1:
-                    own = joined.get(way * hop % ring, own)
                 if (way, piece) in carried:
                     own = add(own, carried[way, piece])
                 carried[way, piece] = lax.ppermute(own, "dp", moves[way])
-    other = across(add(block(0, 0), carried[1, 0], carried[-1, 0]))
-    return block(0, 1), carried[1, 1], carried[-1, 1], other
+        if hop == far:
+            back, *_ = lax.optimization_barrier((back, *carried.values()))
+    other = lax.ppermute(
+        add(block(0, 0), carried[1, 0], carried[-1, 0]),
+        "dp", [(i, (i + ring) % (2 * ring)) for i in range(2 * ring)],
+    )
+    return back, block(0, 1), carried[1, 1], carried[-1, 1], other
 
 
 def on_device(
@@ -382,11 +382,11 @@
     held, early = held[:7], held[7:]
     back, *late = expert_late(place, ring, *held, capacity)
     grads = dict(zip(early_blocks(ring) + late_blocks(ring), [*early, *late]))
+    back, *parts, other = ring_sums(grads, ring, back)
     returned = lax.all_to_all(
         back.reshape(experts, 2 * capacity, back.shape[1]),
         "expert", split_axis=0, concat_axis=0, tiled=True,
     ).reshape(back.shape)
-    *parts, other = ring_sums(grads, ring)
     token_grad, score_grad = combine(
         expert_ids, slot_index, gate_scores, returned, features, capacity
     )

time: 193 us -> 172 us (0.89)
  the two profiles are of different devices: /device:TPU:18 before, /device:TPU:80 now
where the time goes in v6:
time: 172 us; the launch traced here: 171 us
  starting transfers between devices  94.2 us (55%)
  waiting for transfers between devices  58.5 us (34%)
  Pallas kernels  17.1 us (10%)
    ppermute x14, starting transfers between devices, ring_sums(): carried[way, piece] = lax.ppermute(own, 'dp', moves[way])  62.6 us
    all_to_all x1, waiting for transfers between devices, on_device(): lax.all_to_all(send.reshape(experts, 2 * capacity, features), 'expert', s...  48.7 us
    all_to_all x1, starting transfers between devices, on_device(): lax.all_to_all(back.reshape(experts, 2 * capacity, back.shape[1]), 'exper...  14.9 us
    all_to_all x1, starting transfers between devices, on_device(): lax.all_to_all(send.reshape(experts, 2 * capacity, features), 'expert', s...  12.8 us
    ppermute x14, waiting for transfers between devices, ring_sums(): carried[way, piece] = lax.ppermute(own, 'dp', moves[way])  9.79 us
    pallas_call x1, Pallas kernels, expert_first(): pl.pallas_call(functools.partial(expert_kernel, capacity, ring), in_specs...  5.53 us
    pallas_call x1, Pallas kernels, expert_late(): pl.pallas_call(functools.partial(late_kernel, capacity, ring), in_specs=[...  4.7 us
    ppermute x1, starting transfers between devices, ring_sums(): lax.ppermute(add(block(0, 0), carried[1, 0], carried[-1, 0]), 'dp', [(i,...  3.89 us
  transfers between devices with their start and end apart: 17, of which 7 were waited for; matrix products, arithmetic and copies ran while one was open for 0% of the time, Pallas kernels for 4%

profile of v6, /device:TPU:80, one launch (start us, length us, event | category | flops | bytes accessed | tf_op | source)
XLA Modules:
  0.0 171.0 jit_solution(2275324551658185331)
XLA Ops:
  0.6 3.2 %dispatch.1 = bf16[512,2048]{1,0:T(8,128)(2,1)} custom-call(s32[1,128]{1,0:T(1,128)} %bitcast.23, s32[1,128]{1,0:T(1,128)} %bitcast.25, bf16[1,128]{1,0:T(2,128)(2,1)} %bitcast.27, bf16[128,2048]{1,0:T(8,128)(2,1)} %tokens_hbm.1, bf16[128,2048]{1,0:T(8,128)(2,1)} %cotan_hbm.1), custom_call_target="tpu_custom_call" | custom-call | tf_op jit(solution)/shard_map/dispatch/pallas_call | solution.py:74
  3.8 12.8 %all-to-all-start = ((bf16[64,8,2048]{2,1,0:T(8,128)(2,1)}), bf16[64,8,2048]{2,1,0:T(8,128)(2,1)S(1)}, u32[]{:S(2)}, u32[]{:S(2)}) async-start(bf16[64,8,2048]{2,1,0:T(8,128)(2,1)} %bitcast.18), calls=%async_computation | async-start | bytes 4194304 | tf_op jit(solution)/shard_map/all_to_all | solution.py:373
  16.7 0.1 pad_add_fusion.place_ref
  16.7 48.7 %all-to-all-done = bf16[64,8,2048]{2,1,0:T(8,128)(2,1)S(1)} async-done(((bf16[64,8,2048]{2,1,0:T(8,128)(2,1)}), bf16[64,8,2048]{2,1,0:T(8,128)(2,1)S(1)}, u32[]{:S(2)}, u32[]{:S(2)}) %all-to-all-start) | async-done | bytes 2097184 | tf_op jit(solution)/shard_map/all_to_all | solution.py:373
  65.4 5.5 %expert_first.1 = (bf16[2048,384]{1,0:T(8,128)(2,1)S(1)}, bf16[2048,384]{1,0:T(8,128)(2,1)S(1)}, bf16[256,768]{1,0:T(8,128)(2,1)S(1)}, bf16[256,128]{1,0:T(8,128...) custom-call(s32[2]{0:T(128)S(1)} %pad_add_fusion.place_ref, ...), custom_call_target="tpu_custom_call" | custom-call | tf_op jit(solution)/shard_map/expert_first/pallas_call | solution.py:182
  70.9 5.2 %collective-permute-start = (bf16[128,1152]{1,0:T(8,128)(2,1)}, bf16[128,1152]{1,0:T(8,128)(2,1)S(1)}, u32[]{:S(2)}, u32[]{:S(2)}) collective-permute-start(bf16[128,1152]{1,0:T(8,128)(2,1)} %get-tuple-element.45), channel_id=1, source_target_pairs={{0,1},{1,2},{2,3},{3,4},{4,5},{5,6},{6,7},{7,0},{8,9},{9,10},{10,1... | collective-permute-start | bytes 884744 | tf_op jit(solution)/shard_map/ppermute | solution.py:355
  76.1 14.0 %collective-permute-start.1 = (bf16[128,1152]{1,0:T(8,128)(2,1)}, bf16[128,1152]{1,0:T(8,128)(2,1)S(1)}, u32[]{:S(2)}, u32[]{:S(2)}) collective-permute-start(bf16[128,1152]{1,0:T(8,128)(2,1)} %get-tuple-element.46), channel_id=1, source_target_pairs={{0,7},{1,0},{2,1},{3,2},{4,3},{5,4},{6,5},{7,6},{8,15},{9,8},{10,9... | collective-permute-start | bytes 884744 | tf_op jit(solution)/shard_map/ppermute | solution.py:355
  90.1 4.7 %expert_late.1 = (bf16[512,1152]{1,0:T(8,128)(2,1)}, bf16[128,1152]{1,0:T(8,128)(2,1)}, bf16[128,1152]{1,0:T(8,128)(2,1)}, bf16[128,1152]{1,0:T(8,128)(2,1)}, bf...) custom-call(s32[2]{0:T(128)S(1)} %pad_add_fusion.place_ref, ...), custom_call_target="tpu_custom_call" | custom-call | flops 2415919104 | bytes 8388608 | tf_op jit(solution)/shard_map/expert_late/pallas_call | solution.py:243
  94.9 0.0 collective-permute-done.refs_1_
  94.9 1.6 collective-permute-done.1.refs_1_
  96.5 14.9 %all-to-all-start.1 = ((bf16[64,8,1152]{2,1,0:T(8,128)(2,1)}), bf16[64,8,1152]{2,1,0:T(8,128)(2,1)S(1)}, u32[]{:S(2)}, u32[]{:S(2)}) async-start(bf16[64,8,1152]{2,1,0:T(8,128)(2,1)} %bitcast.22), calls=%async_computation.1 | async-start | bytes 2359296 | tf_op jit(solution)/shard_map/all_to_all | solution.py:386
  111.4 5.6 %collective-permute-start.5 = (bf16[128,1152]{1,0:T(8,128)(2,1)S(1)}, bf16[128,1152]{1,0:T(8,128)(2,1)S(1)}, u32[]{:S(2)}, u32[]{:S(2)}) collective-permute-start(bf16[128,1152]{1,0:T(8,128)(2,1)S(1)} %copy-done.13), channel_id=1, source_target_pairs={{0,7},{1,0},{2,1},{3,2},{4,3},{5,4},{6,5},{7,6},{8,15},{9,8},{10,9... | collective-permute-start | bytes 884744 | tf_op jit(solution)/shard_map/ppermute | solution.py:355
  117.1 0.1 add.13
  117.1 1.9 %collective-permute-start.2 = (bf16[128,1152]{1,0:T(8,128)(2,1)S(1)}, bf16[128,1152]{1,0:T(8,128)(2,1)S(1)}, u32[]{:S(2)}, u32[]{:S(2)}) collective-permute-start(bf16[128,1152]{1,0:T(8,128)(2,1)S(1)} %add.13), channel_id=1, source_target_pairs={{0,1},{1,2},{2,3},{3,4},{4,5},{5,6},{6,7},{7,0},{8,9},{9,10},{10,1... | collective-permute-start | bytes 884744 | tf_op jit(solution)/shard_map/ppermute | solution.py:355
  119.1 1.9 %collective-permute-start.9 = (bf16[128,1152]{1,0:T(8,128)(2,1)S(1)}, bf16[128,1152]{1,0:T(8,128)(2,1)S(1)}, u32[]{:S(2)}, u32[]{:S(2)}) collective-permute-start(bf16[128,1152]{1,0:T(8,128)(2,1)S(1)} %copy-done.12), channel_id=1, source_target_pairs={{0,1},{1,2},{2,3},{3,4},{4,5},{5,6},{6,7},{7,0},{8,9},{9,10},{10,1... | collective-permute-start | bytes 884744 | tf_op jit(solution)/shard_map/ppermute | solution.py:355
  121.0 2.6 %collective-permute-done.5.refs_1_ = bf16[128,1152]{1,0:T(8,128)(2,1)S(1)} collective-permute-done((bf16[128,1152]{1,0:T(8,128)(2,1)S(1)}, bf16[128,1152]{1,0:T(8,128)(2,1)S(1)}, u32[]{:S(2)}, u32[]{:S(2)}) %collective-permute-start.5) | collective-permute-done | bytes 294944 | tf_op jit(solution)/shard_map/ppermute | solution.py:355
  123.6 0.1 add.16
  123.7 5.6 %collective-permute-start.6 = (bf16[128,1152]{1,0:T(8,128)(2,1)S(1)}, bf16[128,1152]{1,0:T(8,128)(2,1)S(1)}, u32[]{:S(2)}, u32[]{:S(2)}) collective-permute-start(bf16[128,1152]{1,0:T(8,128)(2,1)S(1)} %add.16), channel_id=1, source_target_pairs={{0,7},{1,0},{2,1},{3,2},{4,3},{5,4},{6,5},{7,6},{8,15},{9,8},{10,9... | collective-permute-start | bytes 884744 | tf_op jit(solution)/shard_map/ppermute | solution.py:355
  129.3 0.8 collective-permute-done.2.refs_1_
  130.1 0.1 add.14
  130.2 1.9 %collective-permute-start.3 = (bf16[128,1152]{1,0:T(8,128)(2,1)S(1)}, bf16[128,1152]{1,0:T(8,128)(2,1)S(1)}, u32[]{:S(2)}, u32[]{:S(2)}) collective-permute-start(bf16[128,1152]{1,0:T(8,128)(2,1)S(1)} %add.14), channel_id=1, source_target_pairs={{0,1},{1,2},{2,3},{3,4},{4,5},{5,6},{6,7},{7,0},{8,9},{9,10},{10,1... | collective-permute-start | bytes 884744 | tf_op jit(solution)/shard_map/ppermute | solution.py:355
  132.2 0.1 add.21
  132.2 5.1 %collective-permute-start.12 = (bf16[128,1152]{1,0:T(8,128)(2,1)S(1)}, bf16[128,1152]{1,0:T(8,128)(2,1)S(1)}, u32[]{:S(2)}, u32[]{:S(2)}) collective-permute-start(bf16[128,1152]{1,0:T(8,128)(2,1)S(1)} %add.21), channel_id=1, source_target_pairs={{0,7},{1,0},{2,1},{3,2},{4,3},{5,4},{6,5},{7,6},{8,15},{9,8},{10,9... | collective-permute-start | bytes 884744 | tf_op jit(solution)/shard_map/ppermute | solution.py:355
  137.4 0.0 collective-permute-done.9.refs_1_
  137.4 0.1 add.19
  137.5 1.9 %collective-permute-start.10 = (bf16[128,1152]{1,0:T(8,128)(2,1)S(1)}, bf16[128,1152]{1,0:T(8,128)(2,1)S(1)}, u32[]{:S(2)}, u32[]{:S(2)}) collective-permute-start(bf16[128,1152]{1,0:T(8,128)(2,1)S(1)} %add.19), channel_id=1, source_target_pairs={{0,1},{1,2},{2,3},{3,4},{4,5},{5,6},{6,7},{7,0},{8,9},{9,10},{10,1... | collective-permute-start | bytes 884744 | tf_op jit(solution)/shard_map/ppermute | solution.py:355
  139.5 0.1 add.17
  139.5 5.1 %collective-permute-start.7 = (bf16[128,1152]{1,0:T(8,128)(2,1)S(1)}, bf16[128,1152]{1,0:T(8,128)(2,1)S(1)}, u32[]{:S(2)}, u32[]{:S(2)}) collective-permute-start(bf16[128,1152]{1,0:T(8,128)(2,1)S(1)} %add.17), channel_id=1, source_target_pairs={{0,7},{1,0},{2,1},{3,2},{4,3},{5,4},{6,5},{7,6},{8,15},{9,8},{10,9... | collective-permute-start | bytes 884744 | tf_op jit(solution)/shard_map/ppermute | solution.py:355
  144.7 0.1 add.15
  144.8 2.1 %collective-permute-start.4 = (bf16[128,1152]{1,0:T(8,128)(2,1)S(1)}, bf16[128,1152]{1,0:T(8,128)(2,1)S(1)}, u32[]{:S(2)}, u32[]{:S(2)}) collective-permute-start(bf16[128,1152]{1,0:T(8,128)(2,1)S(1)} %add.15), channel_id=1, source_target_pairs={{0,1},{1,2},{2,3},{3,4},{4,5},{5,6},{6,7},{7,0},{8,9},{9,10},{10,1... | collective-permute-start | bytes 884744 | tf_op jit(solution)/shard_map/ppermute | solution.py:355
  146.8 0.0 collective-permute-done.12.refs_1_
  146.9 0.1 add.22
  146.9 5.1 %collective-permute-start.13 = (bf16[128,1152]{1,0:T(8,128)(2,1)S(1)}, bf16[128,1152]{1,0:T(8,128)(2,1)S(1)}, u32[]{:S(2)}, u32[]{:S(2)}) collective-permute-start(bf16[128,1152]{1,0:T(8,128)(2,1)S(1)} %add.22), channel_id=1, source_target_pairs={{0,7},{1,0},{2,1},{3,2},{4,3},{5,4},{6,5},{7,6},{8,15},{9,8},{10,9... | collective-permute-start | bytes 884744 | tf_op jit(solution)/shard_map/ppermute | solution.py:355
  152.1 0.0 collective-permute-done.10.refs_1_
  152.1 0.1 add.20
  152.2 2.5 %collective-permute-done.4.refs_1_ = bf16[128,1152]{1,0:T(8,128)(2,1)S(1)} collective-permute-done((bf16[128,1152]{1,0:T(8,128)(2,1)S(1)}, bf16[128,1152]{1,0:T(8,128)(2,1)S(1)}, u32[]{:S(2)}, u32[]{:S(2)}) %collective-permute-start.4) | collective-permute-done | bytes 294944 | tf_op jit(solution)/shard_map/ppermute | solution.py:355
  154.7 0.1 add.18
  154.9 3.9 %collective-permute-start.8 = (bf16[128,1152]{1,0:T(8,128)(2,1)S(1)}, bf16[128,1152]{1,0:T(8,128)(2,1)S(1)}, u32[]{:S(2)}, u32[]{:S(2)}) collective-permute-start(bf16[128,1152]{1,0:T(8,128)(2,1)S(1)} %add.18), channel_id=1, source_target_pairs={{0,8},{1,9},{2,10},{3,11},{4,12},{5,13},{6,14},{7,15},{8,0},{9,1},... | collective-permute-start | bytes 884744 | tf_op jit(solution)/shard_map/ppermute | solution.py:358
  158.8 1.9 %collective-permute-start.11 = (bf16[128,1152]{1,0:T(8,128)(2,1)S(1)}, bf16[128,1152]{1,0:T(8,128)(2,1)S(1)}, u32[]{:S(2)}, u32[]{:S(2)}) collective-permute-start(bf16[128,1152]{1,0:T(8,128)(2,1)S(1)} %add.20), channel_id=1, source_target_pairs={{0,1},{1,2},{2,3},{3,4},{4,5},{5,6},{6,7},{7,0},{8,9},{9,10},{10,1... | collective-permute-start | bytes 884744 | tf_op jit(solution)/shard_map/ppermute | solution.py:355
  160.7 0.0 collective-permute-done.13.refs_1_
  160.7 0.1 add.23
  160.8 5.1 %collective-permute-start.14 = (bf16[128,1152]{1,0:T(8,128)(2,1)S(1)}, bf16[128,1152]{1,0:T(8,128)(2,1)S(1)}, u32[]{:S(2)}, u32[]{:S(2)}) collective-permute-start(bf16[128,1152]{1,0:T(8,128)(2,1)S(1)} %add.23), channel_id=1, source_target_pairs={{0,7},{1,0},{2,1},{3,2},{4,3},{5,4},{6,5},{7,6},{8,15},{9,8},{10,9... | collective-permute-start | bytes 884744 | tf_op jit(solution)/shard_map/ppermute | solution.py:355
  165.9 0.0 all-to-all-done.1
  165.9 2.0 %combine.1 = (bf16[128,2048]{1,0:T(8,128)(2,1)}, bf16[1,128]{1,0:T(2,128)(2,1)}) custom-call(s32[1,128]{1,0:T(1,128)} %bitcast.24, s32[1,128]{1,0:T(1,128)} %bitcast.26, bf16[1,128]{1,0:T(2,128)(2,1)} %bitcast.28, bf16[512,1152]{1,0:T(8,128)(2,1)S(1)} %bitcast.17), custom_call_target="tpu_custom_call" | custom-call | tf_op jit(solution)/shard_map/combine/pallas_call | solution.py:279
  167.9 0.0 collective-permute-done.8.other_ref
  167.9 0.6 collective-permute-done.11.up_way_ref
  168.6 1.6 collective-permute-done.14.down_way_ref
  170.1 0.8 split_grads.1
  (31 shorter events, 0.1 us)
Async XLA Ops:
  3.8 61.6 %all-to-all-start = ((bf16[64,8,2048]{2,1,0:T(8,128)(2,1)}), bf16[64,8,2048]{2,1,0:T(8,128)(2,1)S(1)}, u32[]{:S(2)}, u32[]{:S(2)}) async-start(bf16[64,8,2048]{2,1,0:T(8,128)(2,1)} %bitcast.18), calls=%async_computation | async-start | bytes 4194304 | tf_op jit(solution)/shard_map/all_to_all | solution.py:373
  70.9 23.9 %collective-permute-start = (bf16[128,1152]{1,0:T(8,128)(2,1)}, bf16[128,1152]{1,0:T(8,128)(2,1)S(1)}, u32[]{:S(2)}, u32[]{:S(2)}) collective-permute-start(bf16[128,1152]{1,0:T(8,128)(2,1)} %get-tuple-element.45), channel_id=1, source_target_pairs={{0,1},{1,2},{2,3},{3,4},{4,5},{5,6},{6,7},{7,0},{8,9},{9,10},{10,1... | collective-permute-start | bytes 884744 | tf_op jit(solution)/shard_map/ppermute | solution.py:355
  76.1 20.4 %collective-permute-start.1 = (bf16[128,1152]{1,0:T(8,128)(2,1)}, bf16[128,1152]{1,0:T(8,128)(2,1)S(1)}, u32[]{:S(2)}, u32[]{:S(2)}) collective-permute-start(bf16[128,1152]{1,0:T(8,128)(2,1)} %get-tuple-element.46), channel_id=1, source_target_pairs={{0,7},{1,0},{2,1},{3,2},{4,3},{5,4},{6,5},{7,6},{8,15},{9,8},{10,9... | collective-permute-start | bytes 884744 | tf_op jit(solution)/shard_map/ppermute | solution.py:355
  94.8 16.5 %copy-start.13 = (bf16[128,1152]{1,0:T(8,128)(2,1)S(1)}, bf16[128,1152]{1,0:T(8,128)(2,1)}, u32[]{:S(2)}) copy-start(bf16[128,1152]{1,0:T(8,128)(2,1)} %get-tuple-element.55) | copy-start | bytes 884740
  94.9 22.2 %copy-start.9 = (bf16[128,1152]{1,0:T(8,128)(2,1)S(1)}, bf16[128,1152]{1,0:T(8,128)(2,1)}, u32[]{:S(2)}) copy-start(bf16[128,1152]{1,0:T(8,128)(2,1)} %get-tuple-element.52.refs_0_) | copy-start | bytes 884740
  96.5 22.6 %copy-start.12 = (bf16[128,1152]{1,0:T(8,128)(2,1)S(1)}, bf16[128,1152]{1,0:T(8,128)(2,1)}, u32[]{:S(2)}) copy-start(bf16[128,1152]{1,0:T(8,128)(2,1)} %get-tuple-element.61) | copy-start | bytes 884740
  96.5 27.1 %copy-start.8 = (bf16[128,1152]{1,0:T(8,128)(2,1)S(1)}, bf16[128,1152]{1,0:T(8,128)(2,1)}, u32[]{:S(2)}) copy-start(bf16[128,1152]{1,0:T(8,128)(2,1)} %get-tuple-element.54.refs_0_) | copy-start | bytes 884740
  96.5 33.7 %copy-start.7 = (bf16[128,1152]{1,0:T(8,128)(2,1)S(1)}, bf16[128,1152]{1,0:T(8,128)(2,1)}, u32[]{:S(2)}) copy-start(bf16[128,1152]{1,0:T(8,128)(2,1)} %get-tuple-element.51.refs_0_) | copy-start | bytes 884740
  96.5 69.5 %all-to-all-start.1 = ((bf16[64,8,1152]{2,1,0:T(8,128)(2,1)}), bf16[64,8,1152]{2,1,0:T(8,128)(2,1)S(1)}, u32[]{:S(2)}, u32[]{:S(2)}) async-start(bf16[64,8,1152]{2,1,0:T(8,128)(2,1)} %bitcast.22), calls=%async_computation.1 | async-start | bytes 2359296 | tf_op jit(solution)/shard_map/all_to_all | solution.py:386
  111.4 20.8 %copy-start.6 = (bf16[128,1152]{1,0:T(8,128)(2,1)S(1)}, bf16[128,1152]{1,0:T(8,128)(2,1)}, u32[]{:S(2)}) copy-start(bf16[128,1152]{1,0:T(8,128)(2,1)} %get-tuple-element.64.refs_0_) | copy-start | bytes 884740
  111.4 12.2 %collective-permute-start.5 = (bf16[128,1152]{1,0:T(8,128)(2,1)S(1)}, bf16[128,1152]{1,0:T(8,128)(2,1)S(1)}, u32[]{:S(2)}, u32[]{:S(2)}) collective-permute-start(bf16[128,1152]{1,0:T(8,128)(2,1)S(1)} %copy-done.13), channel_id=1, source_target_pairs={{0,7},{1,0},{2,1},{3,2},{4,3},{5,4},{6,5},{7,6},{8,15},{9,8},{10,9... | collective-permute-start | bytes 884744 | tf_op jit(solution)/shard_map/ppermute | solution.py:355
  117.0 20.3 %copy-start.5 = (bf16[128,1152]{1,0:T(8,128)(2,1)S(1)}, bf16[128,1152]{1,0:T(8,128)(2,1)}, u32[]{:S(2)}) copy-start(bf16[128,1152]{1,0:T(8,128)(2,1)} %get-tuple-element.60.refs_0_) | copy-start | bytes 884740
  117.1 13.0 %collective-permute-start.2 = (bf16[128,1152]{1,0:T(8,128)(2,1)S(1)}, bf16[128,1152]{1,0:T(8,128)(2,1)S(1)}, u32[]{:S(2)}, u32[]{:S(2)}) collective-permute-start(bf16[128,1152]{1,0:T(8,128)(2,1)S(1)} %add.13), channel_id=1, source_target_pairs={{0,1},{1,2},{2,3},{3,4},{4,5},{5,6},{6,7},{7,0},{8,9},{9,10},{10,1... | collective-permute-start | bytes 884744 | tf_op jit(solution)/shard_map/ppermute | solution.py:355
  119.1 18.3 %collective-permute-start.9 = (bf16[128,1152]{1,0:T(8,128)(2,1)S(1)}, bf16[128,1152]{1,0:T(8,128)(2,1)S(1)}, u32[]{:S(2)}, u32[]{:S(2)}) collective-permute-start(bf16[128,1152]{1,0:T(8,128)(2,1)S(1)} %copy-done.12), channel_id=1, source_target_pairs={{0,1},{1,2},{2,3},{3,4},{4,5},{5,6},{6,7},{7,0},{8,9},{9,10},{10,1... | collective-permute-start | bytes 884744 | tf_op jit(solution)/shard_map/ppermute | solution.py:355
  123.6 15.8 %copy-start.4 = (bf16[128,1152]{1,0:T(8,128)(2,1)S(1)}, bf16[128,1152]{1,0:T(8,128)(2,1)}, u32[]{:S(2)}) copy-start(bf16[128,1152]{1,0:T(8,128)(2,1)} %get-tuple-element.53.refs_0_) | copy-start | bytes 884740
  123.7 15.7 %collective-permute-start.6 = (bf16[128,1152]{1,0:T(8,128)(2,1)S(1)}, bf16[128,1152]{1,0:T(8,128)(2,1)S(1)}, u32[]{:S(2)}, u32[]{:S(2)}) collective-permute-start(bf16[128,1152]{1,0:T(8,128)(2,1)S(1)} %add.16), channel_id=1, source_target_pairs={{0,7},{1,0},{2,1},{3,2},{4,3},{5,4},{6,5},{7,6},{8,15},{9,8},{10,9... | collective-permute-start | bytes 884744 | tf_op jit(solution)/shard_map/ppermute | solution.py:355
  130.1 14.6 %copy-start.3 = (bf16[128,1152]{1,0:T(8,128)(2,1)S(1)}, bf16[128,1152]{1,0:T(8,128)(2,1)}, u32[]{:S(2)}) copy-start(bf16[128,1152]{1,0:T(8,128)(2,1)} %get-tuple-element.50.refs_0_) | copy-start | bytes 884740
  130.2 14.5 %collective-permute-start.3 = (bf16[128,1152]{1,0:T(8,128)(2,1)S(1)}, bf16[128,1152]{1,0:T(8,128)(2,1)S(1)}, u32[]{:S(2)}, u32[]{:S(2)}) collective-permute-start(bf16[128,1152]{1,0:T(8,128)(2,1)S(1)} %add.14), channel_id=1, source_target_pairs={{0,1},{1,2},{2,3},{3,4},{4,5},{5,6},{6,7},{7,0},{8,9},{9,10},{10,1... | collective-permute-start | bytes 884744 | tf_op jit(solution)/shard_map/ppermute | solution.py:355
  132.1 14.7 %copy-start.2 = (bf16[128,1152]{1,0:T(8,128)(2,1)S(1)}, bf16[128,1152]{1,0:T(8,128)(2,1)}, u32[]{:S(2)}) copy-start(bf16[128,1152]{1,0:T(8,128)(2,1)} %get-tuple-element.63.refs_0_) | copy-start | bytes 884740
  132.2 14.6 %collective-permute-start.12 = (bf16[128,1152]{1,0:T(8,128)(2,1)S(1)}, bf16[128,1152]{1,0:T(8,128)(2,1)S(1)}, u32[]{:S(2)}, u32[]{:S(2)}) collective-permute-start(bf16[128,1152]{1,0:T(8,128)(2,1)S(1)} %add.21), channel_id=1, source_target_pairs={{0,7},{1,0},{2,1},{3,2},{4,3},{5,4},{6,5},{7,6},{8,15},{9,8},{10,9... | collective-permute-start | bytes 884744 | tf_op jit(solution)/shard_map/ppermute | solution.py:355
  137.4 14.7 %copy-start.1 = (bf16[128,1152]{1,0:T(8,128)(2,1)S(1)}, bf16[128,1152]{1,0:T(8,128)(2,1)}, u32[]{:S(2)}) copy-start(bf16[128,1152]{1,0:T(8,128)(2,1)} %get-tuple-element.59.refs_0_) | copy-start | bytes 884740
  137.5 14.6 %collective-permute-start.10 = (bf16[128,1152]{1,0:T(8,128)(2,1)S(1)}, bf16[128,1152]{1,0:T(8,128)(2,1)S(1)}, u32[]{:S(2)}, u32[]{:S(2)}) collective-permute-start(bf16[128,1152]{1,0:T(8,128)(2,1)S(1)} %add.19), channel_id=1, source_target_pairs={{0,1},{1,2},{2,3},{3,4},{4,5},{5,6},{6,7},{7,0},{8,9},{9,10},{10,1... | collective-permute-start | bytes 884744 | tf_op jit(solution)/shard_map/ppermute | solution.py:355
  139.4 15.3 %copy-start.11 = (bf16[128,1152]{1,0:T(8,128)(2,1)S(1)}, bf16[128,1152]{1,0:T(8,128)(2,1)}, u32[]{:S(2)}) copy-start(bf16[128,1152]{1,0:T(8,128)(2,1)} %get-tuple-element.49.refs_0_) | copy-start | bytes 884740
  139.5 12.7 %collective-permute-start.7 = (bf16[128,1152]{1,0:T(8,128)(2,1)S(1)}, bf16[128,1152]{1,0:T(8,128)(2,1)S(1)}, u32[]{:S(2)}, u32[]{:S(2)}) collective-permute-start(bf16[128,1152]{1,0:T(8,128)(2,1)S(1)} %add.17), channel_id=1, source_target_pairs={{0,7},{1,0},{2,1},{3,2},{4,3},{5,4},{6,5},{7,6},{8,15},{9,8},{10,9... | collective-permute-start | bytes 884744 | tf_op jit(solution)/shard_map/ppermute | solution.py:355
  144.8 15.9 %copy-start = (bf16[128,1152]{1,0:T(8,128)(2,1)S(1)}, bf16[128,1152]{1,0:T(8,128)(2,1)}, u32[]{:S(2)}) copy-start(bf16[128,1152]{1,0:T(8,128)(2,1)} %get-tuple-element.62.refs_0_) | copy-start | bytes 884740
  144.8 10.0 %collective-permute-start.4 = (bf16[128,1152]{1,0:T(8,128)(2,1)S(1)}, bf16[128,1152]{1,0:T(8,128)(2,1)S(1)}, u32[]{:S(2)}, u32[]{:S(2)}) collective-permute-start(bf16[128,1152]{1,0:T(8,128)(2,1)S(1)} %add.15), channel_id=1, source_target_pairs={{0,1},{1,2},{2,3},{3,4},{4,5},{5,6},{6,7},{7,0},{8,9},{9,10},{10,1... | collective-permute-start | bytes 884744 | tf_op jit(solution)/shard_map/ppermute | solution.py:355
  146.9 13.7 %collective-permute-start.13 = (bf16[128,1152]{1,0:T(8,128)(2,1)S(1)}, bf16[128,1152]{1,0:T(8,128)(2,1)S(1)}, u32[]{:S(2)}, u32[]{:S(2)}) collective-permute-start(bf16[128,1152]{1,0:T(8,128)(2,1)S(1)} %add.22), channel_id=1, source_target_pairs={{0,7},{1,0},{2,1},{3,2},{4,3},{5,4},{6,5},{7,6},{8,15},{9,8},{10,9... | collective-permute-start | bytes 884744 | tf_op jit(solution)/shard_map/ppermute | solution.py:355
  154.7 15.4 %copy-start.10 = (bf16[128,1152]{1,0:T(8,128)(2,1)S(1)}, bf16[128,1152]{1,0:T(8,128)(2,1)}, u32[]{:S(2)}) copy-start(bf16[128,1152]{1,0:T(8,128)(2,1)} %get-tuple-element.58.own_ref) | copy-start | bytes 884740
  154.9 13.1 %collective-permute-start.8 = (bf16[128,1152]{1,0:T(8,128)(2,1)S(1)}, bf16[128,1152]{1,0:T(8,128)(2,1)S(1)}, u32[]{:S(2)}, u32[]{:S(2)}) collective-permute-start(bf16[128,1152]{1,0:T(8,128)(2,1)S(1)} %add.18), channel_id=1, source_target_pairs={{0,8},{1,9},{2,10},{3,11},{4,12},{5,13},{6,14},{7,15},{8,0},{9,1},... | collective-permute-start | bytes 884744 | tf_op jit(solution)/shard_map/ppermute | solution.py:358
  158.8 9.8 %collective-permute-start.11 = (bf16[128,1152]{1,0:T(8,128)(2,1)S(1)}, bf16[128,1152]{1,0:T(8,128)(2,1)S(1)}, u32[]{:S(2)}, u32[]{:S(2)}) collective-permute-start(bf16[128,1152]{1,0:T(8,128)(2,1)S(1)} %add.20), channel_id=1, source_target_pairs={{0,1},{1,2},{2,3},{3,4},{4,5},{5,6},{6,7},{7,0},{8,9},{9,10},{10,1... | collective-permute-start | bytes 884744 | tf_op jit(solution)/shard_map/ppermute | solution.py:355
  160.8 9.4 %collective-permute-start.14 = (bf16[128,1152]{1,0:T(8,128)(2,1)S(1)}, bf16[128,1152]{1,0:T(8,128)(2,1)S(1)}, u32[]{:S(2)}, u32[]{:S(2)}) collective-permute-start(bf16[128,1152]{1,0:T(8,128)(2,1)S(1)} %add.23), channel_id=1, source_target_pairs={{0,7},{1,0},{2,1},{3,2},{4,3},{5,4},{6,5},{7,6},{8,15},{9,8},{10,9... | collective-permute-start | bytes 884744 | tf_op jit(solution)/shard_map/ppermute | solution.py:355

commit v7 on v6

--- a/solution.py
+++ b/solution.py
@@ -343,18 +343,21 @@
         for way in (1, -1)
     }
     block = lambda ahead, piece: grads[ahead % ring, piece]
-    carried = {}
+    carried, first = {}, []
     for hop in range(far, 0, -1):
         for piece in range(2):
             for way in (1, -1):
                 if hop == far and piece != (0 if way == 1 else 1):
                     continue
                 own = block(way * hop, piece)
-                if (way, piece) in carried:
+                fresh = (way, piece) not in carried
+                if not fresh:
                     own = add(own, carried[way, piece])
                 carried[way, piece] = lax.ppermute(own, "dp", moves[way])
-        if hop == far:
-            back, *_ = lax.optimization_barrier((back, *carried.values()))
+                if fresh:
+                    first.append(carried[way, piece])
+        if hop == far - 1:
+            back, *_ = lax.optimization_barrier((back, *first))
     other = lax.ppermute(
         add(block(0, 0), carried[1, 0], carried[-1, 0]),
         "dp", [(i, (i + ring) % (2 * ring)) for i in range(2 * ring)],

time: 172 us -> 176 us (1.023)
  waiting for transfers between devices: 58.5 us -> 64.9 us
  starting transfers between devices: 94.2 us -> 92.2 us
    ppermute x14, waiting for transfers between devices: 9.79 us -> 16.2 us  [ring_sums(): carried[way, piece] = lax.ppermute(own, 'dp', moves[way])]
    ppermute x14, starting transfers between devices: 62.6 us -> 60.5 us  [ring_sums(): carried[way, piece] = lax.ppermute(own, 'dp', moves[way])]
    ppermute x1, starting transfers between devices: 3.89 us -> 5.77 us  [ring_sums(): lax.ppermute(add(block(0, 0), carried[1, 0], carried[-1, 0]), 'dp', [(i,...]
    all_to_all x1, starting transfers between devices: 14.9 us -> 13.1 us  [on_device(): lax.all_to_all(back.reshape(experts, 2 * capacity, back.shape[1]), 'exper...]
where the time goes in v7:
time: 176 us; the launch traced here: 175 us
  starting transfers between devices  92.2 us (52%)
  waiting for transfers between devices  64.9 us (37%)
  Pallas kernels  17.1 us (10%)
    ppermute x14, starting transfers between devices, ring_sums(): carried[way, piece] = lax.ppermute(own, 'dp', moves[way])  60.5 us
    all_to_all x1, waiting for transfers between devices, on_device(): lax.all_to_all(send.reshape(experts, 2 * capacity, features), 'expert', s...  48.7 us
    ppermute x14, waiting for transfers between devices, ring_sums(): carried[way, piece] = lax.ppermute(own, 'dp', moves[way])  16.2 us
    all_to_all x1, starting transfers between devices, on_device(): lax.all_to_all(back.reshape(experts, 2 * capacity, back.shape[1]), 'exper...  13.1 us
    all_to_all x1, starting transfers between devices, on_device(): lax.all_to_all(send.reshape(experts, 2 * capacity, features), 'expert', s...  12.8 us
    ppermute x1, starting transfers between devices, ring_sums(): lax.ppermute(add(block(0, 0), carried[1, 0], carried[-1, 0]), 'dp', [(i,...  5.77 us
    pallas_call x1, Pallas kernels, expert_first(): pl.pallas_call(functools.partial(expert_kernel, capacity, ring), in_specs...  5.54 us
    pallas_call x1, Pallas kernels, expert_late(): pl.pallas_call(functools.partial(late_kernel, capacity, ring), in_specs=[...  4.71 us
  transfers between devices with their start and end apart: 17, of which 7 were waited for; matrix products, arithmetic and copies ran while one was open for 0% of the time, Pallas kernels for 4%

profile of v7, /device:TPU:80, one launch (start us, length us, event | category | flops | bytes accessed | tf_op | source)
XLA Modules:
  0.0 175.5 jit_solution(14290367883807084768)
XLA Ops:
  0.6 3.2 %dispatch.1 = bf16[512,2048]{1,0:T(8,128)(2,1)} custom-call(s32[1,128]{1,0:T(1,128)} %bitcast.23, s32[1,128]{1,0:T(1,128)} %bitcast.25, bf16[1,128]{1,0:T(2,128)(2,1)} %bitcast.27, bf16[128,2048]{1,0:T(8,128)(2,1)} %tokens_hbm.1, bf16[128,2048]{1,0:T(8,128)(2,1)} %cotan_hbm.1), custom_call_target="tpu_custom_call" | custom-call | tf_op jit(solution)/shard_map/dispatch/pallas_call | solution.py:74
  3.8 12.8 %all-to-all-start = ((bf16[64,8,2048]{2,1,0:T(8,128)(2,1)}), bf16[64,8,2048]{2,1,0:T(8,128)(2,1)S(1)}, u32[]{:S(2)}, u32[]{:S(2)}) async-start(bf16[64,8,2048]{2,1,0:T(8,128)(2,1)} %bitcast.18), calls=%async_computation | async-start | bytes 4194304 | tf_op jit(solution)/shard_map/all_to_all | solution.py:376
  16.7 0.1 pad_add_fusion.place_ref
  16.7 48.7 %all-to-all-done = bf16[64,8,2048]{2,1,0:T(8,128)(2,1)S(1)} async-done(((bf16[64,8,2048]{2,1,0:T(8,128)(2,1)}), bf16[64,8,2048]{2,1,0:T(8,128)(2,1)S(1)}, u32[]{:S(2)}, u32[]{:S(2)}) %all-to-all-start) | async-done | bytes 2097184 | tf_op jit(solution)/shard_map/all_to_all | solution.py:376
  65.4 5.5 %expert_first.1 = (bf16[2048,384]{1,0:T(8,128)(2,1)S(1)}, bf16[2048,384]{1,0:T(8,128)(2,1)S(1)}, bf16[256,768]{1,0:T(8,128)(2,1)S(1)}, bf16[256,128]{1,0:T(8,128...) custom-call(s32[2]{0:T(128)S(1)} %pad_add_fusion.place_ref, ...), custom_call_target="tpu_custom_call" | custom-call | tf_op jit(solution)/shard_map/expert_first/pallas_call | solution.py:182
  71.0 5.1 %collective-permute-start = (bf16[128,1152]{1,0:T(8,128)(2,1)}, bf16[128,1152]{1,0:T(8,128)(2,1)S(1)}, u32[]{:S(2)}, u32[]{:S(2)}) collective-permute-start(bf16[128,1152]{1,0:T(8,128)(2,1)} %get-tuple-element.45), channel_id=1, source_target_pairs={{0,1},{1,2},{2,3},{3,4},{4,5},{5,6},{6,7},{7,0},{8,9},{9,10},{10,1... | collective-permute-start | bytes 884744 | tf_op jit(solution)/shard_map/ppermute | solution.py:356
  76.1 14.0 %collective-permute-start.1 = (bf16[128,1152]{1,0:T(8,128)(2,1)}, bf16[128,1152]{1,0:T(8,128)(2,1)S(1)}, u32[]{:S(2)}, u32[]{:S(2)}) collective-permute-start(bf16[128,1152]{1,0:T(8,128)(2,1)} %get-tuple-element.46), channel_id=1, source_target_pairs={{0,7},{1,0},{2,1},{3,2},{4,3},{5,4},{6,5},{7,6},{8,15},{9,8},{10,9... | collective-permute-start | bytes 884744 | tf_op jit(solution)/shard_map/ppermute | solution.py:356
  90.2 3.9 %collective-permute-start.2 = (bf16[128,1152]{1,0:T(8,128)(2,1)}, bf16[128,1152]{1,0:T(8,128)(2,1)S(1)}, u32[]{:S(2)}, u32[]{:S(2)}) collective-permute-start(bf16[128,1152]{1,0:T(8,128)(2,1)} %get-tuple-element.47), channel_id=1, source_target_pairs={{0,7},{1,0},{2,1},{3,2},{4,3},{5,4},{6,5},{7,6},{8,15},{9,8},{10,9... | collective-permute-start | bytes 884744 | tf_op jit(solution)/shard_map/ppermute | solution.py:356
  94.1 1.9 %collective-permute-start.3 = (bf16[128,1152]{1,0:T(8,128)(2,1)}, bf16[128,1152]{1,0:T(8,128)(2,1)S(1)}, u32[]{:S(2)}, u32[]{:S(2)}) collective-permute-start(bf16[128,1152]{1,0:T(8,128)(2,1)} %get-tuple-element.48), channel_id=1, source_target_pairs={{0,1},{1,2},{2,3},{3,4},{4,5},{5,6},{6,7},{7,0},{8,9},{9,10},{10,1... | collective-permute-start | bytes 884744 | tf_op jit(solution)/shard_map/ppermute | solution.py:356
  96.0 4.7 %expert_late.1 = (bf16[512,1152]{1,0:T(8,128)(2,1)}, bf16[128,1152]{1,0:T(8,128)(2,1)}, bf16[128,1152]{1,0:T(8,128)(2,1)}, bf16[128,1152]{1,0:T(8,128)(2,1)}, bf...) custom-call(s32[2]{0:T(128)S(1)} %pad_add_fusion.place_ref, ...), custom_call_target="tpu_custom_call" | custom-call | flops 2415919104 | bytes 8388608 | tf_op jit(solution)/shard_map/expert_late/pallas_call | solution.py:243
  100.7 0.0 collective-permute-done.refs_1_
  100.7 0.0 collective-permute-done.1.refs_1_
  100.8 2.0 %collective-permute-done.2.refs_1_ = bf16[128,1152]{1,0:T(8,128)(2,1)S(1)} collective-permute-done((bf16[128,1152]{1,0:T(8,128)(2,1)}, bf16[128,1152]{1,0:T(8,128)(2,1)S(1)}, u32[]{:S(2)}, u32[]{:S(2)}) %collective-permute-start.2) | collective-permute-done | bytes 294944 | tf_op jit(solution)/shard_map/ppermute | solution.py:356
  102.8 4.1 %collective-permute-done.3.refs_1_ = bf16[128,1152]{1,0:T(8,128)(2,1)S(1)} collective-permute-done((bf16[128,1152]{1,0:T(8,128)(2,1)}, bf16[128,1152]{1,0:T(8,128)(2,1)S(1)}, u32[]{:S(2)}, u32[]{:S(2)}) %collective-permute-start.3) | collective-permute-done | bytes 294944 | tf_op jit(solution)/shard_map/ppermute | solution.py:356
  106.8 13.1 %all-to-all-start.1 = ((bf16[64,8,1152]{2,1,0:T(8,128)(2,1)}), bf16[64,8,1152]{2,1,0:T(8,128)(2,1)S(1)}, u32[]{:S(2)}, u32[]{:S(2)}) async-start(bf16[64,8,1152]{2,1,0:T(8,128)(2,1)} %bitcast.22), calls=%async_computation.1 | async-start | bytes 2359296 | tf_op jit(solution)/shard_map/all_to_all | solution.py:389
  120.0 0.1 add.13
  120.1 2.1 %collective-permute-start.4 = (bf16[128,1152]{1,0:T(8,128)(2,1)S(1)}, bf16[128,1152]{1,0:T(8,128)(2,1)S(1)}, u32[]{:S(2)}, u32[]{:S(2)}) collective-permute-start(bf16[128,1152]{1,0:T(8,128)(2,1)S(1)} %add.13), channel_id=1, source_target_pairs={{0,1},{1,2},{2,3},{3,4},{4,5},{5,6},{6,7},{7,0},{8,9},{9,10},{10,1... | collective-permute-start | bytes 884744 | tf_op jit(solution)/shard_map/ppermute | solution.py:356
  122.1 0.1 add.16
  122.2 5.1 %collective-permute-start.7 = (bf16[128,1152]{1,0:T(8,128)(2,1)S(1)}, bf16[128,1152]{1,0:T(8,128)(2,1)S(1)}, u32[]{:S(2)}, u32[]{:S(2)}) collective-permute-start(bf16[128,1152]{1,0:T(8,128)(2,1)S(1)} %add.16), channel_id=1, source_target_pairs={{0,7},{1,0},{2,1},{3,2},{4,3},{5,4},{6,5},{7,6},{8,15},{9,8},{10,9... | collective-permute-start | bytes 884744 | tf_op jit(solution)/shard_map/ppermute | solution.py:356
  127.4 5.0 %collective-permute-done.4.refs_1_ = bf16[128,1152]{1,0:T(8,128)(2,1)S(1)} collective-permute-done((bf16[128,1152]{1,0:T(8,128)(2,1)S(1)}, bf16[128,1152]{1,0:T(8,128)(2,1)S(1)}, u32[]{:S(2)}, u32[]{:S(2)}) %collective-permute-start.4) | collective-permute-done | bytes 294944 | tf_op jit(solution)/shard_map/ppermute | solution.py:356
  132.4 0.1 add.14
  132.4 1.9 %collective-permute-start.5 = (bf16[128,1152]{1,0:T(8,128)(2,1)S(1)}, bf16[128,1152]{1,0:T(8,128)(2,1)S(1)}, u32[]{:S(2)}, u32[]{:S(2)}) collective-permute-start(bf16[128,1152]{1,0:T(8,128)(2,1)S(1)} %add.14), channel_id=1, source_target_pairs={{0,1},{1,2},{2,3},{3,4},{4,5},{5,6},{6,7},{7,0},{8,9},{9,10},{10,1... | collective-permute-start | bytes 884744 | tf_op jit(solution)/shard_map/ppermute | solution.py:356
  134.4 0.1 add.21
  134.5 5.1 %collective-permute-start.12 = (bf16[128,1152]{1,0:T(8,128)(2,1)S(1)}, bf16[128,1152]{1,0:T(8,128)(2,1)S(1)}, u32[]{:S(2)}, u32[]{:S(2)}) collective-permute-start(bf16[128,1152]{1,0:T(8,128)(2,1)S(1)} %add.21), channel_id=1, source_target_pairs={{0,7},{1,0},{2,1},{3,2},{4,3},{5,4},{6,5},{7,6},{8,15},{9,8},{10,9... | collective-permute-start | bytes 884744 | tf_op jit(solution)/shard_map/ppermute | solution.py:356
  139.6 0.1 add.19
  139.7 1.9 %collective-permute-start.10 = (bf16[128,1152]{1,0:T(8,128)(2,1)S(1)}, bf16[128,1152]{1,0:T(8,128)(2,1)S(1)}, u32[]{:S(2)}, u32[]{:S(2)}) collective-permute-start(bf16[128,1152]{1,0:T(8,128)(2,1)S(1)} %add.19), channel_id=1, source_target_pairs={{0,1},{1,2},{2,3},{3,4},{4,5},{5,6},{6,7},{7,0},{8,9},{9,10},{10,1... | collective-permute-start | bytes 884744 | tf_op jit(solution)/shard_map/ppermute | solution.py:356
  141.6 0.0 collective-permute-done.7.refs_1_
  141.7 0.1 add.17
  141.8 5.1 %collective-permute-start.8 = (bf16[128,1152]{1,0:T(8,128)(2,1)S(1)}, bf16[128,1152]{1,0:T(8,128)(2,1)S(1)}, u32[]{:S(2)}, u32[]{:S(2)}) collective-permute-start(bf16[128,1152]{1,0:T(8,128)(2,1)S(1)} %add.17), channel_id=1, source_target_pairs={{0,7},{1,0},{2,1},{3,2},{4,3},{5,4},{6,5},{7,6},{8,15},{9,8},{10,9... | collective-permute-start | bytes 884744 | tf_op jit(solution)/shard_map/ppermute | solution.py:356
  146.9 0.0 collective-permute-done.5.refs_1_
  146.9 0.1 add.15
  147.0 2.1 %collective-permute-start.6 = (bf16[128,1152]{1,0:T(8,128)(2,1)S(1)}, bf16[128,1152]{1,0:T(8,128)(2,1)S(1)}, u32[]{:S(2)}, u32[]{:S(2)}) collective-permute-start(bf16[128,1152]{1,0:T(8,128)(2,1)S(1)} %add.15), channel_id=1, source_target_pairs={{0,1},{1,2},{2,3},{3,4},{4,5},{5,6},{6,7},{7,0},{8,9},{9,10},{10,1... | collective-permute-start | bytes 884744 | tf_op jit(solution)/shard_map/ppermute | solution.py:356
  149.1 0.0 collective-permute-done.12.refs_1_
  149.1 0.1 add.22
  149.2 5.1 %collective-permute-start.13 = (bf16[128,1152]{1,0:T(8,128)(2,1)S(1)}, bf16[128,1152]{1,0:T(8,128)(2,1)S(1)}, u32[]{:S(2)}, u32[]{:S(2)}) collective-permute-start(bf16[128,1152]{1,0:T(8,128)(2,1)S(1)} %add.22), channel_id=1, source_target_pairs={{0,7},{1,0},{2,1},{3,2},{4,3},{5,4},{6,5},{7,6},{8,15},{9,8},{10,9... | collective-permute-start | bytes 884744 | tf_op jit(solution)/shard_map/ppermute | solution.py:356
  154.3 0.0 collective-permute-done.10.refs_1_
  154.3 0.1 add.20
  154.4 2.9 %collective-permute-done.6.refs_1_ = bf16[128,1152]{1,0:T(8,128)(2,1)S(1)} collective-permute-done((bf16[128,1152]{1,0:T(8,128)(2,1)S(1)}, bf16[128,1152]{1,0:T(8,128)(2,1)S(1)}, u32[]{:S(2)}, u32[]{:S(2)}) %collective-permute-start.6) | collective-permute-done | bytes 294944 | tf_op jit(solution)/shard_map/ppermute | solution.py:356
  157.4 0.1 add.18
  157.5 5.8 %collective-permute-start.9 = (bf16[128,1152]{1,0:T(8,128)(2,1)S(1)}, bf16[128,1152]{1,0:T(8,128)(2,1)S(1)}, u32[]{:S(2)}, u32[]{:S(2)}) collective-permute-start(bf16[128,1152]{1,0:T(8,128)(2,1)S(1)} %add.18), channel_id=1, source_target_pairs={{0,8},{1,9},{2,10},{3,11},{4,12},{5,13},{6,14},{7,15},{8,0},{9,1},... | collective-permute-start | bytes 884744 | tf_op jit(solution)/shard_map/ppermute | solution.py:361
  163.2 1.9 %collective-permute-start.11 = (bf16[128,1152]{1,0:T(8,128)(2,1)S(1)}, bf16[128,1152]{1,0:T(8,128)(2,1)S(1)}, u32[]{:S(2)}, u32[]{:S(2)}) collective-permute-start(bf16[128,1152]{1,0:T(8,128)(2,1)S(1)} %add.20), channel_id=1, source_target_pairs={{0,1},{1,2},{2,3},{3,4},{4,5},{5,6},{6,7},{7,0},{8,9},{9,10},{10,1... | collective-permute-start | bytes 884744 | tf_op jit(solution)/shard_map/ppermute | solution.py:356
  165.2 0.1 add.23
  165.3 5.1 %collective-permute-start.14 = (bf16[128,1152]{1,0:T(8,128)(2,1)S(1)}, bf16[128,1152]{1,0:T(8,128)(2,1)S(1)}, u32[]{:S(2)}, u32[]{:S(2)}) collective-permute-start(bf16[128,1152]{1,0:T(8,128)(2,1)S(1)} %add.23), channel_id=1, source_target_pairs={{0,7},{1,0},{2,1},{3,2},{4,3},{5,4},{6,5},{7,6},{8,15},{9,8},{10,9... | collective-permute-start | bytes 884744 | tf_op jit(solution)/shard_map/ppermute | solution.py:356
  170.4 2.0 %combine.1 = (bf16[128,2048]{1,0:T(8,128)(2,1)}, bf16[1,128]{1,0:T(2,128)(2,1)}) custom-call(s32[1,128]{1,0:T(1,128)} %bitcast.24, s32[1,128]{1,0:T(1,128)} %bitcast.26, bf16[1,128]{1,0:T(2,128)(2,1)} %bitcast.28, bf16[512,1152]{1,0:T(8,128)(2,1)S(1)} %bitcast.17), custom_call_target="tpu_custom_call" | custom-call | tf_op jit(solution)/shard_map/combine/pallas_call | solution.py:279
  172.4 0.0 collective-permute-done.9.other_ref
  172.4 0.6 collective-permute-done.11.up_way_ref
  173.1 1.6 collective-permute-done.14.down_way_ref
  174.6 0.8 split_grads.1
  (27 shorter events, 0.1 us)
Async XLA Ops:
  3.8 61.6 %all-to-all-start = ((bf16[64,8,2048]{2,1,0:T(8,128)(2,1)}), bf16[64,8,2048]{2,1,0:T(8,128)(2,1)S(1)}, u32[]{:S(2)}, u32[]{:S(2)}) async-start(bf16[64,8,2048]{2,1,0:T(8,128)(2,1)} %bitcast.18), calls=%async_computation | async-start | bytes 4194304 | tf_op jit(solution)/shard_map/all_to_all | solution.py:376
  71.0 29.8 %collective-permute-start = (bf16[128,1152]{1,0:T(8,128)(2,1)}, bf16[128,1152]{1,0:T(8,128)(2,1)S(1)}, u32[]{:S(2)}, u32[]{:S(2)}) collective-permute-start(bf16[128,1152]{1,0:T(8,128)(2,1)} %get-tuple-element.45), channel_id=1, source_target_pairs={{0,1},{1,2},{2,3},{3,4},{4,5},{5,6},{6,7},{7,0},{8,9},{9,10},{10,1... | collective-permute-start | bytes 884744 | tf_op jit(solution)/shard_map/ppermute | solution.py:356
  76.1 24.6 %collective-permute-start.1 = (bf16[128,1152]{1,0:T(8,128)(2,1)}, bf16[128,1152]{1,0:T(8,128)(2,1)S(1)}, u32[]{:S(2)}, u32[]{:S(2)}) collective-permute-start(bf16[128,1152]{1,0:T(8,128)(2,1)} %get-tuple-element.46), channel_id=1, source_target_pairs={{0,7},{1,0},{2,1},{3,2},{4,3},{5,4},{6,5},{7,6},{8,15},{9,8},{10,9... | collective-permute-start | bytes 884744 | tf_op jit(solution)/shard_map/ppermute | solution.py:356
  90.2 12.6 %collective-permute-start.2 = (bf16[128,1152]{1,0:T(8,128)(2,1)}, bf16[128,1152]{1,0:T(8,128)(2,1)S(1)}, u32[]{:S(2)}, u32[]{:S(2)}) collective-permute-start(bf16[128,1152]{1,0:T(8,128)(2,1)} %get-tuple-element.47), channel_id=1, source_target_pairs={{0,7},{1,0},{2,1},{3,2},{4,3},{5,4},{6,5},{7,6},{8,15},{9,8},{10,9... | collective-permute-start | bytes 884744 | tf_op jit(solution)/shard_map/ppermute | solution.py:356
  94.1 12.8 %collective-permute-start.3 = (bf16[128,1152]{1,0:T(8,128)(2,1)}, bf16[128,1152]{1,0:T(8,128)(2,1)S(1)}, u32[]{:S(2)}, u32[]{:S(2)}) collective-permute-start(bf16[128,1152]{1,0:T(8,128)(2,1)} %get-tuple-element.48), channel_id=1, source_target_pairs={{0,1},{1,2},{2,3},{3,4},{4,5},{5,6},{6,7},{7,0},{8,9},{9,10},{10,1... | collective-permute-start | bytes 884744 | tf_op jit(solution)/shard_map/ppermute | solution.py:356
  100.7 19.2 %copy-start.9 = (bf16[128,1152]{1,0:T(8,128)(2,1)S(1)}, bf16[128,1152]{1,0:T(8,128)(2,1)}, u32[]{:S(2)}) copy-start(bf16[128,1152]{1,0:T(8,128)(2,1)} %get-tuple-element.54.refs_0_) | copy-start | bytes 884740
  106.8 15.3 %copy-start.8 = (bf16[128,1152]{1,0:T(8,128)(2,1)S(1)}, bf16[128,1152]{1,0:T(8,128)(2,1)}, u32[]{:S(2)}) copy-start(bf16[128,1152]{1,0:T(8,128)(2,1)} %get-tuple-element.56.refs_0_) | copy-start | bytes 884740
  106.8 25.5 %copy-start.7 = (bf16[128,1152]{1,0:T(8,128)(2,1)S(1)}, bf16[128,1152]{1,0:T(8,128)(2,1)}, u32[]{:S(2)}) copy-start(bf16[128,1152]{1,0:T(8,128)(2,1)} %get-tuple-element.53.refs_0_) | copy-start | bytes 884740
  106.8 63.6 %all-to-all-start.1 = ((bf16[64,8,1152]{2,1,0:T(8,128)(2,1)}), bf16[64,8,1152]{2,1,0:T(8,128)(2,1)S(1)}, u32[]{:S(2)}, u32[]{:S(2)}) async-start(bf16[64,8,1152]{2,1,0:T(8,128)(2,1)} %bitcast.22), calls=%async_computation.1 | async-start | bytes 2359296 | tf_op jit(solution)/shard_map/all_to_all | solution.py:389
  120.0 14.4 %copy-start.6 = (bf16[128,1152]{1,0:T(8,128)(2,1)S(1)}, bf16[128,1152]{1,0:T(8,128)(2,1)}, u32[]{:S(2)}) copy-start(bf16[128,1152]{1,0:T(8,128)(2,1)} %get-tuple-element.64.refs_0_) | copy-start | bytes 884740
  120.0 19.6 %copy-start.5 = (bf16[128,1152]{1,0:T(8,128)(2,1)S(1)}, bf16[128,1152]{1,0:T(8,128)(2,1)}, u32[]{:S(2)}) copy-start(bf16[128,1152]{1,0:T(8,128)(2,1)} %get-tuple-element.61.refs_0_) | copy-start | bytes 884740
  120.1 12.3 %collective-permute-start.4 = (bf16[128,1152]{1,0:T(8,128)(2,1)S(1)}, bf16[128,1152]{1,0:T(8,128)(2,1)S(1)}, u32[]{:S(2)}, u32[]{:S(2)}) collective-permute-start(bf16[128,1152]{1,0:T(8,128)(2,1)S(1)} %add.13), channel_id=1, source_target_pairs={{0,1},{1,2},{2,3},{3,4},{4,5},{5,6},{6,7},{7,0},{8,9},{9,10},{10,1... | collective-permute-start | bytes 884744 | tf_op jit(solution)/shard_map/ppermute | solution.py:356
  122.1 19.5 %copy-start.4 = (bf16[128,1152]{1,0:T(8,128)(2,1)S(1)}, bf16[128,1152]{1,0:T(8,128)(2,1)}, u32[]{:S(2)}) copy-start(bf16[128,1152]{1,0:T(8,128)(2,1)} %get-tuple-element.55.refs_0_) | copy-start | bytes 884740
  122.2 19.4 %collective-permute-start.7 = (bf16[128,1152]{1,0:T(8,128)(2,1)S(1)}, bf16[128,1152]{1,0:T(8,128)(2,1)S(1)}, u32[]{:S(2)}, u32[]{:S(2)}) collective-permute-start(bf16[128,1152]{1,0:T(8,128)(2,1)S(1)} %add.16), channel_id=1, source_target_pairs={{0,7},{1,0},{2,1},{3,2},{4,3},{5,4},{6,5},{7,6},{8,15},{9,8},{10,9... | collective-permute-start | bytes 884744 | tf_op jit(solution)/shard_map/ppermute | solution.py:356
  132.4 14.5 %copy-start.3 = (bf16[128,1152]{1,0:T(8,128)(2,1)S(1)}, bf16[128,1152]{1,0:T(8,128)(2,1)}, u32[]{:S(2)}) copy-start(bf16[128,1152]{1,0:T(8,128)(2,1)} %get-tuple-element.52.refs_0_) | copy-start | bytes 884740
  132.4 14.5 %collective-permute-start.5 = (bf16[128,1152]{1,0:T(8,128)(2,1)S(1)}, bf16[128,1152]{1,0:T(8,128)(2,1)S(1)}, u32[]{:S(2)}, u32[]{:S(2)}) collective-permute-start(bf16[128,1152]{1,0:T(8,128)(2,1)S(1)} %add.14), channel_id=1, source_target_pairs={{0,1},{1,2},{2,3},{3,4},{4,5},{5,6},{6,7},{7,0},{8,9},{9,10},{10,1... | collective-permute-start | bytes 884744 | tf_op jit(solution)/shard_map/ppermute | solution.py:356
  134.4 14.7 %copy-start.2 = (bf16[128,1152]{1,0:T(8,128)(2,1)S(1)}, bf16[128,1152]{1,0:T(8,128)(2,1)}, u32[]{:S(2)}) copy-start(bf16[128,1152]{1,0:T(8,128)(2,1)} %get-tuple-element.63.refs_0_) | copy-start | bytes 884740
  134.5 14.6 %collective-permute-start.12 = (bf16[128,1152]{1,0:T(8,128)(2,1)S(1)}, bf16[128,1152]{1,0:T(8,128)(2,1)S(1)}, u32[]{:S(2)}, u32[]{:S(2)}) collective-permute-start(bf16[128,1152]{1,0:T(8,128)(2,1)S(1)} %add.21), channel_id=1, source_target_pairs={{0,7},{1,0},{2,1},{3,2},{4,3},{5,4},{6,5},{7,6},{8,15},{9,8},{10,9... | collective-permute-start | bytes 884744 | tf_op jit(solution)/shard_map/ppermute | solution.py:356
  139.6 14.7 %copy-start.1 = (bf16[128,1152]{1,0:T(8,128)(2,1)S(1)}, bf16[128,1152]{1,0:T(8,128)(2,1)}, u32[]{:S(2)}) copy-start(bf16[128,1152]{1,0:T(8,128)(2,1)} %get-tuple-element.60.refs_0_) | copy-start | bytes 884740
  139.7 14.6 %collective-permute-start.10 = (bf16[128,1152]{1,0:T(8,128)(2,1)S(1)}, bf16[128,1152]{1,0:T(8,128)(2,1)S(1)}, u32[]{:S(2)}, u32[]{:S(2)}) collective-permute-start(bf16[128,1152]{1,0:T(8,128)(2,1)S(1)} %add.19), channel_id=1, source_target_pairs={{0,1},{1,2},{2,3},{3,4},{4,5},{5,6},{6,7},{7,0},{8,9},{9,10},{10,1... | collective-permute-start | bytes 884744 | tf_op jit(solution)/shard_map/ppermute | solution.py:356
  141.7 15.7 %copy-start.11 = (bf16[128,1152]{1,0:T(8,128)(2,1)S(1)}, bf16[128,1152]{1,0:T(8,128)(2,1)}, u32[]{:S(2)}) copy-start(bf16[128,1152]{1,0:T(8,128)(2,1)} %get-tuple-element.51.refs_0_) | copy-start | bytes 884740
  141.8 12.7 %collective-permute-start.8 = (bf16[128,1152]{1,0:T(8,128)(2,1)S(1)}, bf16[128,1152]{1,0:T(8,128)(2,1)S(1)}, u32[]{:S(2)}, u32[]{:S(2)}) collective-permute-start(bf16[128,1152]{1,0:T(8,128)(2,1)S(1)} %add.17), channel_id=1, source_target_pairs={{0,7},{1,0},{2,1},{3,2},{4,3},{5,4},{6,5},{7,6},{8,15},{9,8},{10,9... | collective-permute-start | bytes 884744 | tf_op jit(solution)/shard_map/ppermute | solution.py:356
  147.0 18.2 %copy-start = (bf16[128,1152]{1,0:T(8,128)(2,1)S(1)}, bf16[128,1152]{1,0:T(8,128)(2,1)}, u32[]{:S(2)}) copy-start(bf16[128,1152]{1,0:T(8,128)(2,1)} %get-tuple-element.62.refs_0_) | copy-start | bytes 884740
  147.0 10.3 %collective-permute-start.6 = (bf16[128,1152]{1,0:T(8,128)(2,1)S(1)}, bf16[128,1152]{1,0:T(8,128)(2,1)S(1)}, u32[]{:S(2)}, u32[]{:S(2)}) collective-permute-start(bf16[128,1152]{1,0:T(8,128)(2,1)S(1)} %add.15), channel_id=1, source_target_pairs={{0,1},{1,2},{2,3},{3,4},{4,5},{5,6},{6,7},{7,0},{8,9},{9,10},{10,1... | collective-permute-start | bytes 884744 | tf_op jit(solution)/shard_map/ppermute | solution.py:356
  149.2 16.0 %collective-permute-start.13 = (bf16[128,1152]{1,0:T(8,128)(2,1)S(1)}, bf16[128,1152]{1,0:T(8,128)(2,1)S(1)}, u32[]{:S(2)}, u32[]{:S(2)}) collective-permute-start(bf16[128,1152]{1,0:T(8,128)(2,1)S(1)} %add.22), channel_id=1, source_target_pairs={{0,7},{1,0},{2,1},{3,2},{4,3},{5,4},{6,5},{7,6},{8,15},{9,8},{10,9... | collective-permute-start | bytes 884744 | tf_op jit(solution)/shard_map/ppermute | solution.py:356
  157.4 17.3 %copy-start.10 = (bf16[128,1152]{1,0:T(8,128)(2,1)S(1)}, bf16[128,1152]{1,0:T(8,128)(2,1)}, u32[]{:S(2)}) copy-start(bf16[128,1152]{1,0:T(8,128)(2,1)} %get-tuple-element.59.own_ref) | copy-start | bytes 884740
  157.5 15.0 %collective-permute-start.9 = (bf16[128,1152]{1,0:T(8,128)(2,1)S(1)}, bf16[128,1152]{1,0:T(8,128)(2,1)S(1)}, u32[]{:S(2)}, u32[]{:S(2)}) collective-permute-start(bf16[128,1152]{1,0:T(8,128)(2,1)S(1)} %add.18), channel_id=1, source_target_pairs={{0,8},{1,9},{2,10},{3,11},{4,12},{5,13},{6,14},{7,15},{8,0},{9,1},... | collective-permute-start | bytes 884744 | tf_op jit(solution)/shard_map/ppermute | solution.py:361
  163.2 9.8 %collective-permute-start.11 = (bf16[128,1152]{1,0:T(8,128)(2,1)S(1)}, bf16[128,1152]{1,0:T(8,128)(2,1)S(1)}, u32[]{:S(2)}, u32[]{:S(2)}) collective-permute-start(bf16[128,1152]{1,0:T(8,128)(2,1)S(1)} %add.20), channel_id=1, source_target_pairs={{0,1},{1,2},{2,3},{3,4},{4,5},{5,6},{6,7},{7,0},{8,9},{9,10},{10,1... | collective-permute-start | bytes 884744 | tf_op jit(solution)/shard_map/ppermute | solution.py:356
  165.3 9.4 %collective-permute-start.14 = (bf16[128,1152]{1,0:T(8,128)(2,1)S(1)}, bf16[128,1152]{1,0:T(8,128)(2,1)S(1)}, u32[]{:S(2)}, u32[]{:S(2)}) collective-permute-start(bf16[128,1152]{1,0:T(8,128)(2,1)S(1)} %add.23), channel_id=1, source_target_pairs={{0,7},{1,0},{2,1},{3,2},{4,3},{5,4},{6,5},{7,6},{8,15},{9,8},{10,9... | collective-permute-start | bytes 884744 | tf_op jit(solution)/shard_map/ppermute | solution.py:356

commit v8 on v6

--- a/solution.py
+++ b/solution.py
@@ -133,10 +133,11 @@
 
 def expert_kernel(
     capacity, ring, place_ref, recv_ref, gate_hbm, up_hbm, down_hbm,
-    gate_ref, up_ref, inner_ref, score_ref, inputs, scaled, hidden_ref, *rest,
+    inner_ref, inputs, scaled, hidden_ref, back_hbm, *rest,
 ):
     blocks = early_blocks(ring)
-    grads, (down_ref, stage, sems, out_sems) = rest[: len(blocks)], rest[len(blocks) :]
+    grads, scratch = rest[: len(blocks)], rest[len(blocks) :]
+    gate_ref, up_ref, down_ref, stage, back, sems, out_sems = scratch
     rows, features = recv_ref.shape
     slots = rows // 2
     hidden_size = gate_ref.shape[1]
@@ -166,57 +167,11 @@
     ).astype(BF16)
     inner_ref[:, hidden_size:] = (hidden_grad * activated).astype(BF16)
     score = jnp.sum(hidden.astype(F32) * hidden_grad, axis=1, keepdims=True)
-    score_ref[...] = jnp.broadcast_to(score, score_ref.shape).astype(BF16)
-    for write in write_blocks(
-        blocks, ring, place_ref, inputs, scaled, inner_ref, hidden_ref, stage, grads, out_sems
-    ):
-        write.wait()
-
-
-def expert_first(place, ring, received, gate, up, down, capacity):
-    rows, features = received.shape
-    hidden_size = gate.shape[1]
-    slots = rows // 2
-    block = (features // (2 * ring), 3 * hidden_size)
-    count = len(early_blocks(ring))
-    return pl.pallas_call(
-        functools.partial(expert_kernel, capacity, ring),
-        in_specs=[pl.BlockSpec(memory_space=pltpu.SMEM), ON_CHIP, ANYWHERE, ANYWHERE, ANYWHERE],
-        out_specs=[ON_CHIP] * 7 + [ANYWHERE] * count,
-        out_shape=[
-            pltpu.VMEM(gate.shape, BF16),
-            pltpu.VMEM(up.shape, BF16),
-            pltpu.VMEM((slots, 2 * hidden_size), BF16),
-            pltpu.VMEM((slots, LANES), BF16),
-            pltpu.VMEM((slots, features), BF16),
-            pltpu.VMEM((slots, features), BF16),
-            pltpu.VMEM((slots, hidden_size), BF16),
-        ]
-        + [pltpu.HBM(block, BF16)] * count,
-        scratch_shapes=[
-            pltpu.VMEM(down.shape, BF16),
-            pltpu.VMEM((count, *block), BF16),
-            pltpu.SemaphoreType.DMA((3,)),
-            pltpu.SemaphoreType.DMA((count,)),
-        ],
-        compiler_params=pltpu.CompilerParams(vmem_limit_bytes=24 * 2**20),
-        name="expert_first",
-    )(place, *on_chip(received), *in_hbm(gate, up, down))
-
-
-def late_kernel(
-    capacity, ring, place_ref, gate_ref, up_ref, inner_ref, score_ref, inputs, scaled, hidden_ref,
-    back_hbm, *rest,
-):
-    blocks = late_blocks(ring)
-    grads, (stage, back, out_sems) = rest[: len(blocks)], rest[len(blocks) :]
-    slots = inner_ref.shape[0]
-    rows = back.shape[0]
-    hidden_size = gate_ref.shape[1]
-    half = gate_ref.shape[0] // 2
+    score = jnp.broadcast_to(score, (slots, LANES)).astype(BF16)
     writes = write_blocks(
         blocks, ring, place_ref, inputs, scaled, inner_ref, hidden_ref, stage, grads, out_sems
     )
+    half = features // 2
     total = jnp.zeros((rows, half), F32)
     for part in range(2):
         piece = pl.ds(part * half, half)
@@ -226,7 +181,7 @@
         spread = pick_rows(slots, rows, capacity, part)
         total += dot(spread, input_grad.astype(BF16), 0, 0)
         if part == 0:
-            back[:, half:] = dot(spread, score_ref[...], 0, 0).astype(BF16)
+            back[:, half:] = dot(spread, score, 0, 0).astype(BF16)
     back[:, :half] = total.astype(BF16)
     writes.append(pltpu.make_async_copy(back, back_hbm, out_sems.at[len(blocks)]))
     writes[-1].start()
@@ -234,28 +189,68 @@
         write.wait()
 
 
-def expert_late(place, ring, gate, up, inner, score, inputs, scaled, hidden, capacity):
-    slots, features = inputs.shape
+def expert_first(place, ring, received, gate, up, down, capacity):
+    rows, features = received.shape
     hidden_size = gate.shape[1]
+    slots = rows // 2
     block = (features // (2 * ring), 3 * hidden_size)
-    count = len(late_blocks(ring))
-    back = (2 * slots, features // 2 + LANES)
-    return pl.pallas_call(
-        functools.partial(late_kernel, capacity, ring),
-        in_specs=[pl.BlockSpec(memory_space=pltpu.SMEM)] + [ON_CHIP] * 7,
-        out_specs=[ANYWHERE] * (1 + count),
-        out_shape=[pltpu.HBM(back, BF16)] + [pltpu.HBM(block, BF16)] * count,
+    count = len(early_blocks(ring))
+    back = (rows, features // 2 + LANES)
+    return pl.pallas_call(
+        functools.partial(expert_kernel, capacity, ring),
+        in_specs=[pl.BlockSpec(memory_space=pltpu.SMEM), ON_CHIP, ANYWHERE, ANYWHERE, ANYWHERE],
+        out_specs=[ON_CHIP] * 4 + [ANYWHERE] * (1 + count),
+        out_shape=[
+            pltpu.VMEM((slots, 2 * hidden_size), BF16),
+            pltpu.VMEM((slots, features), BF16),
+            pltpu.VMEM((slots, features), BF16),
+            pltpu.VMEM((slots, hidden_size), BF16),
+            pltpu.HBM(back, BF16),
+        ]
+        + [pltpu.HBM(block, BF16)] * count,
         scratch_shapes=[
+            pltpu.VMEM(gate.shape, BF16),
+            pltpu.VMEM(up.shape, BF16),
+            pltpu.VMEM(down.shape, BF16),
             pltpu.VMEM((count, *block), BF16),
             pltpu.VMEM(back, BF16),
+            pltpu.SemaphoreType.DMA((3,)),
             pltpu.SemaphoreType.DMA((count + 1,)),
         ],
         compiler_params=pltpu.CompilerParams(vmem_limit_bytes=24 * 2**20),
-        cost_estimate=pl.CostEstimate(
-            flops=2 * slots * features * 6 * hidden_size, bytes_accessed=2**23, transcendentals=0
-        ),
+        name="expert_first",
+    )(place, *on_chip(received), *in_hbm(gate, up, down))
+
+
+def late_kernel(
+    ring, place_ref, inner_ref, inputs, scaled, hidden_ref, *rest
+):
+    blocks = late_blocks(ring)
+    grads, (stage, out_sems) = rest[: len(blocks)], rest[len(blocks) :]
+    writes = write_blocks(
+        blocks, ring, place_ref, inputs, scaled, inner_ref, hidden_ref, stage, grads, out_sems
+    )
+    for write in writes:
+        write.wait()
+
+
+def expert_late(place, ring, inner, inputs, scaled, hidden):
+    slots, features = inputs.shape
+    hidden_size = hidden.shape[1]
+    block = (features // (2 * ring), 3 * hidden_size)
+    count = len(late_blocks(ring))
+    return pl.pallas_call(
+        functools.partial(late_kernel, ring),
+        in_specs=[pl.BlockSpec(memory_space=pltpu.SMEM)] + [ON_CHIP] * 4,
+        out_specs=[ANYWHERE] * count,
+        out_shape=[pltpu.HBM(block, BF16)] * count,
+        scratch_shapes=[
+            pltpu.VMEM((count, *block), BF16),
+            pltpu.SemaphoreType.DMA((count,)),
+        ],
+        compiler_params=pltpu.CompilerParams(vmem_limit_bytes=16 * 2**20),
         name="expert_late",
-    )(place, *on_chip(gate, up, inner, score, inputs, scaled, hidden))
+    )(place, *on_chip(inner, inputs, scaled, hidden))
 
 
 def combine_kernel(capacity, ids_ref, slot_ref, score_ref, rows_ref, token_ref, grad_ref):
@@ -336,7 +331,7 @@
     )(*on_chip(*parts))
 
 
-def ring_sums(grads, ring, back):
+def ring_sums(grads, ring):
     far = ring // 2
     moves = {
         way: [(s * ring + i, s * ring + (i + way) % ring) for s in range(2) for i in range(ring)]
@@ -353,13 +348,11 @@
                 if (way, piece) in carried:
                     own = add(own, carried[way, piece])
                 carried[way, piece] = lax.ppermute(own, "dp", moves[way])
-        if hop == far:
-            back, *_ = lax.optimization_barrier((back, *carried.values()))
     other = lax.ppermute(
         add(block(0, 0), carried[1, 0], carried[-1, 0]),
         "dp", [(i, (i + ring) % (2 * ring)) for i in range(2 * ring)],
     )
-    return back, block(0, 1), carried[1, 1], carried[-1, 1], other
+    return block(0, 1), carried[1, 1], carried[-1, 1], other
 
 
 def on_device(
@@ -378,11 +371,10 @@
     index = lax.axis_index("dp")
     side = (index >= ring).astype(jnp.int32)
     place = jnp.stack([side, index - side * ring])
-    held = expert_first(place, ring, received, gate, up, down, capacity)
-    held, early = held[:7], held[7:]
-    back, *late = expert_late(place, ring, *held, capacity)
-    grads = dict(zip(early_blocks(ring) + late_blocks(ring), [*early, *late]))
-    back, *parts, other = ring_sums(grads, ring, back)
+    *held, back, f0, f1, f2, f3 = expert_first(place, ring, received, gate, up, down, capacity)
+    late = expert_late(place, ring, *held)
+    grads = dict(zip(early_blocks(ring) + late_blocks(ring), [f0, f1, f2, f3, *late]))
+    *parts, other = ring_sums(grads, ring)
     returned = lax.all_to_all(
         back.reshape(experts, 2 * capacity, back.shape[1]),
         "expert", split_axis=0, concat_axis=0, tiled=True,

time: 172 us -> 173 us (level)
  local copies, waits for them, and re-layouts: 0.06 us -> 4.84 us
  waiting for transfers between devices: 58.5 us -> 55 us
    unnamed x28 -> x36, local copies, waits for them, and re-layouts: 0.06 us -> 4.84 us
    ppermute x14, waiting for transfers between devices: 9.79 us -> 6.36 us  [ring_sums(): carried[way, piece] = lax.ppermute(own, 'dp', moves[way])]
    pallas_call x1, Pallas kernels: 5.53 us -> 7.67 us  [expert_first(): pl.pallas_call(functools.partial(expert_kernel, capacity, ring), in_specs...]
    pallas_call x1, Pallas kernels: 4.7 us -> 2.73 us  [expert_late(): pl.pallas_call(functools.partial(late_kernel, ring), in_specs=[pl.BlockSp...]
  transfers between devices with their start and end apart: 17 -> 17, of which waited for: 7 -> 5; matrix products, arithmetic and copies ran while one was open for 0% -> 0% of each run, Pallas kernels for 4% -> 3%
where the time goes in v8:
time: 173 us
  starting transfers between devices  94.2 us (54%)
  waiting for transfers between devices  55 us (32%)
  Pallas kernels  17.3 us (10%)
  local copies, waits for them, and re-layouts  4.84 us (3%)
    ppermute x14, starting transfers between devices, ring_sums(): carried[way, piece] = lax.ppermute(own, 'dp', moves[way])  61.3 us
    all_to_all x1, waiting for transfers between devices, on_device(): lax.all_to_all(send.reshape(experts, 2 * capacity, features), 'expert', s...  48.7 us
    all_to_all x1, starting transfers between devices, on_device(): lax.all_to_all(back.reshape(experts, 2 * capacity, back.shape[1]), 'exper...  15.5 us
    all_to_all x1, starting transfers between devices, on_device(): lax.all_to_all(send.reshape(experts, 2 * capacity, features), 'expert', s...  12.8 us
    pallas_call x1, Pallas kernels, expert_first(): pl.pallas_call(functools.partial(expert_kernel, capacity, ring), in_specs...  7.67 us
    ppermute x14, waiting for transfers between devices, ring_sums(): carried[way, piece] = lax.ppermute(own, 'dp', moves[way])  6.36 us
    unnamed x36, local copies, waits for them, and re-layouts  4.84 us
    ppermute x1, starting transfers between devices, ring_sums(): lax.ppermute(add(block(0, 0), carried[1, 0], carried[-1, 0]), 'dp', [(i,...  4.52 us
  transfers between devices with their start and end apart: 17, of which 5 were waited for; matrix products, arithmetic and copies ran while one was open for 0% of the time, Pallas kernels for 3%

profile of v8, /device:TPU:80, one launch (start us, length us, event | category | flops | bytes accessed | tf_op | source)
XLA Modules:
  0.0 172.5 jit_solution(12217966863101664903)
XLA Ops:
  0.6 3.2 %dispatch.1 = bf16[512,2048]{1,0:T(8,128)(2,1)} custom-call(s32[1,128]{1,0:T(1,128)} %bitcast.23, s32[1,128]{1,0:T(1,128)} %bitcast.25, bf16[1,128]{1,0:T(2,128)(2,1)} %bitcast.27, bf16[128,2048]{1,0:T(8,128)(2,1)} %tokens_hbm.1, bf16[128,2048]{1,0:T(8,128)(2,1)} %cotan_hbm.1), custom_call_target="tpu_custom_call" | custom-call | tf_op jit(solution)/shard_map/dispatch/pallas_call | solution.py:74
  3.8 12.8 %all-to-all-start = ((bf16[64,8,2048]{2,1,0:T(8,128)(2,1)}), bf16[64,8,2048]{2,1,0:T(8,128)(2,1)S(1)}, u32[]{:S(2)}, u32[]{:S(2)}) async-start(bf16[64,8,2048]{2,1,0:T(8,128)(2,1)} %bitcast.18), calls=%async_computation | async-start | bytes 4194304 | tf_op jit(solution)/shard_map/all_to_all | solution.py:366
  16.7 0.1 pad_add_fusion.place_ref
  16.7 48.7 %all-to-all-done = bf16[64,8,2048]{2,1,0:T(8,128)(2,1)S(1)} async-done(((bf16[64,8,2048]{2,1,0:T(8,128)(2,1)}), bf16[64,8,2048]{2,1,0:T(8,128)(2,1)S(1)}, u32[]{:S(2)}, u32[]{:S(2)}) %all-to-all-start) | async-done | bytes 2097184 | tf_op jit(solution)/shard_map/all_to_all | solution.py:366
  65.4 7.7 %expert_first.1 = (bf16[256,768]{1,0:T(8,128)(2,1)S(1)}, bf16[256,2048]{1,0:T(8,128)(2,1)S(1)}, bf16[256,2048]{1,0:T(8,128)(2,1)S(1)}, bf16[256,384]{1,0:T(8,128...) custom-call(s32[2]{0:T(128)S(1)} %pad_add_fusion.place_ref, ...), custom_call_target="tpu_custom_call" | custom-call | tf_op jit(solution)/shard_map/expert_first/pallas_call | solution.py:199
  73.1 1.0 copy-done
  74.1 0.7 copy-done.14
  74.7 15.5 %all-to-all-start.1 = ((bf16[64,8,1152]{2,1,0:T(8,128)(2,1)}), bf16[64,8,1152]{2,1,0:T(8,128)(2,1)S(1)}, u32[]{:S(2)}, u32[]{:S(2)}) async-start(bf16[64,8,1152]{2,1,0:T(8,128)(2,1)} %bitcast.22), calls=%async_computation.1 | async-start | bytes 2359296 | tf_op jit(solution)/shard_map/all_to_all | solution.py:378
  90.3 4.8 %collective-permute-start = (bf16[128,1152]{1,0:T(8,128)(2,1)}, bf16[128,1152]{1,0:T(8,128)(2,1)S(1)}, u32[]{:S(2)}, u32[]{:S(2)}) collective-permute-start(bf16[128,1152]{1,0:T(8,128)(2,1)} %get-tuple-element.43), channel_id=1, source_target_pairs={{0,1},{1,2},{2,3},{3,4},{4,5},{5,6},{6,7},{7,0},{8,9},{9,10},{10,1... | collective-permute-start | bytes 884744 | tf_op jit(solution)/shard_map/ppermute | solution.py:350
  95.1 14.0 %collective-permute-start.4 = (bf16[128,1152]{1,0:T(8,128)(2,1)}, bf16[128,1152]{1,0:T(8,128)(2,1)S(1)}, u32[]{:S(2)}, u32[]{:S(2)}) collective-permute-start(bf16[128,1152]{1,0:T(8,128)(2,1)} %get-tuple-element.46), channel_id=1, source_target_pairs={{0,7},{1,0},{2,1},{3,2},{4,3},{5,4},{6,5},{7,6},{8,15},{9,8},{10,9... | collective-permute-start | bytes 884744 | tf_op jit(solution)/shard_map/ppermute | solution.py:350
  109.2 1.2 copy-done.1
  110.4 2.7 %expert_late.1 = (bf16[128,1152]{1,0:T(8,128)(2,1)}, bf16[128,1152]{1,0:T(8,128)(2,1)}, bf16[128,1152]{1,0:T(8,128)(2,1)}, bf16[128,1152]{1,0:T(8,128)(2,1)}, bf...) custom-call(s32[2]{0:T(128)S(1)} %pad_add_fusion.place_ref, ...), custom_call_target="tpu_custom_call" | custom-call | tf_op jit(solution)/shard_map/expert_late/pallas_call | solution.py:242
  113.2 1.6 collective-permute-done.refs_1_
  114.8 1.0 copy-done.11
  115.7 0.1 add.13
  115.8 1.9 %collective-permute-start.1 = (bf16[128,1152]{1,0:T(8,128)(2,1)S(1)}, bf16[128,1152]{1,0:T(8,128)(2,1)S(1)}, u32[]{:S(2)}, u32[]{:S(2)}) collective-permute-start(bf16[128,1152]{1,0:T(8,128)(2,1)S(1)} %add.13), channel_id=1, source_target_pairs={{0,1},{1,2},{2,3},{3,4},{4,5},{5,6},{6,7},{7,0},{8,9},{9,10},{10,1... | collective-permute-start | bytes 884744 | tf_op jit(solution)/shard_map/ppermute | solution.py:350
  117.8 5.1 %collective-permute-start.11 = (bf16[128,1152]{1,0:T(8,128)(2,1)S(1)}, bf16[128,1152]{1,0:T(8,128)(2,1)S(1)}, u32[]{:S(2)}, u32[]{:S(2)}) collective-permute-start(bf16[128,1152]{1,0:T(8,128)(2,1)S(1)} %copy-done.17), channel_id=1, source_target_pairs={{0,7},{1,0},{2,1},{3,2},{4,3},{5,4},{6,5},{7,6},{8,15},{9,8},{10,9... | collective-permute-start | bytes 884744 | tf_op jit(solution)/shard_map/ppermute | solution.py:350
  122.9 1.9 %collective-permute-start.8 = (bf16[128,1152]{1,0:T(8,128)(2,1)S(1)}, bf16[128,1152]{1,0:T(8,128)(2,1)S(1)}, u32[]{:S(2)}, u32[]{:S(2)}) collective-permute-start(bf16[128,1152]{1,0:T(8,128)(2,1)S(1)} %copy-done.16), channel_id=1, source_target_pairs={{0,1},{1,2},{2,3},{3,4},{4,5},{5,6},{6,7},{7,0},{8,9},{9,10},{10,1... | collective-permute-start | bytes 884744 | tf_op jit(solution)/shard_map/ppermute | solution.py:350
  124.8 0.0 collective-permute-done.4.refs_1_
  124.9 1.0 copy-done.10
  125.8 0.1 add.16
  125.9 5.1 %collective-permute-start.5 = (bf16[128,1152]{1,0:T(8,128)(2,1)S(1)}, bf16[128,1152]{1,0:T(8,128)(2,1)S(1)}, u32[]{:S(2)}, u32[]{:S(2)}) collective-permute-start(bf16[128,1152]{1,0:T(8,128)(2,1)S(1)} %add.16), channel_id=1, source_target_pairs={{0,7},{1,0},{2,1},{3,2},{4,3},{5,4},{6,5},{7,6},{8,15},{9,8},{10,9... | collective-permute-start | bytes 884744 | tf_op jit(solution)/shard_map/ppermute | solution.py:350
  131.1 0.1 add.14
  131.1 1.9 %collective-permute-start.2 = (bf16[128,1152]{1,0:T(8,128)(2,1)S(1)}, bf16[128,1152]{1,0:T(8,128)(2,1)S(1)}, u32[]{:S(2)}, u32[]{:S(2)}) collective-permute-start(bf16[128,1152]{1,0:T(8,128)(2,1)S(1)} %add.14), channel_id=1, source_target_pairs={{0,1},{1,2},{2,3},{3,4},{4,5},{5,6},{6,7},{7,0},{8,9},{9,10},{10,1... | collective-permute-start | bytes 884744 | tf_op jit(solution)/shard_map/ppermute | solution.py:350
  133.1 0.1 add.21
  133.2 5.1 %collective-permute-start.12 = (bf16[128,1152]{1,0:T(8,128)(2,1)S(1)}, bf16[128,1152]{1,0:T(8,128)(2,1)S(1)}, u32[]{:S(2)}, u32[]{:S(2)}) collective-permute-start(bf16[128,1152]{1,0:T(8,128)(2,1)S(1)} %add.21), channel_id=1, source_target_pairs={{0,7},{1,0},{2,1},{3,2},{4,3},{5,4},{6,5},{7,6},{8,15},{9,8},{10,9... | collective-permute-start | bytes 884744 | tf_op jit(solution)/shard_map/ppermute | solution.py:350
  138.3 0.0 collective-permute-done.8.refs_1_
  138.4 0.1 add.19
  138.4 1.9 %collective-permute-start.9 = (bf16[128,1152]{1,0:T(8,128)(2,1)S(1)}, bf16[128,1152]{1,0:T(8,128)(2,1)S(1)}, u32[]{:S(2)}, u32[]{:S(2)}) collective-permute-start(bf16[128,1152]{1,0:T(8,128)(2,1)S(1)} %add.19), channel_id=1, source_target_pairs={{0,1},{1,2},{2,3},{3,4},{4,5},{5,6},{6,7},{7,0},{8,9},{9,10},{10,1... | collective-permute-start | bytes 884744 | tf_op jit(solution)/shard_map/ppermute | solution.py:350
  140.4 0.0 collective-permute-done.5.refs_1_
  140.4 0.1 add.17
  140.5 5.1 %collective-permute-start.6 = (bf16[128,1152]{1,0:T(8,128)(2,1)S(1)}, bf16[128,1152]{1,0:T(8,128)(2,1)S(1)}, u32[]{:S(2)}, u32[]{:S(2)}) collective-permute-start(bf16[128,1152]{1,0:T(8,128)(2,1)S(1)} %add.17), channel_id=1, source_target_pairs={{0,7},{1,0},{2,1},{3,2},{4,3},{5,4},{6,5},{7,6},{8,15},{9,8},{10,9... | collective-permute-start | bytes 884744 | tf_op jit(solution)/shard_map/ppermute | solution.py:350
  145.6 0.0 collective-permute-done.2.refs_1_
  145.6 0.1 add.15
  145.7 2.1 %collective-permute-start.3 = (bf16[128,1152]{1,0:T(8,128)(2,1)S(1)}, bf16[128,1152]{1,0:T(8,128)(2,1)S(1)}, u32[]{:S(2)}, u32[]{:S(2)}) collective-permute-start(bf16[128,1152]{1,0:T(8,128)(2,1)S(1)} %add.15), channel_id=1, source_target_pairs={{0,1},{1,2},{2,3},{3,4},{4,5},{5,6},{6,7},{7,0},{8,9},{9,10},{10,1... | collective-permute-start | bytes 884744 | tf_op jit(solution)/shard_map/ppermute | solution.py:350
  147.8 0.1 add.22
  147.9 5.1 %collective-permute-start.13 = (bf16[128,1152]{1,0:T(8,128)(2,1)S(1)}, bf16[128,1152]{1,0:T(8,128)(2,1)S(1)}, u32[]{:S(2)}, u32[]{:S(2)}) collective-permute-start(bf16[128,1152]{1,0:T(8,128)(2,1)S(1)} %add.22), channel_id=1, source_target_pairs={{0,7},{1,0},{2,1},{3,2},{4,3},{5,4},{6,5},{7,6},{8,15},{9,8},{10,9... | collective-permute-start | bytes 884744 | tf_op jit(solution)/shard_map/ppermute | solution.py:350
  153.1 0.1 add.20
  153.1 2.5 %collective-permute-done.3.refs_1_ = bf16[128,1152]{1,0:T(8,128)(2,1)S(1)} collective-permute-done((bf16[128,1152]{1,0:T(8,128)(2,1)S(1)}, bf16[128,1152]{1,0:T(8,128)(2,1)S(1)}, u32[]{:S(2)}, u32[]{:S(2)}) %collective-permute-start.3) | collective-permute-done | bytes 294944 | tf_op jit(solution)/shard_map/ppermute | solution.py:350
  155.7 0.1 add.18
  155.8 4.5 %collective-permute-start.7 = (bf16[128,1152]{1,0:T(8,128)(2,1)S(1)}, bf16[128,1152]{1,0:T(8,128)(2,1)S(1)}, u32[]{:S(2)}, u32[]{:S(2)}) collective-permute-start(bf16[128,1152]{1,0:T(8,128)(2,1)S(1)} %add.18), channel_id=1, source_target_pairs={{0,8},{1,9},{2,10},{3,11},{4,12},{5,13},{6,14},{7,15},{8,0},{9,1},... | collective-permute-start | bytes 884744 | tf_op jit(solution)/shard_map/ppermute | solution.py:351
  160.3 1.9 %collective-permute-start.10 = (bf16[128,1152]{1,0:T(8,128)(2,1)S(1)}, bf16[128,1152]{1,0:T(8,128)(2,1)S(1)}, u32[]{:S(2)}, u32[]{:S(2)}) collective-permute-start(bf16[128,1152]{1,0:T(8,128)(2,1)S(1)} %add.20), channel_id=1, source_target_pairs={{0,1},{1,2},{2,3},{3,4},{4,5},{5,6},{6,7},{7,0},{8,9},{9,10},{10,1... | collective-permute-start | bytes 884744 | tf_op jit(solution)/shard_map/ppermute | solution.py:350
  162.3 0.1 add.23
  162.4 5.1 %collective-permute-start.14 = (bf16[128,1152]{1,0:T(8,128)(2,1)S(1)}, bf16[128,1152]{1,0:T(8,128)(2,1)S(1)}, u32[]{:S(2)}, u32[]{:S(2)}) collective-permute-start(bf16[128,1152]{1,0:T(8,128)(2,1)S(1)} %add.23), channel_id=1, source_target_pairs={{0,7},{1,0},{2,1},{3,2},{4,3},{5,4},{6,5},{7,6},{8,15},{9,8},{10,9... | collective-permute-start | bytes 884744 | tf_op jit(solution)/shard_map/ppermute | solution.py:350
  167.5 2.0 %combine.1 = (bf16[128,2048]{1,0:T(8,128)(2,1)}, bf16[1,128]{1,0:T(2,128)(2,1)}) custom-call(s32[1,128]{1,0:T(1,128)} %bitcast.24, s32[1,128]{1,0:T(1,128)} %bitcast.26, bf16[1,128]{1,0:T(2,128)(2,1)} %bitcast.28, bf16[512,1152]{1,0:T(8,128)(2,1)S(1)} %bitcast.17), custom_call_target="tpu_custom_call" | custom-call | tf_op jit(solution)/shard_map/combine/pallas_call | solution.py:274
  169.5 0.6 collective-permute-done.10.up_way_ref
  170.2 1.6 collective-permute-done.14.down_way_ref
  171.7 0.8 split_grads.1
  (39 shorter events, 0.1 us)
Async XLA Ops:
  3.8 61.6 %all-to-all-start = ((bf16[64,8,2048]{2,1,0:T(8,128)(2,1)}), bf16[64,8,2048]{2,1,0:T(8,128)(2,1)S(1)}, u32[]{:S(2)}, u32[]{:S(2)}) async-start(bf16[64,8,2048]{2,1,0:T(8,128)(2,1)} %bitcast.18), calls=%async_computation | async-start | bytes 4194304 | tf_op jit(solution)/shard_map/all_to_all | solution.py:366
  73.1 1.0 copy-start
  74.1 0.7 copy-start.14
  74.7 34.4 %copy-start.15 = (bf16[256,384]{1,0:T(8,128)(2,1)S(1)}, bf16[256,384]{1,0:T(8,128)(2,1)}, u32[]{:S(2)}) copy-start(bf16[256,384]{1,0:T(8,128)(2,1)} %copy-done.14) | copy-start | bytes 589828
  74.7 92.8 %all-to-all-start.1 = ((bf16[64,8,1152]{2,1,0:T(8,128)(2,1)}), bf16[64,8,1152]{2,1,0:T(8,128)(2,1)S(1)}, u32[]{:S(2)}, u32[]{:S(2)}) async-start(bf16[64,8,1152]{2,1,0:T(8,128)(2,1)} %bitcast.22), calls=%async_computation.1 | async-start | bytes 2359296 | tf_op jit(solution)/shard_map/all_to_all | solution.py:378
  90.3 24.5 %collective-permute-start = (bf16[128,1152]{1,0:T(8,128)(2,1)}, bf16[128,1152]{1,0:T(8,128)(2,1)S(1)}, u32[]{:S(2)}, u32[]{:S(2)}) collective-permute-start(bf16[128,1152]{1,0:T(8,128)(2,1)} %get-tuple-element.43), channel_id=1, source_target_pairs={{0,1},{1,2},{2,3},{3,4},{4,5},{5,6},{6,7},{7,0},{8,9},{9,10},{10,1... | collective-permute-start | bytes 884744 | tf_op jit(solution)/shard_map/ppermute | solution.py:350
  95.1 29.7 %collective-permute-start.4 = (bf16[128,1152]{1,0:T(8,128)(2,1)}, bf16[128,1152]{1,0:T(8,128)(2,1)S(1)}, u32[]{:S(2)}, u32[]{:S(2)}) collective-permute-start(bf16[128,1152]{1,0:T(8,128)(2,1)} %get-tuple-element.46), channel_id=1, source_target_pairs={{0,7},{1,0},{2,1},{3,2},{4,3},{5,4},{6,5},{7,6},{8,15},{9,8},{10,9... | collective-permute-start | bytes 884744 | tf_op jit(solution)/shard_map/ppermute | solution.py:350
  109.2 1.2 copy-start.1
  110.4 7.3 %copy-start.17 = (bf16[128,1152]{1,0:T(8,128)(2,1)S(1)}, bf16[128,1152]{1,0:T(8,128)(2,1)}, u32[]{:S(2)}) copy-start(bf16[128,1152]{1,0:T(8,128)(2,1)} %get-tuple-element.56) | copy-start | bytes 884740
  110.4 12.5 %copy-start.16 = (bf16[128,1152]{1,0:T(8,128)(2,1)S(1)}, bf16[128,1152]{1,0:T(8,128)(2,1)}, u32[]{:S(2)}) copy-start(bf16[128,1152]{1,0:T(8,128)(2,1)} %get-tuple-element.52) | copy-start | bytes 884740
  113.2 17.9 %copy-start.9 = (bf16[128,1152]{1,0:T(8,128)(2,1)S(1)}, bf16[128,1152]{1,0:T(8,128)(2,1)}, u32[]{:S(2)}) copy-start(bf16[128,1152]{1,0:T(8,128)(2,1)} %get-tuple-element.41.refs_0_) | copy-start | bytes 884740
  113.2 19.9 %copy-start.8 = (bf16[128,1152]{1,0:T(8,128)(2,1)S(1)}, bf16[128,1152]{1,0:T(8,128)(2,1)}, u32[]{:S(2)}) copy-start(bf16[128,1152]{1,0:T(8,128)(2,1)} %get-tuple-element.55.refs_0_) | copy-start | bytes 884740
  114.8 1.0 copy-start.11
  115.7 22.6 %copy-start.7 = (bf16[128,1152]{1,0:T(8,128)(2,1)S(1)}, bf16[128,1152]{1,0:T(8,128)(2,1)}, u32[]{:S(2)}) copy-start(bf16[128,1152]{1,0:T(8,128)(2,1)} %get-tuple-element.51.refs_0_) | copy-start | bytes 884740
  115.8 15.2 %collective-permute-start.1 = (bf16[128,1152]{1,0:T(8,128)(2,1)S(1)}, bf16[128,1152]{1,0:T(8,128)(2,1)S(1)}, u32[]{:S(2)}, u32[]{:S(2)}) collective-permute-start(bf16[128,1152]{1,0:T(8,128)(2,1)S(1)} %add.13), channel_id=1, source_target_pairs={{0,1},{1,2},{2,3},{3,4},{4,5},{5,6},{6,7},{7,0},{8,9},{9,10},{10,1... | collective-permute-start | bytes 884744 | tf_op jit(solution)/shard_map/ppermute | solution.py:350
  117.8 15.3 %collective-permute-start.11 = (bf16[128,1152]{1,0:T(8,128)(2,1)S(1)}, bf16[128,1152]{1,0:T(8,128)(2,1)S(1)}, u32[]{:S(2)}, u32[]{:S(2)}) collective-permute-start(bf16[128,1152]{1,0:T(8,128)(2,1)S(1)} %copy-done.17), channel_id=1, source_target_pairs={{0,7},{1,0},{2,1},{3,2},{4,3},{5,4},{6,5},{7,6},{8,15},{9,8},{10,9... | collective-permute-start | bytes 884744 | tf_op jit(solution)/shard_map/ppermute | solution.py:350
  122.9 15.4 %collective-permute-start.8 = (bf16[128,1152]{1,0:T(8,128)(2,1)S(1)}, bf16[128,1152]{1,0:T(8,128)(2,1)S(1)}, u32[]{:S(2)}, u32[]{:S(2)}) collective-permute-start(bf16[128,1152]{1,0:T(8,128)(2,1)S(1)} %copy-done.16), channel_id=1, source_target_pairs={{0,1},{1,2},{2,3},{3,4},{4,5},{5,6},{6,7},{7,0},{8,9},{9,10},{10,1... | collective-permute-start | bytes 884744 | tf_op jit(solution)/shard_map/ppermute | solution.py:350
  124.8 1.0 copy-start.10
  125.8 14.6 %copy-start.6 = (bf16[128,1152]{1,0:T(8,128)(2,1)S(1)}, bf16[128,1152]{1,0:T(8,128)(2,1)}, u32[]{:S(2)}) copy-start(bf16[128,1152]{1,0:T(8,128)(2,1)} %get-tuple-element.44.refs_0_) | copy-start | bytes 884740
  125.9 14.5 %collective-permute-start.5 = (bf16[128,1152]{1,0:T(8,128)(2,1)S(1)}, bf16[128,1152]{1,0:T(8,128)(2,1)S(1)}, u32[]{:S(2)}, u32[]{:S(2)}) collective-permute-start(bf16[128,1152]{1,0:T(8,128)(2,1)S(1)} %add.16), channel_id=1, source_target_pairs={{0,7},{1,0},{2,1},{3,2},{4,3},{5,4},{6,5},{7,6},{8,15},{9,8},{10,9... | collective-permute-start | bytes 884744 | tf_op jit(solution)/shard_map/ppermute | solution.py:350
  131.1 14.6 %copy-start.5 = (bf16[128,1152]{1,0:T(8,128)(2,1)S(1)}, bf16[128,1152]{1,0:T(8,128)(2,1)}, u32[]{:S(2)}) copy-start(bf16[128,1152]{1,0:T(8,128)(2,1)} %get-tuple-element.40.refs_0_) | copy-start | bytes 884740
  131.1 14.5 %collective-permute-start.2 = (bf16[128,1152]{1,0:T(8,128)(2,1)S(1)}, bf16[128,1152]{1,0:T(8,128)(2,1)S(1)}, u32[]{:S(2)}, u32[]{:S(2)}) collective-permute-start(bf16[128,1152]{1,0:T(8,128)(2,1)S(1)} %add.14), channel_id=1, source_target_pairs={{0,1},{1,2},{2,3},{3,4},{4,5},{5,6},{6,7},{7,0},{8,9},{9,10},{10,1... | collective-permute-start | bytes 884744 | tf_op jit(solution)/shard_map/ppermute | solution.py:350
  133.1 14.7 %copy-start.4 = (bf16[128,1152]{1,0:T(8,128)(2,1)S(1)}, bf16[128,1152]{1,0:T(8,128)(2,1)}, u32[]{:S(2)}) copy-start(bf16[128,1152]{1,0:T(8,128)(2,1)} %get-tuple-element.54.refs_0_) | copy-start | bytes 884740
  133.2 14.6 %collective-permute-start.12 = (bf16[128,1152]{1,0:T(8,128)(2,1)S(1)}, bf16[128,1152]{1,0:T(8,128)(2,1)S(1)}, u32[]{:S(2)}, u32[]{:S(2)}) collective-permute-start(bf16[128,1152]{1,0:T(8,128)(2,1)S(1)} %add.21), channel_id=1, source_target_pairs={{0,7},{1,0},{2,1},{3,2},{4,3},{5,4},{6,5},{7,6},{8,15},{9,8},{10,9... | collective-permute-start | bytes 884744 | tf_op jit(solution)/shard_map/ppermute | solution.py:350
  138.3 14.7 %copy-start.3 = (bf16[128,1152]{1,0:T(8,128)(2,1)S(1)}, bf16[128,1152]{1,0:T(8,128)(2,1)}, u32[]{:S(2)}) copy-start(bf16[128,1152]{1,0:T(8,128)(2,1)} %get-tuple-element.50.refs_0_) | copy-start | bytes 884740
  138.4 14.6 %collective-permute-start.9 = (bf16[128,1152]{1,0:T(8,128)(2,1)S(1)}, bf16[128,1152]{1,0:T(8,128)(2,1)S(1)}, u32[]{:S(2)}, u32[]{:S(2)}) collective-permute-start(bf16[128,1152]{1,0:T(8,128)(2,1)S(1)} %add.19), channel_id=1, source_target_pairs={{0,1},{1,2},{2,3},{3,4},{4,5},{5,6},{6,7},{7,0},{8,9},{9,10},{10,1... | collective-permute-start | bytes 884744 | tf_op jit(solution)/shard_map/ppermute | solution.py:350
  140.4 15.3 %copy-start.13 = (bf16[128,1152]{1,0:T(8,128)(2,1)S(1)}, bf16[128,1152]{1,0:T(8,128)(2,1)}, u32[]{:S(2)}) copy-start(bf16[128,1152]{1,0:T(8,128)(2,1)} %get-tuple-element.39.refs_0_) | copy-start | bytes 884740
  140.5 12.7 %collective-permute-start.6 = (bf16[128,1152]{1,0:T(8,128)(2,1)S(1)}, bf16[128,1152]{1,0:T(8,128)(2,1)S(1)}, u32[]{:S(2)}, u32[]{:S(2)}) collective-permute-start(bf16[128,1152]{1,0:T(8,128)(2,1)S(1)} %add.17), channel_id=1, source_target_pairs={{0,7},{1,0},{2,1},{3,2},{4,3},{5,4},{6,5},{7,6},{8,15},{9,8},{10,9... | collective-permute-start | bytes 884744 | tf_op jit(solution)/shard_map/ppermute | solution.py:350
  145.7 16.6 %copy-start.2 = (bf16[128,1152]{1,0:T(8,128)(2,1)S(1)}, bf16[128,1152]{1,0:T(8,128)(2,1)}, u32[]{:S(2)}) copy-start(bf16[128,1152]{1,0:T(8,128)(2,1)} %get-tuple-element.53.refs_0_) | copy-start | bytes 884740
  145.7 10.0 %collective-permute-start.3 = (bf16[128,1152]{1,0:T(8,128)(2,1)S(1)}, bf16[128,1152]{1,0:T(8,128)(2,1)S(1)}, u32[]{:S(2)}, u32[]{:S(2)}) collective-permute-start(bf16[128,1152]{1,0:T(8,128)(2,1)S(1)} %add.15), channel_id=1, source_target_pairs={{0,1},{1,2},{2,3},{3,4},{4,5},{5,6},{6,7},{7,0},{8,9},{9,10},{10,1... | collective-permute-start | bytes 884744 | tf_op jit(solution)/shard_map/ppermute | solution.py:350
  147.9 14.4 %collective-permute-start.13 = (bf16[128,1152]{1,0:T(8,128)(2,1)S(1)}, bf16[128,1152]{1,0:T(8,128)(2,1)S(1)}, u32[]{:S(2)}, u32[]{:S(2)}) collective-permute-start(bf16[128,1152]{1,0:T(8,128)(2,1)S(1)} %add.22), channel_id=1, source_target_pairs={{0,7},{1,0},{2,1},{3,2},{4,3},{5,4},{6,5},{7,6},{8,15},{9,8},{10,9... | collective-permute-start | bytes 884744 | tf_op jit(solution)/shard_map/ppermute | solution.py:350
  155.7 16.0 %copy-start.12 = (bf16[128,1152]{1,0:T(8,128)(2,1)S(1)}, bf16[128,1152]{1,0:T(8,128)(2,1)}, u32[]{:S(2)}) copy-start(bf16[128,1152]{1,0:T(8,128)(2,1)} %get-tuple-element.49.own_ref) | copy-start | bytes 884740
  155.8 13.7 %collective-permute-start.7 = (bf16[128,1152]{1,0:T(8,128)(2,1)S(1)}, bf16[128,1152]{1,0:T(8,128)(2,1)S(1)}, u32[]{:S(2)}, u32[]{:S(2)}) collective-permute-start(bf16[128,1152]{1,0:T(8,128)(2,1)S(1)} %add.18), channel_id=1, source_target_pairs={{0,8},{1,9},{2,10},{3,11},{4,12},{5,13},{6,14},{7,15},{8,0},{9,1},... | collective-permute-start | bytes 884744 | tf_op jit(solution)/shard_map/ppermute | solution.py:351
  160.3 9.8 %collective-permute-start.10 = (bf16[128,1152]{1,0:T(8,128)(2,1)S(1)}, bf16[128,1152]{1,0:T(8,128)(2,1)S(1)}, u32[]{:S(2)}, u32[]{:S(2)}) collective-permute-start(bf16[128,1152]{1,0:T(8,128)(2,1)S(1)} %add.20), channel_id=1, source_target_pairs={{0,1},{1,2},{2,3},{3,4},{4,5},{5,6},{6,7},{7,0},{8,9},{9,10},{10,1... | collective-permute-start | bytes 884744 | tf_op jit(solution)/shard_map/ppermute | solution.py:350
  162.4 9.4 %collective-permute-start.14 = (bf16[128,1152]{1,0:T(8,128)(2,1)S(1)}, bf16[128,1152]{1,0:T(8,128)(2,1)S(1)}, u32[]{:S(2)}, u32[]{:S(2)}) collective-permute-start(bf16[128,1152]{1,0:T(8,128)(2,1)S(1)} %add.23), channel_id=1, source_target_pairs={{0,7},{1,0},{2,1},{3,2},{4,3},{5,4},{6,5},{7,6},{8,15},{9,8},{10,9... | collective-permute-start | bytes 884744 | tf_op jit(solution)/shard_map/ppermute | solution.py:350

commit v9 on v4

--- a/solution.py
+++ b/solution.py
@@ -351,6 +351,7 @@
     token_grad, score_grad = combine(
         expert_ids, slot_index, gate_scores, returned, features, capacity
     )
+    other, score_grad = lax.optimization_barrier((other, score_grad))
     grad_gate, grad_up, grad_down = split_grads(*kept, other)
     return token_grad, score_grad.reshape(count), grad_gate[None], grad_up[None], grad_down[None]
 

time: 172 us -> 172 us (level)
  the two profiles are of different devices: /device:TPU:2 before, /device:TPU:80 now
where the time goes in v9:
time: 172 us; the launch traced here: 171 us
  starting transfers between devices  94.3 us (55%)
  waiting for transfers between devices  58.8 us (34%)
  Pallas kernels  16.7 us (10%)
    ppermute x14, starting transfers between devices, ring_sums(): carried[way, piece] = lax.ppermute(own, 'dp', moves[way])  61.5 us
    all_to_all x1, waiting for transfers between devices, on_device(): lax.all_to_all(send.reshape(experts, 2 * capacity, features), 'expert', s...  48.7 us
    all_to_all x1, starting transfers between devices, on_device(): lax.all_to_all(back.reshape(experts, 2 * capacity, back.shape[1]), 'exper...  15.5 us
    all_to_all x1, starting transfers between devices, on_device(): lax.all_to_all(send.reshape(experts, 2 * capacity, features), 'expert', s...  12.8 us
    ppermute x14, waiting for transfers between devices, ring_sums(): carried[way, piece] = lax.ppermute(own, 'dp', moves[way])  10.1 us
    pallas_call x1, Pallas kernels, expert_grads(): pl.pallas_call(functools.partial(expert_kernel, capacity, ring), in_specs...  6.93 us
    ppermute x1, starting transfers between devices, on_device(): lax.ppermute(add(*for_other), 'dp', [(i, (i + ring) % (2 * ring)) for i i...  4.48 us
  transfers between devices with their start and end apart: 17, of which 5 were waited for; matrix products, arithmetic and copies ran while one was open for 0% of the time, Pallas kernels for 2%

profile of v9, /device:TPU:80, one launch (start us, length us, event | category | flops | bytes accessed | tf_op | source)
XLA Modules:
  0.0 171.2 jit_solution(5890704340697770569)
XLA Ops:
  0.6 3.2 %dispatch.1 = bf16[512,2048]{1,0:T(8,128)(2,1)} custom-call(s32[1,128]{1,0:T(1,128)} %bitcast.22, s32[1,128]{1,0:T(1,128)} %bitcast.24, bf16[1,128]{1,0:T(2,128)(2,1)} %bitcast.26, bf16[128,2048]{1,0:T(8,128)(2,1)} %tokens_hbm.1, bf16[128,2048]{1,0:T(8,128)(2,1)} %cotan_hbm.1), custom_call_target="tpu_custom_call" | custom-call | tf_op jit(solution)/shard_map/dispatch/pallas_call | solution.py:74
  3.8 12.8 %all-to-all-start = ((bf16[64,8,2048]{2,1,0:T(8,128)(2,1)}), bf16[64,8,2048]{2,1,0:T(8,128)(2,1)S(1)}, u32[]{:S(2)}, u32[]{:S(2)}) async-start(bf16[64,8,2048]{2,1,0:T(8,128)(2,1)} %bitcast.18), calls=%async_computation | async-start | bytes 4194304 | tf_op jit(solution)/shard_map/all_to_all | solution.py:333
  16.6 0.1 pad_add_fusion.place_ref
  16.7 48.7 %all-to-all-done = bf16[64,8,2048]{2,1,0:T(8,128)(2,1)S(1)} async-done(((bf16[64,8,2048]{2,1,0:T(8,128)(2,1)}), bf16[64,8,2048]{2,1,0:T(8,128)(2,1)S(1)}, u32[]{:S(2)}, u32[]{:S(2)}) %all-to-all-start) | async-done | bytes 2097184 | tf_op jit(solution)/shard_map/all_to_all | solution.py:333
  65.4 6.9 %expert_grads.1 = (bf16[2048,384]{1,0:T(8,128)(2,1)S(1)}, bf16[2048,384]{1,0:T(8,128)(2,1)S(1)}, bf16[256,768]{1,0:T(8,128)(2,1)S(1)}, bf16[256,128]{1,0:T(8,128...) custom-call(s32[2]{0:T(128)S(1)} %pad_add_fusion.place_ref, ...), custom_call_target="tpu_custom_call" | custom-call | tf_op jit(solution)/shard_map/expert_grads/pallas_call | solution.py:171
  72.3 2.9 %return_rows.1 = bf16[512,1152]{1,0:T(8,128)(2,1)} custom-call(bf16[256,768]{1,0:T(8,128)(2,1)S(1)} %get-tuple-element.32.inner_ref, bf16[256,128]{1,0:T(8,128)(2,1)S(1)} %get-tuple-element.33.score_ref, bf16[2048,384]{1,0:T(8,128)(2,1)S(1)} %get-tuple-element.34.gate_ref, bf16[2048,384]{1,0:T(8,128)(2,1)S(1)} %get-tuple-element.35.up_ref), custom_call_target="tpu_custom_call" | custom-call | tf_op jit(solution)/shard_map/return_rows/pallas_call | solution.py:217
  75.3 15.5 %all-to-all-start.1 = ((bf16[64,8,1152]{2,1,0:T(8,128)(2,1)}), bf16[64,8,1152]{2,1,0:T(8,128)(2,1)S(1)}, u32[]{:S(2)}, u32[]{:S(2)}) async-start(bf16[64,8,1152]{2,1,0:T(8,128)(2,1)} %bitcast.10), calls=%async_computation.1 | async-start | bytes 2359296 | tf_op jit(solution)/shard_map/all_to_all | solution.py:343
  90.9 5.0 %collective-permute-start = (bf16[128,1152]{1,0:T(8,128)(2,1)S(1)}, bf16[128,1152]{1,0:T(8,128)(2,1)S(1)}, u32[]{:S(2)}, u32[]{:S(2)}) collective-permute-start(bf16[128,1152]{1,0:T(8,128)(2,1)S(1)} %copy-done.15), channel_id=1, source_target_pairs={{0,1},{1,2},{2,3},{3,4},{4,5},{5,6},{6,7},{7,0},{8,9},{9,10},{10,1... | collective-permute-start | bytes 884744 | tf_op jit(solution)/shard_map/ppermute | solution.py:319
  95.9 14.1 %collective-permute-start.4 = (bf16[128,1152]{1,0:T(8,128)(2,1)S(1)}, bf16[128,1152]{1,0:T(8,128)(2,1)S(1)}, u32[]{:S(2)}, u32[]{:S(2)}) collective-permute-start(bf16[128,1152]{1,0:T(8,128)(2,1)S(1)} %copy-done.14), channel_id=1, source_target_pairs={{0,7},{1,0},{2,1},{3,2},{4,3},{5,4},{6,5},{7,6},{8,15},{9,8},{10,9... | collective-permute-start | bytes 884744 | tf_op jit(solution)/shard_map/ppermute | solution.py:319
  110.0 5.4 %collective-permute-done.refs_1_ = bf16[128,1152]{1,0:T(8,128)(2,1)S(1)} collective-permute-done((bf16[128,1152]{1,0:T(8,128)(2,1)S(1)}, bf16[128,1152]{1,0:T(8,128)(2,1)S(1)}, u32[]{:S(2)}, u32[]{:S(2)}) %collective-permute-start) | collective-permute-done | bytes 294944 | tf_op jit(solution)/shard_map/ppermute | solution.py:319
  115.3 0.1 add.13
  115.4 1.9 %collective-permute-start.1 = (bf16[128,1152]{1,0:T(8,128)(2,1)S(1)}, bf16[128,1152]{1,0:T(8,128)(2,1)S(1)}, u32[]{:S(2)}, u32[]{:S(2)}) collective-permute-start(bf16[128,1152]{1,0:T(8,128)(2,1)S(1)} %add.13), channel_id=1, source_target_pairs={{0,1},{1,2},{2,3},{3,4},{4,5},{5,6},{6,7},{7,0},{8,9},{9,10},{10,1... | collective-permute-start | bytes 884744 | tf_op jit(solution)/shard_map/ppermute | solution.py:319
  117.3 5.1 %collective-permute-start.11 = (bf16[128,1152]{1,0:T(8,128)(2,1)S(1)}, bf16[128,1152]{1,0:T(8,128)(2,1)S(1)}, u32[]{:S(2)}, u32[]{:S(2)}) collective-permute-start(bf16[128,1152]{1,0:T(8,128)(2,1)S(1)} %copy-done.13), channel_id=1, source_target_pairs={{0,7},{1,0},{2,1},{3,2},{4,3},{5,4},{6,5},{7,6},{8,15},{9,8},{10,9... | collective-permute-start | bytes 884744 | tf_op jit(solution)/shard_map/ppermute | solution.py:319
  122.5 1.9 %collective-permute-start.8 = (bf16[128,1152]{1,0:T(8,128)(2,1)S(1)}, bf16[128,1152]{1,0:T(8,128)(2,1)S(1)}, u32[]{:S(2)}, u32[]{:S(2)}) collective-permute-start(bf16[128,1152]{1,0:T(8,128)(2,1)S(1)} %copy-done.12), channel_id=1, source_target_pairs={{0,1},{1,2},{2,3},{3,4},{4,5},{5,6},{6,7},{7,0},{8,9},{9,10},{10,1... | collective-permute-start | bytes 884744 | tf_op jit(solution)/shard_map/ppermute | solution.py:319
  124.4 0.0 collective-permute-done.4.refs_1_
  124.5 0.1 add.16
  124.5 5.1 %collective-permute-start.5 = (bf16[128,1152]{1,0:T(8,128)(2,1)S(1)}, bf16[128,1152]{1,0:T(8,128)(2,1)S(1)}, u32[]{:S(2)}, u32[]{:S(2)}) collective-permute-start(bf16[128,1152]{1,0:T(8,128)(2,1)S(1)} %add.16), channel_id=1, source_target_pairs={{0,7},{1,0},{2,1},{3,2},{4,3},{5,4},{6,5},{7,6},{8,15},{9,8},{10,9... | collective-permute-start | bytes 884744 | tf_op jit(solution)/shard_map/ppermute | solution.py:319
  129.7 0.0 collective-permute-done.1.refs_1_
  129.7 0.1 add.14
  129.8 1.9 %collective-permute-start.2 = (bf16[128,1152]{1,0:T(8,128)(2,1)S(1)}, bf16[128,1152]{1,0:T(8,128)(2,1)S(1)}, u32[]{:S(2)}, u32[]{:S(2)}) collective-permute-start(bf16[128,1152]{1,0:T(8,128)(2,1)S(1)} %add.14), channel_id=1, source_target_pairs={{0,1},{1,2},{2,3},{3,4},{4,5},{5,6},{6,7},{7,0},{8,9},{9,10},{10,1... | collective-permute-start | bytes 884744 | tf_op jit(solution)/shard_map/ppermute | solution.py:319
  131.7 0.0 collective-permute-done.11.refs_1_
  131.7 0.1 add.21
  131.8 5.1 %collective-permute-start.12 = (bf16[128,1152]{1,0:T(8,128)(2,1)S(1)}, bf16[128,1152]{1,0:T(8,128)(2,1)S(1)}, u32[]{:S(2)}, u32[]{:S(2)}) collective-permute-start(bf16[128,1152]{1,0:T(8,128)(2,1)S(1)} %add.21), channel_id=1, source_target_pairs={{0,7},{1,0},{2,1},{3,2},{4,3},{5,4},{6,5},{7,6},{8,15},{9,8},{10,9... | collective-permute-start | bytes 884744 | tf_op jit(solution)/shard_map/ppermute | solution.py:319
  137.0 0.0 collective-permute-done.8.refs_1_
  137.0 0.1 add.19
  137.1 1.9 %collective-permute-start.9 = (bf16[128,1152]{1,0:T(8,128)(2,1)S(1)}, bf16[128,1152]{1,0:T(8,128)(2,1)S(1)}, u32[]{:S(2)}, u32[]{:S(2)}) collective-permute-start(bf16[128,1152]{1,0:T(8,128)(2,1)S(1)} %add.19), channel_id=1, source_target_pairs={{0,1},{1,2},{2,3},{3,4},{4,5},{5,6},{6,7},{7,0},{8,9},{9,10},{10,1... | collective-permute-start | bytes 884744 | tf_op jit(solution)/shard_map/ppermute | solution.py:319
  139.0 0.0 collective-permute-done.5.refs_1_
  139.0 0.0 copy-start.11
  139.0 0.1 add.17
  139.1 5.1 %collective-permute-start.6 = (bf16[128,1152]{1,0:T(8,128)(2,1)S(1)}, bf16[128,1152]{1,0:T(8,128)(2,1)S(1)}, u32[]{:S(2)}, u32[]{:S(2)}) collective-permute-start(bf16[128,1152]{1,0:T(8,128)(2,1)S(1)} %add.17), channel_id=1, source_target_pairs={{0,7},{1,0},{2,1},{3,2},{4,3},{5,4},{6,5},{7,6},{8,15},{9,8},{10,9... | collective-permute-start | bytes 884744 | tf_op jit(solution)/shard_map/ppermute | solution.py:319
  144.3 0.1 add.15
  144.4 2.1 %collective-permute-start.3 = (bf16[128,1152]{1,0:T(8,128)(2,1)S(1)}, bf16[128,1152]{1,0:T(8,128)(2,1)S(1)}, u32[]{:S(2)}, u32[]{:S(2)}) collective-permute-start(bf16[128,1152]{1,0:T(8,128)(2,1)S(1)} %add.15), channel_id=1, source_target_pairs={{0,1},{1,2},{2,3},{3,4},{4,5},{5,6},{6,7},{7,0},{8,9},{9,10},{10,1... | collective-permute-start | bytes 884744 | tf_op jit(solution)/shard_map/ppermute | solution.py:319
  146.4 0.0 collective-permute-done.12.refs_1_
  146.4 0.1 add.22
  146.5 5.1 %collective-permute-start.13 = (bf16[128,1152]{1,0:T(8,128)(2,1)S(1)}, bf16[128,1152]{1,0:T(8,128)(2,1)S(1)}, u32[]{:S(2)}, u32[]{:S(2)}) collective-permute-start(bf16[128,1152]{1,0:T(8,128)(2,1)S(1)} %add.22), channel_id=1, source_target_pairs={{0,7},{1,0},{2,1},{3,2},{4,3},{5,4},{6,5},{7,6},{8,15},{9,8},{10,9... | collective-permute-start | bytes 884744 | tf_op jit(solution)/shard_map/ppermute | solution.py:319
  151.7 0.0 collective-permute-done.9.refs_1_
  151.7 0.1 add.20
  151.8 0.0 collective-permute-done.6.refs_2_
  151.8 2.5 %collective-permute-done.3.refs_1_ = bf16[128,1152]{1,0:T(8,128)(2,1)S(1)} collective-permute-done((bf16[128,1152]{1,0:T(8,128)(2,1)S(1)}, bf16[128,1152]{1,0:T(8,128)(2,1)S(1)}, u32[]{:S(2)}, u32[]{:S(2)}) %collective-permute-start.3) | collective-permute-done | bytes 294944 | tf_op jit(solution)/shard_map/ppermute | solution.py:319
  154.3 0.1 add.18
  154.4 4.5 %collective-permute-start.7 = (bf16[128,1152]{1,0:T(8,128)(2,1)S(1)}, bf16[128,1152]{1,0:T(8,128)(2,1)S(1)}, u32[]{:S(2)}, u32[]{:S(2)}) collective-permute-start(bf16[128,1152]{1,0:T(8,128)(2,1)S(1)} %add.18), channel_id=1, source_target_pairs={{0,8},{1,9},{2,10},{3,11},{4,12},{5,13},{6,14},{7,15},{8,0},{9,1},... | collective-permute-start | bytes 884744 | tf_op jit(solution)/shard_map/ppermute | solution.py:348
  158.9 1.9 %collective-permute-start.10 = (bf16[128,1152]{1,0:T(8,128)(2,1)S(1)}, bf16[128,1152]{1,0:T(8,128)(2,1)S(1)}, u32[]{:S(2)}, u32[]{:S(2)}) collective-permute-start(bf16[128,1152]{1,0:T(8,128)(2,1)S(1)} %add.20), channel_id=1, source_target_pairs={{0,1},{1,2},{2,3},{3,4},{4,5},{5,6},{6,7},{7,0},{8,9},{9,10},{10,1... | collective-permute-start | bytes 884744 | tf_op jit(solution)/shard_map/ppermute | solution.py:319
  160.9 0.1 add.23
  161.0 5.1 %collective-permute-start.14 = (bf16[128,1152]{1,0:T(8,128)(2,1)S(1)}, bf16[128,1152]{1,0:T(8,128)(2,1)S(1)}, u32[]{:S(2)}, u32[]{:S(2)}) collective-permute-start(bf16[128,1152]{1,0:T(8,128)(2,1)S(1)} %add.23), channel_id=1, source_target_pairs={{0,7},{1,0},{2,1},{3,2},{4,3},{5,4},{6,5},{7,6},{8,15},{9,8},{10,9... | collective-permute-start | bytes 884744 | tf_op jit(solution)/shard_map/ppermute | solution.py:319
  166.1 2.0 %combine.1 = (bf16[128,2048]{1,0:T(8,128)(2,1)}, bf16[1,128]{1,0:T(2,128)(2,1)}) custom-call(s32[1,128]{1,0:T(1,128)} %bitcast.23, s32[1,128]{1,0:T(1,128)} %bitcast.25, bf16[1,128]{1,0:T(2,128)(2,1)} %bitcast.27, bf16[512,1152]{1,0:T(8,128)(2,1)S(1)} %bitcast.17), custom_call_target="tpu_custom_call" | custom-call | tf_op jit(solution)/shard_map/combine/pallas_call | solution.py:243
  168.1 0.6 collective-permute-done.10.up_way_ref
  168.8 1.6 collective-permute-done.14.down_way_ref
  170.3 0.8 split_grads.1
  (35 shorter events, 0.1 us)
Async XLA Ops:
  3.8 61.6 %all-to-all-start = ((bf16[64,8,2048]{2,1,0:T(8,128)(2,1)}), bf16[64,8,2048]{2,1,0:T(8,128)(2,1)S(1)}, u32[]{:S(2)}, u32[]{:S(2)}) async-start(bf16[64,8,2048]{2,1,0:T(8,128)(2,1)} %bitcast.18), calls=%async_computation | async-start | bytes 4194304 | tf_op jit(solution)/shard_map/all_to_all | solution.py:333
  75.3 15.6 %copy-start.15 = (bf16[128,1152]{1,0:T(8,128)(2,1)S(1)}, bf16[128,1152]{1,0:T(8,128)(2,1)}, u32[]{:S(2)}) copy-start(bf16[128,1152]{1,0:T(8,128)(2,1)} %get-tuple-element.41) | copy-start | bytes 884740
  75.3 20.6 %copy-start.14 = (bf16[128,1152]{1,0:T(8,128)(2,1)S(1)}, bf16[128,1152]{1,0:T(8,128)(2,1)}, u32[]{:S(2)}) copy-start(bf16[128,1152]{1,0:T(8,128)(2,1)} %get-tuple-element.44) | copy-start | bytes 884740
  75.3 40.1 %copy-start.9 = (bf16[128,1152]{1,0:T(8,128)(2,1)S(1)}, bf16[128,1152]{1,0:T(8,128)(2,1)}, u32[]{:S(2)}) copy-start(bf16[128,1152]{1,0:T(8,128)(2,1)} %get-tuple-element.40.refs_0_) | copy-start | bytes 884740
  75.3 42.1 %copy-start.13 = (bf16[128,1152]{1,0:T(8,128)(2,1)S(1)}, bf16[128,1152]{1,0:T(8,128)(2,1)}, u32[]{:S(2)}) copy-start(bf16[128,1152]{1,0:T(8,128)(2,1)} %get-tuple-element.54) | copy-start | bytes 884740
  75.3 47.2 %copy-start.12 = (bf16[128,1152]{1,0:T(8,128)(2,1)S(1)}, bf16[128,1152]{1,0:T(8,128)(2,1)}, u32[]{:S(2)}) copy-start(bf16[128,1152]{1,0:T(8,128)(2,1)} %get-tuple-element.50) | copy-start | bytes 884740
  75.3 49.1 %copy-start.8 = (bf16[128,1152]{1,0:T(8,128)(2,1)S(1)}, bf16[128,1152]{1,0:T(8,128)(2,1)}, u32[]{:S(2)}) copy-start(bf16[128,1152]{1,0:T(8,128)(2,1)} %get-tuple-element.43.refs_0_) | copy-start | bytes 884740
  75.3 54.4 %copy-start.7 = (bf16[128,1152]{1,0:T(8,128)(2,1)S(1)}, bf16[128,1152]{1,0:T(8,128)(2,1)}, u32[]{:S(2)}) copy-start(bf16[128,1152]{1,0:T(8,128)(2,1)} %get-tuple-element.39.refs_0_) | copy-start | bytes 884740
  75.3 90.8 %all-to-all-start.1 = ((bf16[64,8,1152]{2,1,0:T(8,128)(2,1)}), bf16[64,8,1152]{2,1,0:T(8,128)(2,1)S(1)}, u32[]{:S(2)}, u32[]{:S(2)}) async-start(bf16[64,8,1152]{2,1,0:T(8,128)(2,1)} %bitcast.10), calls=%async_computation.1 | async-start | bytes 2359296 | tf_op jit(solution)/shard_map/all_to_all | solution.py:343
  90.9 40.9 %copy-start.6 = (bf16[128,1152]{1,0:T(8,128)(2,1)S(1)}, bf16[128,1152]{1,0:T(8,128)(2,1)}, u32[]{:S(2)}) copy-start(bf16[128,1152]{1,0:T(8,128)(2,1)} %get-tuple-element.53.refs_0_) | copy-start | bytes 884740
  90.9 24.4 %collective-permute-start = (bf16[128,1152]{1,0:T(8,128)(2,1)S(1)}, bf16[128,1152]{1,0:T(8,128)(2,1)S(1)}, u32[]{:S(2)}, u32[]{:S(2)}) collective-permute-start(bf16[128,1152]{1,0:T(8,128)(2,1)S(1)} %copy-done.15), channel_id=1, source_target_pairs={{0,1},{1,2},{2,3},{3,4},{4,5},{5,6},{6,7},{7,0},{8,9},{9,10},{10,1... | collective-permute-start | bytes 884744 | tf_op jit(solution)/shard_map/ppermute | solution.py:319
  95.9 28.5 %collective-permute-start.4 = (bf16[128,1152]{1,0:T(8,128)(2,1)S(1)}, bf16[128,1152]{1,0:T(8,128)(2,1)S(1)}, u32[]{:S(2)}, u32[]{:S(2)}) collective-permute-start(bf16[128,1152]{1,0:T(8,128)(2,1)S(1)} %copy-done.14), channel_id=1, source_target_pairs={{0,7},{1,0},{2,1},{3,2},{4,3},{5,4},{6,5},{7,6},{8,15},{9,8},{10,9... | collective-permute-start | bytes 884744 | tf_op jit(solution)/shard_map/ppermute | solution.py:319
  115.3 21.6 %copy-start.5 = (bf16[128,1152]{1,0:T(8,128)(2,1)S(1)}, bf16[128,1152]{1,0:T(8,128)(2,1)}, u32[]{:S(2)}) copy-start(bf16[128,1152]{1,0:T(8,128)(2,1)} %get-tuple-element.49.refs_0_) | copy-start | bytes 884740
  115.4 14.3 %collective-permute-start.1 = (bf16[128,1152]{1,0:T(8,128)(2,1)S(1)}, bf16[128,1152]{1,0:T(8,128)(2,1)S(1)}, u32[]{:S(2)}, u32[]{:S(2)}) collective-permute-start(bf16[128,1152]{1,0:T(8,128)(2,1)S(1)} %add.13), channel_id=1, source_target_pairs={{0,1},{1,2},{2,3},{3,4},{4,5},{5,6},{6,7},{7,0},{8,9},{9,10},{10,1... | collective-permute-start | bytes 884744 | tf_op jit(solution)/shard_map/ppermute | solution.py:319
  117.3 14.4 %collective-permute-start.11 = (bf16[128,1152]{1,0:T(8,128)(2,1)S(1)}, bf16[128,1152]{1,0:T(8,128)(2,1)S(1)}, u32[]{:S(2)}, u32[]{:S(2)}) collective-permute-start(bf16[128,1152]{1,0:T(8,128)(2,1)S(1)} %copy-done.13), channel_id=1, source_target_pairs={{0,7},{1,0},{2,1},{3,2},{4,3},{5,4},{6,5},{7,6},{8,15},{9,8},{10,9... | collective-permute-start | bytes 884744 | tf_op jit(solution)/shard_map/ppermute | solution.py:319
  122.5 14.5 %collective-permute-start.8 = (bf16[128,1152]{1,0:T(8,128)(2,1)S(1)}, bf16[128,1152]{1,0:T(8,128)(2,1)S(1)}, u32[]{:S(2)}, u32[]{:S(2)}) collective-permute-start(bf16[128,1152]{1,0:T(8,128)(2,1)S(1)} %copy-done.12), channel_id=1, source_target_pairs={{0,1},{1,2},{2,3},{3,4},{4,5},{5,6},{6,7},{7,0},{8,9},{9,10},{10,1... | collective-permute-start | bytes 884744 | tf_op jit(solution)/shard_map/ppermute | solution.py:319
  124.4 14.6 %copy-start.4 = (bf16[128,1152]{1,0:T(8,128)(2,1)S(1)}, bf16[128,1152]{1,0:T(8,128)(2,1)}, u32[]{:S(2)}) copy-start(bf16[128,1152]{1,0:T(8,128)(2,1)} %get-tuple-element.42.refs_0_) | copy-start | bytes 884740
  124.5 14.5 %collective-permute-start.5 = (bf16[128,1152]{1,0:T(8,128)(2,1)S(1)}, bf16[128,1152]{1,0:T(8,128)(2,1)S(1)}, u32[]{:S(2)}, u32[]{:S(2)}) collective-permute-start(bf16[128,1152]{1,0:T(8,128)(2,1)S(1)} %add.16), channel_id=1, source_target_pairs={{0,7},{1,0},{2,1},{3,2},{4,3},{5,4},{6,5},{7,6},{8,15},{9,8},{10,9... | collective-permute-start | bytes 884744 | tf_op jit(solution)/shard_map/ppermute | solution.py:319
  129.7 14.6 %copy-start.3 = (bf16[128,1152]{1,0:T(8,128)(2,1)S(1)}, bf16[128,1152]{1,0:T(8,128)(2,1)}, u32[]{:S(2)}) copy-start(bf16[128,1152]{1,0:T(8,128)(2,1)} %get-tuple-element.38.refs_0_) | copy-start | bytes 884740
  129.8 14.5 %collective-permute-start.2 = (bf16[128,1152]{1,0:T(8,128)(2,1)S(1)}, bf16[128,1152]{1,0:T(8,128)(2,1)S(1)}, u32[]{:S(2)}, u32[]{:S(2)}) collective-permute-start(bf16[128,1152]{1,0:T(8,128)(2,1)S(1)} %add.14), channel_id=1, source_target_pairs={{0,1},{1,2},{2,3},{3,4},{4,5},{5,6},{6,7},{7,0},{8,9},{9,10},{10,1... | collective-permute-start | bytes 884744 | tf_op jit(solution)/shard_map/ppermute | solution.py:319
  131.7 14.7 %copy-start.2 = (bf16[128,1152]{1,0:T(8,128)(2,1)S(1)}, bf16[128,1152]{1,0:T(8,128)(2,1)}, u32[]{:S(2)}) copy-start(bf16[128,1152]{1,0:T(8,128)(2,1)} %get-tuple-element.52.refs_0_) | copy-start | bytes 884740
  131.8 14.6 %collective-permute-start.12 = (bf16[128,1152]{1,0:T(8,128)(2,1)S(1)}, bf16[128,1152]{1,0:T(8,128)(2,1)S(1)}, u32[]{:S(2)}, u32[]{:S(2)}) collective-permute-start(bf16[128,1152]{1,0:T(8,128)(2,1)S(1)} %add.21), channel_id=1, source_target_pairs={{0,7},{1,0},{2,1},{3,2},{4,3},{5,4},{6,5},{7,6},{8,15},{9,8},{10,9... | collective-permute-start | bytes 884744 | tf_op jit(solution)/shard_map/ppermute | solution.py:319
  137.0 14.7 %copy-start.1 = (bf16[128,1152]{1,0:T(8,128)(2,1)S(1)}, bf16[128,1152]{1,0:T(8,128)(2,1)}, u32[]{:S(2)}) copy-start(bf16[128,1152]{1,0:T(8,128)(2,1)} %get-tuple-element.48.refs_0_) | copy-start | bytes 884740
  137.1 14.6 %collective-permute-start.9 = (bf16[128,1152]{1,0:T(8,128)(2,1)S(1)}, bf16[128,1152]{1,0:T(8,128)(2,1)S(1)}, u32[]{:S(2)}, u32[]{:S(2)}) collective-permute-start(bf16[128,1152]{1,0:T(8,128)(2,1)S(1)} %add.19), channel_id=1, source_target_pairs={{0,1},{1,2},{2,3},{3,4},{4,5},{5,6},{6,7},{7,0},{8,9},{9,10},{10,1... | collective-permute-start | bytes 884744 | tf_op jit(solution)/shard_map/ppermute | solution.py:319
  139.0 15.3 %copy-start.11 = (bf16[128,1152]{1,0:T(8,128)(2,1)S(1)}, bf16[128,1152]{1,0:T(8,128)(2,1)}, u32[]{:S(2)}) copy-start(bf16[128,1152]{1,0:T(8,128)(2,1)} %get-tuple-element.37.refs_0_) | copy-start | bytes 884740
  139.1 12.7 %collective-permute-start.6 = (bf16[128,1152]{1,0:T(8,128)(2,1)S(1)}, bf16[128,1152]{1,0:T(8,128)(2,1)S(1)}, u32[]{:S(2)}, u32[]{:S(2)}) collective-permute-start(bf16[128,1152]{1,0:T(8,128)(2,1)S(1)} %add.17), channel_id=1, source_target_pairs={{0,7},{1,0},{2,1},{3,2},{4,3},{5,4},{6,5},{7,6},{8,15},{9,8},{10,9... | collective-permute-start | bytes 884744 | tf_op jit(solution)/shard_map/ppermute | solution.py:319
  144.4 16.5 %copy-start = (bf16[128,1152]{1,0:T(8,128)(2,1)S(1)}, bf16[128,1152]{1,0:T(8,128)(2,1)}, u32[]{:S(2)}) copy-start(bf16[128,1152]{1,0:T(8,128)(2,1)} %get-tuple-element.51.refs_0_) | copy-start | bytes 884740
  144.4 10.0 %collective-permute-start.3 = (bf16[128,1152]{1,0:T(8,128)(2,1)S(1)}, bf16[128,1152]{1,0:T(8,128)(2,1)S(1)}, u32[]{:S(2)}, u32[]{:S(2)}) collective-permute-start(bf16[128,1152]{1,0:T(8,128)(2,1)S(1)} %add.15), channel_id=1, source_target_pairs={{0,1},{1,2},{2,3},{3,4},{4,5},{5,6},{6,7},{7,0},{8,9},{9,10},{10,1... | collective-permute-start | bytes 884744 | tf_op jit(solution)/shard_map/ppermute | solution.py:319
  146.5 14.3 %collective-permute-start.13 = (bf16[128,1152]{1,0:T(8,128)(2,1)S(1)}, bf16[128,1152]{1,0:T(8,128)(2,1)S(1)}, u32[]{:S(2)}, u32[]{:S(2)}) collective-permute-start(bf16[128,1152]{1,0:T(8,128)(2,1)S(1)} %add.22), channel_id=1, source_target_pairs={{0,7},{1,0},{2,1},{3,2},{4,3},{5,4},{6,5},{7,6},{8,15},{9,8},{10,9... | collective-permute-start | bytes 884744 | tf_op jit(solution)/shard_map/ppermute | solution.py:319
  154.3 16.0 %copy-start.10 = (bf16[128,1152]{1,0:T(8,128)(2,1)S(1)}, bf16[128,1152]{1,0:T(8,128)(2,1)}, u32[]{:S(2)}) copy-start(bf16[128,1152]{1,0:T(8,128)(2,1)} %get-tuple-element.47.own_ref) | copy-start | bytes 884740
  154.4 13.7 %collective-permute-start.7 = (bf16[128,1152]{1,0:T(8,128)(2,1)S(1)}, bf16[128,1152]{1,0:T(8,128)(2,1)S(1)}, u32[]{:S(2)}, u32[]{:S(2)}) collective-permute-start(bf16[128,1152]{1,0:T(8,128)(2,1)S(1)} %add.18), channel_id=1, source_target_pairs={{0,8},{1,9},{2,10},{3,11},{4,12},{5,13},{6,14},{7,15},{8,0},{9,1},... | collective-permute-start | bytes 884744 | tf_op jit(solution)/shard_map/ppermute | solution.py:348
  158.9 9.8 %collective-permute-start.10 = (bf16[128,1152]{1,0:T(8,128)(2,1)S(1)}, bf16[128,1152]{1,0:T(8,128)(2,1)S(1)}, u32[]{:S(2)}, u32[]{:S(2)}) collective-permute-start(bf16[128,1152]{1,0:T(8,128)(2,1)S(1)} %add.20), channel_id=1, source_target_pairs={{0,1},{1,2},{2,3},{3,4},{4,5},{5,6},{6,7},{7,0},{8,9},{9,10},{10,1... | collective-permute-start | bytes 884744 | tf_op jit(solution)/shard_map/ppermute | solution.py:319
  161.0 9.4 %collective-permute-start.14 = (bf16[128,1152]{1,0:T(8,128)(2,1)S(1)}, bf16[128,1152]{1,0:T(8,128)(2,1)S(1)}, u32[]{:S(2)}, u32[]{:S(2)}) collective-permute-start(bf16[128,1152]{1,0:T(8,128)(2,1)S(1)} %add.23), channel_id=1, source_target_pairs={{0,7},{1,0},{2,1},{3,2},{4,3},{5,4},{6,5},{7,6},{8,15},{9,8},{10,9... | collective-permute-start | bytes 884744 | tf_op jit(solution)/shard_map/ppermute | solution.py:319
